TPU v7x, 32 devices: a whole 2x2x4 slice. The times are simulated.
32 devices in a mesh: parts: 2 (over y), mp: 4 (over z), shot: 4 (over x, core).
Axes of the slice: x: 2, y: 2, z: 4, core: 2. Of those that a mesh axis runs over, the one named last changes fastest.
Arguments:
- courant: float32 [192, 256, 128], P(('parts', 'mp')), parts along dimension 0, may hold values from 0.04 to 0.2
- forward_old: float32 [8, 96, 256, 128], P(('parts', 'shot'), 'mp'), parts along dimension 0, may hold values from -5 to 5
- forward_now: float32 [8, 96, 256, 128], P(('parts', 'shot'), 'mp'), parts along dimension 0, may hold values from -5 to 5
- adjoint_late: float32 [8, 96, 256, 128], P(('parts', 'shot'), 'mp'), parts along dimension 0, may hold values from -5 to 5
- adjoint_now: float32 [8, 96, 256, 128], P(('parts', 'shot'), 'mp'), parts along dimension 0, may hold values from -5 to 5
- src_cell: int32 [8, 64], P(('parts', 'shot')), parts along dimension 0, may hold values from 0 to 3145727
- src_sign: int32 [8, 64], P(('parts', 'shot')), parts along dimension 0, may hold values from 0 to 1
- wavelet: float32 [8, 2, 64], P(('parts', 'shot')), parts along dimension 0, may hold values from -16 to 16
- rec_cell: int32 [4096], P('parts'), parts along dimension 0, may hold values from 0 to 3145727
- rec_data: float32 [8, 2, 2048], P(('parts', 'shot')), parts along dimension 0, may hold values from -16 to 16
Outputs:
- raw_gradient: float32 [192, 256, 128], P(('parts', 'mp'), 'shot'), parts along dimension 0
- smooth_gradient: float32 [192, 256, 128], P(('parts', 'shot'), None, 'mp'), parts along dimension 0
There are 2 independent parts, one for each index of `parts`. A program takes and returns all parts, laid end to end along the dimension named above; each array names one. Nothing has to cross between parts.
All inputs are finite; a program needn't handle non-finite values.
Results may differ from a plain program's by a relative error of at most 0.00025.
Values sent between devices are 32-bit elements; how exact they have to be, the bound alone decides.
No kernel may reach another device: no remote copies, remote signals or barrier semaphores. Data moves between devices by JAX's collectives and lax.ppermute only.
A program may use at most 128 MiB of HBM per device.

v0:
```python
import jax
import jax.numpy as jnp
from jax import lax
from jax.sharding import PartitionSpec as P

SMOOTH_X = 32
SMOOTH_YZ = 4


COEFS = (8.0 / 5.0, -1.0 / 5.0, 8.0 / 315.0, -1.0 / 560.0)
CENTER = -205.0 / 72.0


def with_halo(block, sides, width):
    for axis, dim in sides:
        count = lax.axis_size(axis)
        forward = [(i, i + 1) for i in range(count - 1)]
        backward = [(target, source) for source, target in forward]
        low = lax.ppermute(
            lax.slice_in_dim(block, block.shape[dim] - width, None, axis=dim), axis, forward
        )
        high = lax.ppermute(lax.slice_in_dim(block, 0, width, axis=dim), axis, backward)
        block = jnp.concatenate([low, block, high], axis=dim)
    return block


def laplace(padded):
    row_count = padded.shape[-3] - 8
    center_rows = padded[..., 4 : 4 + row_count, :, :]
    leading = ((0, 0),) * (padded.ndim - 3)
    padded_yz = jnp.pad(center_rows, leading + ((0, 0), (4, 4), (4, 4)))
    width_y = center_rows.shape[-2]
    width_z = center_rows.shape[-1]
    accum_sum = 3.0 * CENTER * center_rows
    for offset, weight in enumerate(COEFS):
        reach = offset + 1
        along_x = (
            padded[..., 4 + reach : 4 + reach + row_count, :, :]
            + padded[..., 4 - reach : 4 - reach + row_count, :, :]
        )
        along_y = (
            padded_yz[..., :, 4 + reach : 4 + reach + width_y, 4 : 4 + width_z]
            + padded_yz[..., :, 4 - reach : 4 - reach + width_y, 4 : 4 + width_z]
        )
        along_z = (
            padded_yz[..., :, 4 : 4 + width_y, 4 + reach : 4 + reach + width_z]
            + padded_yz[..., :, 4 : 4 + width_y, 4 - reach : 4 - reach + width_z]
        )
        accum_sum = accum_sum + weight * (along_x + along_y + along_z)
    return accum_sum


def inject(field, cells, values, first_row):
    plane_size = field.shape[-2] * field.shape[-1]
    local_cell = cells - first_row * plane_size
    valid = (local_cell >= 0) & (local_cell < field.size)
    target = jnp.where(valid, local_cell, field.size)
    return field.reshape(-1).at[target].add(values, mode="drop").reshape(field.shape)


def sine_table(length):
    counter = jnp.arange(length, dtype=jnp.int32) + 1
    product = counter[:, None] * counter[None, :] % (2 * (length + 1))
    return jnp.sin(jnp.pi * product.astype(jnp.float32) / (length + 1))


def response(length, strength):
    counter = jnp.arange(length, dtype=jnp.int32) + 1
    half_sine = jnp.sin(jnp.pi * counter.astype(jnp.float32) / (2 * (length + 1)))
    return 1.0 / (1.0 + strength * 4.0 * half_sine * half_sine)


def filter_matrix(length, resp):
    table = sine_table(length)
    return (
        2.0 / (length + 1) * jnp.dot(table * resp[None, :], table, precision=lax.Precision.HIGHEST)
    )


def add_rims(stacked):
    return with_halo(stacked, (("mp", 1),), 4)


def per_device(
    courant,
    forward_old,
    forward_now,
    adjoint_late,
    adjoint_now,
    src_cell,
    src_sign,
    wavelet,
    rec_cell,
    rec_data,
):
    highest = lax.Precision.HIGHEST
    slab_rows = courant.shape[0]
    first_row = lax.axis_index("mp") * slab_rows
    cells = src_cell[0]
    signed = (2 * src_sign[0] - 1).astype(jnp.float32)
    source_first = signed * wavelet[0, 0]
    source_second = signed * wavelet[0, 1]
    old_fwd = forward_old[0]
    now_fwd = forward_now[0]
    late_adj = adjoint_late[0]
    now_adj = adjoint_now[0]
    first_laps = laplace(add_rims(jnp.stack([now_fwd, now_adj])))
    accel_first = inject(courant * first_laps[0], cells, source_first, first_row)
    next_fwd = 2.0 * now_fwd - old_fwd + accel_first
    mid_adj = (
        2.0 * now_adj
        - late_adj
        + inject(courant * first_laps[1], rec_cell, rec_data[0, 0], first_row)
    )
    laps = laplace(add_rims(jnp.stack([next_fwd, mid_adj])))
    accel_second = inject(courant * laps[0], cells, source_second, first_row)
    first_adj = (
        2.0 * mid_adj - now_adj + inject(courant * laps[1], rec_cell, rec_data[0, 1], first_row)
    )
    group_term = first_adj * accel_first + mid_adj * accel_second
    summed = lax.psum_scatter(group_term, "shot", scatter_dimension=1, tiled=True)
    raw_gradient = summed / lax.axis_size("shot")
    full_x = slab_rows * lax.axis_size("mp")
    full_y = courant.shape[1]
    full_z = courant.shape[2]
    fx_resp = response(full_x, float(SMOOTH_X * SMOOTH_X))
    fy_resp = response(full_y, float(SMOOTH_YZ * SMOOTH_YZ))
    fz_resp = response(full_z, float(SMOOTH_YZ * SMOOTH_YZ))
    kappa = (
        1.0
        / jnp.sqrt(jnp.mean(fx_resp * fx_resp))
        * (1.0 / jnp.sqrt(jnp.mean(fy_resp * fy_resp)))
        * (1.0 / jnp.sqrt(jnp.mean(fz_resp * fz_resp)))
    )
    matrix_x = filter_matrix(full_x, fx_resp)
    matrix_y = filter_matrix(full_y, fy_resp)
    matrix_z = filter_matrix(full_z, fz_resp)
    depth_done = jnp.einsum("abk,jk->abj", raw_gradient, matrix_z, precision=highest)
    x_done = jnp.einsum(
        "ia,abc->ibc",
        matrix_x,
        lax.all_to_all(depth_done, "mp", split_axis=2, concat_axis=0, tiled=True),
        precision=highest,
    )
    y_done = jnp.einsum(
        "jb,abc->ajc",
        matrix_y,
        lax.all_to_all(x_done, "shot", split_axis=0, concat_axis=1, tiled=True),
        precision=highest,
    )
    smooth_gradient = y_done * kappa
    return (raw_gradient, smooth_gradient)


def solution(mesh):
    return jax.shard_map(
        per_device,
        mesh=mesh,
        in_specs=(
            P(("parts", "mp"), None, None),
            P(("parts", "shot"), "mp", None, None),
            P(("parts", "shot"), "mp", None, None),
            P(("parts", "shot"), "mp", None, None),
            P(("parts", "shot"), "mp", None, None),
            P(("parts", "shot"), None),
            P(("parts", "shot"), None),
            P(("parts", "shot"), None, None),
            P("parts"),
            P(("parts", "shot"), None, None),
        ),
        out_specs=(P(("parts", "mp"), "shot", None), P(("parts", "shot"), None, "mp")),
        check_vma=False,
    )
```

profile of v0, /device:TPU:0, one launch (start us, length us, event | category | flops | bytes accessed | tf_op | source)
XLA Modules:
  0.0 398.9 jit_solution(15239315147120798997)
XLA Ops:
  7.2 2.2 constant_dynamic-update-slice_fusion.1
  10.3 2.7 copy-done.2
  12.9 1.1 fusion.135
  14.1 1.3 collective-permute-start
  15.4 5.6 %collective-permute-start.1 = (f32[2,4,256,128]{3,2,1,0:T(8,128)S(1)}, f32[2,4,256,128]{3,2,1,0:T(8,128)S(1)}, u32[]{:S(2)}, u32[]{:S(2)}) collective-permute-start(f32[2,4,256,128]{3,2,1,0:T(8,128)S(1)} %get-tuple-element.11), channel_id=1, source_target_pairs={{0,4},{4,8},{8,12},{1,5},{5,9},{9,13},{2,6},{6,10},{10,14},{3,7},{... | collective-permute-start | bytes 3145736 | tf_op jit(solution)/shard_map/ppermute | solution.py:19
  21.1 21.2 %collective-permute-done = f32[2,4,256,128]{3,2,1,0:T(8,128)S(1)} collective-permute-done((f32[2,4,256,128]{3,2,1,0:T(8,128)}, f32[2,4,256,128]{3,2,1,0:T(8,128)S(1)}, u32[]{:S(2)}, u32[]{:S(2)}) %collective-permute-start) | collective-permute-done | bytes 1048608 | tf_op jit(solution)/shard_map/ppermute | solution.py:22
  42.4 1.0 collective-permute-done.1
  43.3 77.9 %fusion.6 = f32[2,24,256,128]{3,2,1,0:T(8,128)} fusion(f32[2,24,256,128]{3,2,1,0:T(8,128)} %copy-done.2, f32[2,4,256,128]{3,2,1,0:T(8,128)S(1)} %collective-permute-done.1, f32[2,4,256,128]{3,2,1,0:T(8,128)S(1)} %collective-permute-done), kind=kLoop, calls=%fused_computation.61 | loop fusion | flops 58195968 | bytes 14680064 | tf_op jit(solution)/shard_map/add | solution.py:49
  121.3 5.2 %fusion.61 = (f32[24,256,128]{2,1,0:T(8,128)S(1)}, f32[24,256,128]{2,1,0:T(8,128)}) fusion(f32[24,256,128]{2,1,0:T(8,128)S(1)} %copy-done.3, f32[2,24,256,128]{3,2,1,0:T(8,128)} %fusion.6), kind=kLoop, calls=%fused_computation.126 | loop fusion | flops 1572864 | bytes 15728640 | tf_op jit(solution)/shard_map/mul | solution.py:113
  126.5 12.6 %scatter_fusion = f32[786432]{0:T(1024)S(1)} fusion(f32[786432]{0:T(1024)S(1)} %bitcast.84, s32[2048]{0:T(1024)S(1)} %compare_select_fusion, f32[2048]{0:T(1024)S(1)} %bitcast.100), kind=kCustom, calls=%fused_computation | custom fusion | flops 2048 | bytes 32768 | tf_op jit(solution)/shard_map/scatter-add | solution.py:58
  139.1 4.5 %scatter_fusion.1 = f32[786432]{0:T(1024)} fusion(f32[786432]{0:T(1024)} %bitcast.89, s32[64]{0:T(128)S(1)} %fusion.125, f32[64]{0:T(128)S(1)} %get-tuple-element.15), kind=kCustom, calls=%fused_computation.1 | custom fusion | flops 64 | bytes 1024 | tf_op jit(solution)/shard_map/scatter-add | solution.py:58
  143.6 9.1 %subtract_add_fusion = (f32[1,24,256,128]{3,2,1,0:T(8,128)S(1)}, f32[1,24,256,128]{3,2,1,0:T(8,128)}) fusion(f32[1,24,256,128]{3,2,1,0:T(8,128)S(1)} %bitcast.85, f32[1,24,256,128]{3,2,1,0:T(8,128)} %param.13, f32[1,24,256,128]{3,2,1,0:T(8,128)} %param.14, f32[1,24,256,128]{3,2,1,0:T(8,128)} %bitcast.90, f32[1,24,256,128]{3,2,1,0:T(8,128)} %param.11, ...), kind=kLoop, calls=%fused_computation.134 | loop fusion | flops 4718592 | bytes 25165824 | tf_op jit(solution)/shard_map/add | solution.py:111
  152.7 1.5 fusion.72
  154.3 1.3 collective-permute-start.2
  155.6 5.3 %collective-permute-start.3 = (f32[2,4,256,128]{3,2,1,0:T(8,128)S(1)}, f32[2,4,256,128]{3,2,1,0:T(8,128)S(1)}, u32[]{:S(2)}, u32[]{:S(2)}) collective-permute-start(f32[2,4,256,128]{3,2,1,0:T(8,128)S(1)} %get-tuple-element.9), channel_id=1, source_target_pairs={{0,4},{4,8},{8,12},{1,5},{5,9},{9,13},{2,6},{6,10},{10,14},{3,7},{... | collective-permute-start | bytes 3145736 | tf_op jit(solution)/shard_map/ppermute | solution.py:19
  160.8 3.1 pad_maximum_fusion
  163.9 17.0 %collective-permute-done.2 = f32[2,4,256,128]{3,2,1,0:T(8,128)S(1)} collective-permute-done((f32[2,4,256,128]{3,2,1,0:T(8,128)S(1)}, f32[2,4,256,128]{3,2,1,0:T(8,128)S(1)}, u32[]{:S(2)}, u32[]{:S(2)}) %collective-permute-start.2) | collective-permute-done | bytes 1048608 | tf_op jit(solution)/shard_map/ppermute | solution.py:22
  180.9 1.2 collective-permute-done.3
  182.1 5.7 %pad_maximum_fusion.1 = (f32[2,28,256,128]{3,2,1,0:T(8,128)}, f32[2,28,256,128]{3,2,1,0:T(8,128)}) fusion(f32[2,4,256,128]{3,2,1,0:T(8,128)S(1)} %collective-permute-done.2, f32[1,24,256,128]{3,2,1,0:T(8,128)S(1)} %get-tuple-element.16, f32[1,24,256,128]{3,2,1,0:T(8,128)S(1)} %copy-done, f32[2,4,256,128]{3,2,1,0:T(8,128)S(1)} %collective-permute-done.3), kind=kLoop, calls=%fused_computation.53 | loop fusion | flops 7340032 | bytes 23068672 | tf_op jit(solution)/shard_map/concatenate | solution.py:23
  187.8 64.8 %fusion.40 = f32[2,24,256,128]{3,2,1,0:T(8,128)} fusion(f32[2,24,256,128]{3,2,1,0:T(8,128)} %pad_maximum_fusion, f32[2,28,256,128]{3,2,1,0:T(8,128)} %get-tuple-element.7, f32[2,28,256,128]{3,2,1,0:T(8,128)} %get-tuple-element.6), kind=kLoop, calls=%fused_computation.95 | loop fusion | flops 45613056 | bytes 62914560 | tf_op jit(solution)/shard_map/add | solution.py:49
  252.6 7.3 %fusion.58 = (f32[24,256,128]{2,1,0:T(8,128)}, f32[24,256,128]{2,1,0:T(8,128)}) fusion(f32[24,256,128]{2,1,0:T(8,128)} %param.10, f32[2,24,256,128]{3,2,1,0:T(8,128)} %fusion.40), kind=kLoop, calls=%fused_computation.120 | loop fusion | flops 1572864 | bytes 15728640 | tf_op jit(solution)/shard_map/mul | solution.py:116
  259.9 4.5 %scatter_fusion.3 = f32[786432]{0:T(1024)} fusion(f32[786432]{0:T(1024)} %bitcast.92, s32[64]{0:T(128)S(1)} %fusion.125, f32[64]{0:T(128)S(1)} %get-tuple-element.14), kind=kCustom, calls=%fused_computation.3 | custom fusion | flops 64 | bytes 1024 | tf_op jit(solution)/shard_map/scatter-add | solution.py:58
  264.3 13.9 %scatter_fusion.2 = f32[786432]{0:T(1024)} fusion(f32[786432]{0:T(1024)} %bitcast.87, s32[2048]{0:T(1024)S(1)} %compare_select_fusion, f32[2048]{0:T(1024)S(1)} %bitcast.99), kind=kCustom, calls=%fused_computation.2 | custom fusion | flops 2048 | bytes 32768 | tf_op jit(solution)/shard_map/scatter-add | solution.py:58
  278.2 9.2 %fusion.65 = f32[24,256,128]{2,1,0:T(8,128)} fusion(f32[24,256,128]{2,1,0:T(8,128)} %bitcast.91, f32[24,256,128]{2,1,0:T(8,128)} %bitcast.88, f32[1,24,256,128]{3,2,1,0:T(8,128)} %param.14, f32[24,256,128]{2,1,0:T(8,128)} %bitcast.93, f32[24,256,128]{2,1,0:T(8,128)S(1)} %bitcast.86, f32[1,24,256,128]{3,2,1,0:T(8,128)} %param.13), kind=kLoop, calls=%fused_computation.133 | loop fusion | flops 7077888 | bytes 22020096 | tf_op jit(solution)/shard_map/add | solution.py:120
  287.5 0.8 fusion.70
  288.3 39.4 %reduce-scatter.2.cloned.1.call-done = f32[24,64,128]{2,1,0:T(8,128)} async-done(((f32[24,256,128]{2,1,0:T(8,128)}), f32[24,64,128]{2,1,0:T(8,128)}) %reduce-scatter.2.cloned.1.call-update) | async-done | bytes 786448 | tf_op jit(solution)/shard_map/reduce_scatter | solution.py:121
  327.7 1.2 broadcast_multiply_fusion
  328.9 0.9 copy-done.4
  329.8 0.8 fusion.137
  331.1 1.8 reshape.170
  332.9 4.8 %all-to-all-start = ((f32[4,1,49152]{2,1,0:T(1,128)}), f32[4,1,49152]{2,1,0:T(1,128)S(1)}, u32[]{:S(2)}, u32[]{:S(2)}) async-start(f32[4,1,49152]{2,1,0:T(1,128)} %reshape.170), calls=%async_computation.1 | async-start | bytes 1572864 | tf_op jit(solution)/shard_map/all_to_all | solution.py:142
  337.8 0.7 fusion.71
  338.4 19.4 %all-to-all-done = f32[4,1,49152]{2,1,0:T(1,128)S(1)} async-done(((f32[4,1,49152]{2,1,0:T(1,128)}), f32[4,1,49152]{2,1,0:T(1,128)S(1)}, u32[]{:S(2)}, u32[]{:S(2)}) %all-to-all-start) | async-done | bytes 786464 | tf_op jit(solution)/shard_map/all_to_all | solution.py:142
  358.4 3.0 reduce
  361.4 0.8 reshape.171
  362.4 3.2 fusion.66
  365.6 1.4 copy.23
  367.0 1.8 reshape.172
  368.7 3.7 all-to-all-start.1
  372.5 0.7 multiply_reduce_fusion
  375.0 0.7 multiply_reduce_fusion.1
  376.3 2.4 fusion.69
  378.8 5.3 %all-to-all-done.1 = f32[4,1,49152]{2,1,0:T(1,128)S(1)} async-done(((f32[4,1,49152]{2,1,0:T(1,128)}), f32[4,1,49152]{2,1,0:T(1,128)S(1)}, u32[]{:S(2)}, u32[]{:S(2)}) %all-to-all-start.1) | async-done | bytes 786464 | tf_op jit(solution)/shard_map/all_to_all | solution.py:148
  384.1 3.0 reduce.1
  387.1 0.8 reshape.173
  387.8 1.2 copy.24
  389.1 0.9 all_to_all.33
  389.9 1.7 fusion.68
  (35 shorter events, 3.1 us)
Async XLA Ops:
  7.2 2.8 copy-start.1
  7.2 320.6 %reduce-scatter.2.cloned.1.call-start = ((), (), s32[]{:S(2)}) async-start(), calls=%async_computation.3 | async-start | bytes 3932160 | tf_op jit(solution)/shard_map/reduce_scatter | solution.py:121
  10.0 11.0 %copy-start.9 = (s32[1,64]{1,0:T(1,128)S(1)}, s32[1,64]{1,0:T(1,128)}, u32[]{:S(2)}) copy-start(s32[1,64]{1,0:T(1,128)} %param.15) | copy-start | bytes 772
  10.0 11.0 %copy-start.7 = (f32[1,2,64]{2,1,0:T(2,128)S(1)}, f32[1,2,64]{2,1,0:T(2,128)}, u32[]{:S(2)}) copy-start(f32[1,2,64]{2,1,0:T(2,128)} %param.17) | copy-start | bytes 1540
  10.0 11.0 %copy-start.8 = (s32[1,64]{1,0:T(1,128)S(1)}, s32[1,64]{1,0:T(1,128)}, u32[]{:S(2)}) copy-start(s32[1,64]{1,0:T(1,128)} %param.16) | copy-start | bytes 772
  10.0 11.1 %copy-start.6 = (s32[2048]{0:T(1024)S(1)}, s32[2048]{0:T(1024)}, u32[]{:S(2)}) copy-start(s32[2048]{0:T(1024)} %param.18) | copy-start | bytes 24580
  10.0 11.1 %copy-start.5 = (f32[1,2,2048]{2,1,0:T(2,128)S(1)}, f32[1,2,2048]{2,1,0:T(2,128)}, u32[]{:S(2)}) copy-start(f32[1,2,2048]{2,1,0:T(2,128)} %param.19) | copy-start | bytes 49156
  10.3 2.7 copy-start.2
  14.1 28.3 %collective-permute-start = (f32[2,4,256,128]{3,2,1,0:T(8,128)}, f32[2,4,256,128]{3,2,1,0:T(8,128)S(1)}, u32[]{:S(2)}, u32[]{:S(2)}) collective-permute-start(f32[2,4,256,128]{3,2,1,0:T(8,128)} %get-tuple-element.10), channel_id=1, source_target_pairs={{4,0},{8,4},{12,8},{5,1},{9,5},{13,9},{6,2},{10,6},{14,10},{7,3},{... | collective-permute-start | bytes 3145736 | tf_op jit(solution)/shard_map/ppermute | solution.py:22
  15.4 28.0 %collective-permute-start.1 = (f32[2,4,256,128]{3,2,1,0:T(8,128)S(1)}, f32[2,4,256,128]{3,2,1,0:T(8,128)S(1)}, u32[]{:S(2)}, u32[]{:S(2)}) collective-permute-start(f32[2,4,256,128]{3,2,1,0:T(8,128)S(1)} %get-tuple-element.11), channel_id=1, source_target_pairs={{0,4},{4,8},{8,12},{1,5},{5,9},{9,13},{2,6},{6,10},{10,14},{3,7},{... | collective-permute-start | bytes 3145736 | tf_op jit(solution)/shard_map/ppermute | solution.py:19
  21.1 100.1 %copy-start.3 = (f32[24,256,128]{2,1,0:T(8,128)S(1)}, f32[24,256,128]{2,1,0:T(8,128)}, u32[]{:S(2)}) copy-start(f32[24,256,128]{2,1,0:T(8,128)} %param.10) | copy-start | bytes 9437188
  152.7 8.1 %copy-start = (f32[1,24,256,128]{3,2,1,0:T(8,128)S(1)}, f32[1,24,256,128]{3,2,1,0:T(8,128)}, u32[]{:S(2)}) copy-start(f32[1,24,256,128]{3,2,1,0:T(8,128)} %get-tuple-element.17) | copy-start | bytes 9437188
  154.3 26.7 %collective-permute-start.2 = (f32[2,4,256,128]{3,2,1,0:T(8,128)S(1)}, f32[2,4,256,128]{3,2,1,0:T(8,128)S(1)}, u32[]{:S(2)}, u32[]{:S(2)}) collective-permute-start(f32[2,4,256,128]{3,2,1,0:T(8,128)S(1)} %get-tuple-element.8), channel_id=1, source_target_pairs={{4,0},{8,4},{12,8},{5,1},{9,5},{13,9},{6,2},{10,6},{14,10},{7,3},{... | collective-permute-start | bytes 3145736 | tf_op jit(solution)/shard_map/ppermute | solution.py:22
  155.6 26.6 %collective-permute-start.3 = (f32[2,4,256,128]{3,2,1,0:T(8,128)S(1)}, f32[2,4,256,128]{3,2,1,0:T(8,128)S(1)}, u32[]{:S(2)}, u32[]{:S(2)}) collective-permute-start(f32[2,4,256,128]{3,2,1,0:T(8,128)S(1)} %get-tuple-element.9), channel_id=1, source_target_pairs={{0,4},{4,8},{8,12},{1,5},{5,9},{9,13},{2,6},{6,10},{10,14},{3,7},{... | collective-permute-start | bytes 3145736 | tf_op jit(solution)/shard_map/ppermute | solution.py:19
  328.9 0.9 copy-start.4
  332.9 24.9 %all-to-all-start = ((f32[4,1,49152]{2,1,0:T(1,128)}), f32[4,1,49152]{2,1,0:T(1,128)S(1)}, u32[]{:S(2)}, u32[]{:S(2)}) async-start(f32[4,1,49152]{2,1,0:T(1,128)} %reshape.170), calls=%async_computation.1 | async-start | bytes 1572864 | tf_op jit(solution)/shard_map/all_to_all | solution.py:142
  368.7 15.4 %all-to-all-start.1 = ((f32[4,1,49152]{2,1,0:T(1,128)}), f32[4,1,49152]{2,1,0:T(1,128)S(1)}, u32[]{:S(2)}, u32[]{:S(2)}) async-start(f32[4,1,49152]{2,1,0:T(1,128)} %reshape.172), calls=%async_computation.2 | async-start | bytes 1572864 | tf_op jit(solution)/shard_map/all_to_all | solution.py:148
Sparse Core Ops, SparseCore 0:
  287.6 40.1 reduce-scatter.1
where the time goes:
time: 406 us; the launch traced here: 399 us
  other arithmetic  228 us (56%)
  waiting for transfers between devices  105 us (26%)
  starting transfers between devices  22 us (5%)
  local copies, waits for them, and re-layouts  17.7 us (4%)
  between operations  16.6 us (4%)
  matrix products  9.53 us (2%)
    add x2, other arithmetic, laplace(): accum_sum = accum_sum + weight * (along_x + along_y + along_z)  143 us
    reduce_scatter x1, waiting for transfers between devices, per_device(): lax.psum_scatter(group_term, 'shot', scatter_dimension=1, tiled=True)  39.4 us
    ppermute x2, waiting for transfers between devices, with_halo(): lax.ppermute(lax.slice_in_dim(block, 0, width, axis=dim), axis, backward)  38.3 us
    scatter-add x4, other arithmetic, inject(): field.reshape(-1).at[target].add(values, mode='drop').reshape(field.shape)  35.5 us
    all_to_all x1, waiting for transfers between devices, per_device(): lax.all_to_all(depth_done, 'mp', split_axis=2, concat_axis=0, tiled=True)  19.4 us
    unnamed x25, local copies, waits for them, and re-layouts  11.3 us
    ppermute x2, starting transfers between devices, with_halo(): lax.ppermute(lax.slice_in_dim(block, block.shape[dim] - width, None, axis...  10.9 us
    add x1, other arithmetic, per_device(): group_term = first_adj * accel_first + mid_adj * accel_second  9.21 us
  transfers between devices with their start and end apart: 7, of which 7 were waited for; matrix products, arithmetic and copies ran while one was open for 2% of the time, Pallas kernels for 0%

commit v1 on v0

v1 whole, which is shorter than its diff:
```python
import functools
import math

import jax
import jax.numpy as jnp
import ml_dtypes
import numpy as np
from jax import lax
from jax.experimental import pallas as pl
from jax.experimental.pallas import tpu as pltpu
from jax.sharding import PartitionSpec as P

SMOOTH_X = 32
SMOOTH_YZ = 4

COEFS = (8.0 / 5.0, -1.0 / 5.0, 8.0 / 315.0, -1.0 / 560.0)
CENTER = -205.0 / 72.0
REACH = len(COEFS)
SCALE = 5040.0
WHOLE = tuple(float(round(SCALE * a)) for a in COEFS)

LANES = 128
BF16 = jnp.bfloat16
F32 = jnp.float32
ANY = pl.BlockSpec(memory_space=pl.ANY)
VMEM = pl.BlockSpec(memory_space=pltpu.VMEM)
SMEM = pl.BlockSpec(memory_space=pltpu.SMEM)
PARAMS = pltpu.CompilerParams(vmem_limit_bytes=56 * 1024 * 1024)


def band(length):
    table = np.zeros((length, length), np.float32)
    for k, weight in enumerate(WHOLE, 1):
        near = np.arange(length - k)
        table[near, near + k] = weight
        table[near + k, near] = weight
    return table


def response(length, strength):
    counter = np.arange(1, length + 1, dtype=np.float64)
    half_sine = np.sin(np.pi * counter / (2 * (length + 1)))
    return 1.0 / (1.0 + strength * 4.0 * half_sine * half_sine)


def filter_matrix(length, strength):
    counter = np.arange(1, length + 1, dtype=np.float64)
    table = np.sin(np.pi * counter[:, None] * counter[None, :] / (length + 1))
    return 2.0 / (length + 1) * (table * response(length, strength)[None, :]) @ table


def scan_tables(length, strength, block):
    rate = math.acosh(1.0 + 0.5 / strength)
    index = np.arange(1, length + 1, dtype=np.float64)
    rise = np.sinh(rate * index)
    fall = np.sinh(rate * (length + 1 - index))
    whole = strength * math.sinh(rate) * math.sinh(rate * (length + 1))
    diag = rise * fall / whole
    left = np.concatenate([[0.0], rise[:-1] / rise[1:]])
    right = np.concatenate([fall[1:] / fall[:-1], [0.0]])
    first = (np.arange(length) // block) * block
    last = first + block - 1
    from_left = np.where(first > 0, rise[np.maximum(first - 1, 0)], 0.0) / rise
    from_right = np.where(last + 1 < length, fall[np.minimum(last + 1, length - 1)], 0.0) / fall
    rows = np.stack([diag, left, right, diag * from_left, diag * from_right])
    blocks = length // block
    carry = np.zeros((blocks, blocks))
    for here in range(blocks):
        for there in range(blocks):
            if there < here:
                carry[here, there] = rise[there * block + block - 1] / rise[here * block - 1]
            elif there > here:
                carry[here, there] = fall[there * block] / fall[here * block + block]
    return rows.astype(np.float32), carry.astype(np.float32)


def split_table(table):
    high = table.astype(np.float32).astype(ml_dtypes.bfloat16)
    low = (table - high.astype(np.float64)).astype(np.float32).astype(ml_dtypes.bfloat16)
    return jnp.asarray(high), jnp.asarray(low)


def split(value):
    high = value.astype(BF16)
    low = (value - high.astype(F32)).astype(BF16)
    return high, low


def dot(a, b):
    return jnp.dot(a, b, preferred_element_type=F32)


def dot_t(a, b):
    return lax.dot_general(a, b, (((1,), (1,)), ((), ())), preferred_element_type=F32)


def laplace_plane(pad, p, band_y, band_z):
    here = pad[p + REACH]
    width = here.shape[1]
    both = jnp.concatenate(split(here), axis=1)
    along_y = dot(band_y[...], both)
    along_z = dot(both, band_z[...])
    total = (3.0 * SCALE * CENTER) * here
    for k, weight in enumerate(WHOLE, 1):
        total += weight * (pad[p + REACH + k] + pad[p + REACH - k])
    return total + (along_y[:, :width] + along_y[:, width:]) + along_z


def divmod_fixed(value, size):
    if size & (size - 1) == 0:
        return lax.shift_right_logical(value, size.bit_length() - 1), value & (size - 1)
    return lax.div(value, size), lax.rem(value, size)


def step_one_kernel(
    first_ref, src_cell, src_sign, wavelet, rec_cell, rec_data,
    courant, f_old, f_now, a_late, a_now, band_y, band_z,
    accel_out, next_out, mid_out, src_out, rec_out,
    f_pad, a_pad, c_buf, f_buf, a_buf, acc_buf, s_first, r_first, s_second, r_second,
    found, place, sems, out_sems,
):
    rows, ny, nz = courant.shape
    inside = pl.ds(REACH, rows)
    loads = [
        pltpu.make_async_copy(f_now, f_pad.at[inside], sems.at[0]),
        pltpu.make_async_copy(courant, c_buf, sems.at[1]),
        pltpu.make_async_copy(f_old, f_buf, sems.at[2]),
        pltpu.make_async_copy(a_now, a_pad.at[inside], sems.at[3]),
        pltpu.make_async_copy(a_late, a_buf, sems.at[4]),
    ]
    for load in loads:
        load.start()
    edge = jnp.zeros((REACH, ny, nz), F32)
    for pad in (f_pad, a_pad):
        pad[:REACH] = edge
        pad[REACH + rows :] = edge

    tiles = rows * ny // 8
    group = ny // 8

    def clear(p, _):
        blank = jnp.zeros((group, 8, nz), F32)
        for ref in (s_first, r_first, s_second, r_second):
            ref[pl.ds(p * group, group)] = blank
        return 0

    lax.fori_loop(0, rows, clear, 0)

    start = first_ref[0]
    size = rows * ny * nz
    flat = lax.broadcasted_iota(jnp.int32, (8, nz), 0) * nz + lax.broadcasted_iota(jnp.int32, (8, nz), 1)

    def put(refs, local, values):
        tile, within = divmod_fixed(local, 8 * nz)
        spot = flat == within
        for ref, value in zip(refs, values, strict=True):
            ref[tile] = ref[tile] + jnp.where(spot, value, 0.0)

    nsrc = src_cell.shape[1]

    def one_source(i, _):
        local = src_cell[0, i] - start
        mine = (local >= 0) & (local < size)
        local = jnp.where(mine, local, 0)
        sign = jnp.where(mine, (2 * src_sign[0, i] - 1).astype(F32), 0.0)
        put((s_first, s_second), local, (sign * wavelet[0, 0, i], sign * wavelet[0, 1, i]))
        return 0

    lax.fori_loop(0, nsrc, one_source, 0, unroll=8 if nsrc % 8 == 0 else 1)

    nrec = rec_cell.shape[0]

    def look(j, count):
        local = rec_cell[j] - start
        mine = (local >= 0) & (local < size)
        found[count] = j
        place[count] = local
        return count + mine.astype(jnp.int32)

    count = lax.fori_loop(0, nrec, look, 0, unroll=16 if nrec % 16 == 0 else 1)

    def some_receivers(g, _):
        for e in range(8):
            i = g * 8 + e
            mine = i < count
            j = jnp.where(mine, found[i], 0)
            local = jnp.where(mine, place[i], 0)
            first = jnp.where(mine, rec_data[0, 0, j], 0.0)
            second = jnp.where(mine, rec_data[0, 1, j], 0.0)
            put((r_first, r_second), local, (first, second))
        return 0

    lax.fori_loop(0, (count + 7) // 8, some_receivers, 0)
    stores = [
        pltpu.make_async_copy(s_second, src_out, out_sems.at[0]),
        pltpu.make_async_copy(r_second, rec_out, out_sems.at[1]),
    ]
    for store in stores:
        store.start()

    for load in loads[:3]:
        load.wait()

    def forward(p, _):
        courant_here = c_buf[p] * (1.0 / SCALE)
        c_buf[p] = courant_here
        spike = s_first[pl.ds(p * group, group)].reshape(ny, nz)
        accel = courant_here * laplace_plane(f_pad, p, band_y, band_z) + spike
        acc_buf[p] = accel
        f_buf[p] = (2.0 * f_pad[p + REACH] - f_buf[p]) + accel
        return 0

    lax.fori_loop(0, rows, forward, 0)
    more = [
        pltpu.make_async_copy(acc_buf, accel_out, out_sems.at[2]),
        pltpu.make_async_copy(f_buf, next_out, out_sems.at[3]),
    ]
    for store in more:
        store.start()
    stores += more
    for load in loads[3:]:
        load.wait()

    def adjoint(p, _):
        spike = r_first[pl.ds(p * group, group)].reshape(ny, nz)
        change = c_buf[p] * laplace_plane(a_pad, p, band_y, band_z) + spike
        a_buf[p] = (2.0 * a_pad[p + REACH] - a_buf[p]) + change
        return 0

    lax.fori_loop(0, rows, adjoint, 0)
    last = pltpu.make_async_copy(a_buf, mid_out, out_sems.at[4])
    last.start()
    stores.append(last)
    for store in stores:
        store.wait()


def step_one(first, src_cell, src_sign, wavelet, rec_cell, rec_data, courant, f_old, f_now, a_late, a_now, bands):
    rows, ny, nz = courant.shape
    field = jax.ShapeDtypeStruct((rows, ny, nz), F32)
    spikes = jax.ShapeDtypeStruct((rows * ny // 8, 8, nz), F32)
    whole = pltpu.VMEM((rows, ny, nz), F32)
    padded = pltpu.VMEM((rows + 2 * REACH, ny, nz), F32)
    sparse = pltpu.VMEM((rows * ny // 8, 8, nz), F32)
    nrec = rec_cell.shape[0]
    return pl.pallas_call(
        step_one_kernel,
        out_shape=(field, field, field, spikes, spikes),
        in_specs=[SMEM] * 6 + [ANY] * 5 + [VMEM] * 2,
        out_specs=(ANY,) * 5,
        scratch_shapes=[
            padded, padded, whole, whole, whole, whole, sparse, sparse, sparse, sparse,
            pltpu.SMEM((nrec + 8,), jnp.int32),
            pltpu.SMEM((nrec + 8,), jnp.int32),
            pltpu.SemaphoreType.DMA((5,)),
            pltpu.SemaphoreType.DMA((5,)),
        ],
        compiler_params=PARAMS,
        cost_estimate=pl.CostEstimate(flops=10**10, bytes_accessed=40 * 2**20, transcendentals=0),
        name="step_one",
    )(first, src_cell, src_sign, wavelet, rec_cell, rec_data, courant, f_old, f_now, a_late, a_now, *bands)


def sides(first_ref, rows):
    even = first_ref[1] == 0
    high = rows - REACH
    return (jnp.where(even, high, 0), even), (jnp.where(even, 0, high), jnp.logical_not(even))


def halo_sum(halo, q, upper):
    total = None
    for k, weight in enumerate(COEFS, 1):
        if q + k >= REACH:
            h = q + k - REACH
            term = weight * halo[jnp.where(upper, h, REACH - 1 - h)]
            total = term if total is None else total + term
    return total


def correct_kernel(count, first_ref, *refs):
    courant, parts, halos = refs[0], refs[1 : 1 + count], refs[1 + count : 3 + count]
    outs = refs[3 + count : 3 + 3 * count]
    c_buf, bufs, sems, out_sems = refs[3 + 3 * count], refs[4 + 3 * count], refs[5 + 3 * count], refs[6 + 3 * count]
    rows = courant.shape[0]
    slots = sides(first_ref, rows)
    loads, stores = [], []
    for s, (base, _) in enumerate(slots):
        for i, ref in enumerate((courant, *parts)):
            target = c_buf.at[s] if i == 0 else bufs.at[i - 1, s]
            loads.append(pltpu.make_async_copy(ref.at[pl.ds(base, REACH)], target, sems.at[s, i]))
            loads[-1].start()
    for s, (_, upper) in enumerate(slots):
        for load in loads[s * (1 + count) : (s + 1) * (1 + count)]:
            load.wait()
        for q in range(REACH):
            here = jnp.where(upper, q, REACH - 1 - q)
            change = c_buf[s, here] * halo_sum(halos[s], q, upper)
            for i in range(count):
                bufs[i, s, here] = bufs[i, s, here] + change
        for i in range(count):
            stores.append(pltpu.make_async_copy(bufs.at[i, s], outs[2 * i + s], out_sems.at[i, s]))
            stores[-1].start()
    for store in stores:
        store.wait()


def correct(first, courant, parts, halos):
    _, ny, nz = courant.shape
    slot = jax.ShapeDtypeStruct((REACH, ny, nz), F32)
    count = len(parts)
    return pl.pallas_call(
        functools.partial(correct_kernel, count),
        out_shape=(slot,) * (2 * count),
        in_specs=[SMEM] + [ANY] * (1 + count) + [VMEM] * 2,
        out_specs=(ANY,) * (2 * count),
        scratch_shapes=[
            pltpu.VMEM((2, REACH, ny, nz), F32),
            pltpu.VMEM((count, 2, REACH, ny, nz), F32),
            pltpu.SemaphoreType.DMA((2, 1 + count)),
            pltpu.SemaphoreType.DMA((count, 2)),
        ],
        compiler_params=PARAMS,
        cost_estimate=pl.CostEstimate(flops=10**7, bytes_accessed=6 * 2**20, transcendentals=0),
        name="correct",
    )(first, courant, *parts, *halos)


def step_two_kernel(
    first_ref, courant, a_now, accel_in, next_in, mid_in, src_in, rec_in, f0, f1, c0, c1, m0, m1, band_y, band_z,
    send_out, keep_out, edge_out, by_f_out, by_a_out,
    f_pad, a_pad, c_buf, now_buf, acc_buf, s_buf, r_buf, gt_buf, edge_buf, by_f, by_a, sems, out_sems,
):
    rows, ny, nz = courant.shape
    slots = sides(first_ref, rows)
    bit = first_ref[2]
    middle = pl.ds(REACH, rows - 2 * REACH)
    group = ny // 8
    blocks = gt_buf.shape[1]
    loads = []

    def fetch(source, target):
        loads.append(pltpu.make_async_copy(source, target, sems.at[len(loads)]))
        loads[-1].start()

    for source, edges, target, offset in (
        (next_in, (f0, f1), f_pad, REACH),
        (mid_in, (m0, m1), a_pad, REACH),
        (accel_in, (c0, c1), acc_buf, 0),
    ):
        fetch(source.at[middle], target.at[pl.ds(REACH + offset, rows - 2 * REACH)])
        for (base, _), edge in zip(slots, edges, strict=True):
            fetch(edge, target.at[pl.ds(base + offset, REACH)])
    for source, target in ((courant, c_buf), (a_now, now_buf), (src_in, s_buf), (rec_in, r_buf)):
        fetch(source, target)
    blank = jnp.zeros((REACH, ny, nz), F32)
    for pad in (f_pad, a_pad):
        pad[:REACH] = blank
        pad[REACH + rows :] = blank
    for load in loads:
        load.wait()

    def plane(p, _):
        c = c_buf[p] * (1.0 / SCALE)
        spike_s = s_buf[pl.ds(p * group, group)].reshape(ny, nz)
        spike_r = r_buf[pl.ds(p * group, group)].reshape(ny, nz)
        mid = a_pad[p + REACH]
        accel = c * laplace_plane(f_pad, p, band_y, band_z) + spike_s
        first = (2.0 * mid - now_buf[p]) + (c * laplace_plane(a_pad, p, band_y, band_z) + spike_r)
        gt_buf[p] = (first * acc_buf[p] + mid * accel).reshape(blocks, ny // blocks, nz)
        return 0

    lax.fori_loop(0, rows, plane, 0)
    stores = []

    def put(source, target):
        stores.append(pltpu.make_async_copy(source, target, out_sems.at[len(stores)]))
        stores[-1].start()

    for j in range(blocks // 2):
        put(gt_buf.at[middle, 2 * j + 1 - bit], send_out.at[:, j])
        put(gt_buf.at[middle, 2 * j + bit], keep_out.at[:, j])
    for s, (base, _) in enumerate(slots):
        for q in range(REACH):
            c = c_buf[base + q]
            by_f[s, q] = c * a_pad[base + q + REACH]
            by_a[s, q] = c * acc_buf[base + q]
            edge_buf[s, q] = gt_buf[base + q].reshape(ny, nz)
    put(edge_buf, edge_out)
    put(by_f, by_f_out)
    put(by_a, by_a_out)
    for store in stores:
        store.wait()


def step_two(first, courant, a_now, accel, nxt, mid, src, rec, edges, bands, blocks):
    rows, ny, nz = courant.shape
    inner = rows - 2 * REACH
    half = jax.ShapeDtypeStruct((inner, blocks // 2, ny // blocks, nz), F32)
    edge = jax.ShapeDtypeStruct((2, REACH, ny, nz), F32)
    whole = pltpu.VMEM((rows, ny, nz), F32)
    padded = pltpu.VMEM((rows + 2 * REACH, ny, nz), F32)
    sparse = pltpu.VMEM((rows * ny // 8, 8, nz), F32)
    slot = pltpu.VMEM((2, REACH, ny, nz), F32)
    return pl.pallas_call(
        step_two_kernel,
        out_shape=(half, half, edge, edge, edge),
        in_specs=[SMEM] + [ANY] * 13 + [VMEM] * 2,
        out_specs=(ANY,) * 5,
        scratch_shapes=[
            padded, padded, whole, whole, whole, sparse, sparse,
            pltpu.VMEM((rows, blocks, ny // blocks, nz), F32),
            slot, slot, slot,
            pltpu.SemaphoreType.DMA((13,)),
            pltpu.SemaphoreType.DMA((blocks + 3,)),
        ],
        compiler_params=PARAMS,
        cost_estimate=pl.CostEstimate(flops=10**10, bytes_accessed=40 * 2**20, transcendentals=0),
        name="step_two",
    )(first, courant, a_now, accel, nxt, mid, src, rec, *edges, *bands)


def finish_kernel(first_ref, edge, by_f, by_a, f0, f1, a0, a1, send_out, keep_out, buf, out_sems):
    blocks = buf.shape[1]
    _, reach, ny, nz = edge.shape
    bit = first_ref[2]
    rows = first_ref[3]
    for s, (_, upper) in enumerate(sides(first_ref, rows)):
        f_halo, a_halo = (f0, f1)[s], (a0, a1)[s]
        for q in range(reach):
            here = jnp.where(upper, q, reach - 1 - q)
            total = edge[s, here] + by_f[s, here] * halo_sum(f_halo, q, upper)
            total += by_a[s, here] * halo_sum(a_halo, q, upper)
            buf[s * reach + here] = total.reshape(blocks, ny // blocks, nz)
    stores = []
    for j in range(blocks // 2):
        stores.append(pltpu.make_async_copy(buf.at[:, 2 * j + 1 - bit], send_out.at[:, j], out_sems.at[2 * j]))
        stores.append(pltpu.make_async_copy(buf.at[:, 2 * j + bit], keep_out.at[:, j], out_sems.at[2 * j + 1]))
    for store in stores:
        store.start()
    for store in stores:
        store.wait()


def finish(first, edge, by_f, by_a, f_halos, a_halos, blocks):
    _, reach, ny, nz = edge.shape
    half = jax.ShapeDtypeStruct((2 * reach, blocks // 2, ny // blocks, nz), F32)
    return pl.pallas_call(
        finish_kernel,
        out_shape=(half, half),
        in_specs=[SMEM] + [VMEM] * 7,
        out_specs=(ANY,) * 2,
        scratch_shapes=[
            pltpu.VMEM((2 * reach, blocks, ny // blocks, nz), F32),
            pltpu.SemaphoreType.DMA((blocks,)),
        ],
        compiler_params=PARAMS,
        cost_estimate=pl.CostEstimate(flops=10**7, bytes_accessed=7 * 2**20, transcendentals=0),
        name="finish",
    )(first, edge, by_f, by_a, *f_halos, *a_halos)


def depth_kernel(edge_chunk, pieces, ratio, first_ref, keep, got, z_high, z_low, *refs):
    if edge_chunk:
        refs = refs[1:]
    raw_out, outs, (raw_buf, spectrum, sem) = refs[0], refs[1 : 1 + pieces], refs[1 + pieces :]
    planes, yb, nz = raw_buf.shape
    shots = first_ref[4].astype(F32)
    raw_buf[...] = (keep[...] + got[...]).reshape(planes, yb, nz) / shots
    rows = raw_out.shape[0]
    stores = []
    if edge_chunk:
        for s, (base, _) in enumerate(sides(first_ref, rows)):
            stores.append(
                pltpu.make_async_copy(raw_buf.at[pl.ds(s * REACH, REACH)], raw_out.at[pl.ds(base, REACH)], sem.at[s])
            )
    else:
        stores.append(pltpu.make_async_copy(raw_buf, raw_out.at[pl.ds(REACH, planes)], sem.at[0]))
    for store in stores:
        store.start()
    lanes = LANES // yb
    count = planes // lanes
    zb = nz // pieces
    for p in range(count):
        rows_here = jnp.concatenate([raw_buf[h * count + p] for h in range(lanes)], axis=0)
        high, low = split(rows_here)
        table = z_high[...]
        spectrum[p] = (dot_t(table, high) + dot_t(table, low) + dot_t(z_low[...], high)).reshape(pieces, zb, LANES)
    offset = first_ref[5]
    for k, out in enumerate(outs):
        out[...] = spectrum[:, lax.rem(offset + k, pieces)]
    for store in stores:
        store.wait()


def depth(first, keep, got, tables, raw_shape, pieces, previous=None):
    planes, _, yb, nz = keep.shape
    lanes = LANES // yb
    count = planes // lanes
    piece = jax.ShapeDtypeStruct((count, nz // pieces, LANES), F32)
    edge_chunk = previous is not None
    return pl.pallas_call(
        functools.partial(depth_kernel, edge_chunk, pieces, None),
        out_shape=(jax.ShapeDtypeStruct(raw_shape, F32),) + (piece,) * pieces,
        in_specs=[SMEM] + [VMEM] * 4 + ([ANY] if edge_chunk else []),
        out_specs=(ANY,) + (VMEM,) * pieces,
        scratch_shapes=[
            pltpu.VMEM((planes, yb, nz), F32),
            pltpu.VMEM((count, pieces, nz // pieces, LANES), F32),
            pltpu.SemaphoreType.DMA((2,)),
        ],
        input_output_aliases={5: 0} if edge_chunk else {},
        compiler_params=PARAMS,
        cost_estimate=pl.CostEstimate(flops=10**8, bytes_accessed=2 * 2**20, transcendentals=0),
        name="depth",
    )(first, keep, got, *tables, *([previous] if edge_chunk else []))


def rows_kernel(pieces, ratio, shots, rows, first_ref, scan, *refs):
    mains, edges = refs[:pieces], refs[pieces : 2 * pieces]
    y_high, y_low = refs[2 * pieces : 2 * pieces + 2]
    out, sends = refs[2 * pieces + 2], refs[2 * pieces + 3 : 2 * pieces + 2 + shots]
    main_buf, edge_buf, field, ends, sems = refs[2 * pieces + 2 + shots :]
    shot, mp = first_ref[6], first_ref[7]
    total, zb, ny = field.shape
    yb = ny // shots
    lanes = LANES // yb
    loads = []
    for k in range(pieces):
        q = lax.rem(mp - k + pieces, pieces)
        source, sub = lax.div(q, ratio), lax.rem(q, ratio)
        loads.append(pltpu.make_async_copy(mains[k], main_buf.at[sub, source], sems.at[0, k]))
        loads.append(pltpu.make_async_copy(edges[k], edge_buf.at[sub, source], sems.at[1, k]))
    for load in loads:
        load.start()
    for load in loads:
        load.wait()
    lane = lax.broadcasted_iota(jnp.int32, (zb, LANES), 1)
    slot_of = lane // yb
    main_count, edge_count = mains[0].shape[0], edges[0].shape[0]
    for sub in range(ratio):
        even = lax.rem(shot * ratio + sub, 2) == 0
        base = (jnp.where(even, rows - REACH, 0), jnp.where(even, 0, rows - REACH))
        for buf, count in ((main_buf, main_count), (edge_buf, edge_count)):
            for p in range(count):
                for h in range(lanes):
                    chunk_plane = h * count + p
                    if buf is main_buf:
                        x = sub * rows + REACH + chunk_plane
                    else:
                        x = sub * rows + base[chunk_plane // REACH] + chunk_plane % REACH
                    for t in range(shots // lanes):
                        value = None
                        for e in range(lanes):
                            piece = buf[sub, t * lanes + e, p]
                            if e != h:
                                piece = pltpu.roll(piece, (e - h) * yb % LANES, 1)
                            value = piece if value is None else jnp.where(slot_of == e, piece, value)
                        field[x, :, pl.ds(t * LANES, LANES)] = value
    first_x = shot * total

    def up(x, carry):
        carry = field[x] + scan[1, first_x + x] * carry
        out[x] = carry
        return carry

    ends[0] = lax.fori_loop(0, total, up, jnp.zeros((zb, ny), F32))

    def down(i, carry):
        x = total - 1 - i
        both = (out[x] + carry) * scan[0, first_x + x]
        before = field[x] + carry
        out[x] = both
        return scan[2, jnp.maximum(first_x + x - 1, 0)] * before

    def down_all():
        carry = jnp.zeros((zb, ny), F32)
        carry = lax.fori_loop(0, total - 1, down, carry)
        out[0] = (out[0] + carry) * scan[0, first_x]
        return field[0] + carry

    ends[1] = down_all()
    high_t, low_t = y_high[...], y_low[...]

    step = max(1, 256 // zb)
    while total % step:
        step -= 1

    def across(i, _):
        block = out[pl.ds(i * step, step)].reshape(step * zb, ny)
        high, low = split(block)
        result = dot_t(high, high_t) + dot_t(low, high_t) + dot_t(high, low_t)
        out[pl.ds(i * step, step)] = result.reshape(step, zb, ny)
        return 0

    lax.fori_loop(0, total // step, across, 0)
    for j, send in enumerate(sends, 1):
        send[...] = jnp.where((shot ^ j) > shot, ends[0], ends[1])


def rows_filter(first, scan, mains, edges, tables, ratio, shots, rows):
    pieces = len(mains)
    main_count, zb, _ = mains[0].shape
    edge_count = edges[0].shape[0]
    ny = tables[0].shape[0]
    total = ratio * rows
    end = jax.ShapeDtypeStruct((zb, ny), F32)
    return pl.pallas_call(
        functools.partial(rows_kernel, pieces, ratio, shots, rows),
        out_shape=(jax.ShapeDtypeStruct((total, zb, ny), F32),) + (end,) * (shots - 1),
        in_specs=[SMEM] * 2 + [ANY] * (2 * pieces) + [VMEM] * 2,
        out_specs=(VMEM,) * shots,
        scratch_shapes=[
            pltpu.VMEM((ratio, shots, main_count, zb, LANES), F32),
            pltpu.VMEM((ratio, shots, edge_count, zb, LANES), F32),
            pltpu.VMEM((total, zb, ny), F32),
            pltpu.VMEM((2, zb, ny), F32),
            pltpu.SemaphoreType.DMA((2, pieces)),
        ],
        compiler_params=PARAMS,
        cost_estimate=pl.CostEstimate(flops=10**8, bytes_accessed=2 * 2**20, transcendentals=0),
        name="rows",
    )(first, scan, *mains, *edges, *tables)


def join_kernel(shots, first_ref, scan, carry, part, *refs):
    ends, (y_high, y_low, out) = refs[: shots - 1], refs[shots - 1 :]
    total, zb, ny = part.shape
    shot = first_ref[6]
    first_x = shot * total
    below = jnp.zeros((zb, ny), F32)
    above = jnp.zeros((zb, ny), F32)
    for j, end in enumerate(ends, 1):
        other = shot ^ j
        term = carry[shot, other] * end[...]
        below += jnp.where(other < shot, term, 0.0)
        above += jnp.where(other > shot, term, 0.0)
    high, low = split(jnp.concatenate([below, above], axis=0))
    both = dot_t(high, y_high[...]) + dot_t(low, y_high[...]) + dot_t(high, y_low[...])
    below, above = both[:zb], both[zb:]
    for x in range(total):
        value = part[x] + scan[3, first_x + x] * below + scan[4, first_x + x] * above
        out[x] = value.T


def join(first, scan, carry, part, ends, tables):
    total, zb, ny = part.shape
    shots = len(ends) + 1
    return pl.pallas_call(
        functools.partial(join_kernel, shots),
        out_shape=jax.ShapeDtypeStruct((total, ny, zb), F32),
        in_specs=[SMEM] * 3 + [VMEM] * (shots + 2),
        out_specs=VMEM,
        compiler_params=PARAMS,
        cost_estimate=pl.CostEstimate(flops=10**8, bytes_accessed=2 * 2**20, transcendentals=0),
        name="join",
    )(first, scan, carry, part, *ends, *tables)


def neighbours(count, start):
    low = range(start, count - 1, 2)
    return [(i, i + 1) for i in low] + [(i + 1, i) for i in low]


def swap(values):
    count = lax.axis_size("mp")
    return tuple(lax.ppermute(v, "mp", neighbours(count, start)) for start, v in enumerate(values))


def boundary(field, even):
    high = field.shape[0] - REACH
    return tuple(
        lax.dynamic_slice_in_dim(field, jnp.where(even == (slot == 0), high, 0), REACH, axis=0) for slot in (0, 1)
    )


def flip(value, bit):
    count = lax.axis_size("shot")
    return lax.ppermute(value, "shot", [(i, i ^ bit) for i in range(count)])


def sum_groups(send, keep, shot):
    got = flip(send, 1)
    bit = 2
    while keep.shape[1] > 1:
        planes, blocks, yb, nz = keep.shape
        mine = (shot // bit) % 2
        shape = (planes, blocks // 2, 2, yb, nz)
        keep, got = keep.reshape(shape), got.reshape(shape)

        def part(which):
            return tuple(lax.dynamic_index_in_dim(v, which, 2, keepdims=False) for v in (keep, got))

        to_send = sum(part(1 - mine))
        keep = sum(part(mine))
        got = flip(to_send, bit)
        bit *= 2
    return keep, got


def spread(pieces, ratio):
    mp, shots = lax.axis_size("mp"), lax.axis_size("shot")
    out = []
    for k, piece in enumerate(pieces):
        pairs = []
        for m in range(mp):
            for s in range(shots):
                target = (s * ratio + m % ratio + k) % mp
                pairs.append((m * shots + s, target * shots + m // ratio))
        out.append(lax.ppermute(piece, ("mp", "shot"), pairs))
    return out


def per_device(
    courant, forward_old, forward_now, adjoint_late, adjoint_now,
    src_cell, src_sign, wavelet, rec_cell, rec_data,
):
    mp_count, shots = lax.axis_size("mp"), lax.axis_size("shot")
    mp, shot = lax.axis_index("mp"), lax.axis_index("shot")
    rows, ny, nz = courant.shape
    ratio = mp_count // shots
    full_x = rows * mp_count
    even = mp % 2 == 0
    first = jnp.stack(
        [
            mp * (rows * ny * nz), mp % 2, shot % 2, jnp.int32(rows), jnp.int32(shots),
            shot * ratio + mp % ratio, shot, mp,
        ]
    ).astype(jnp.int32)
    band_y, band_z = band(ny), band(nz)
    bands = (jnp.asarray(band_y, BF16), jnp.asarray(np.concatenate([band_z, band_z]), BF16))
    strength = float(SMOOTH_YZ * SMOOTH_YZ)
    strength_x = float(SMOOTH_X * SMOOTH_X)
    scan, carry = scan_tables(full_x, strength_x, rows * ratio)
    kappa = 1.0
    for length, e in ((full_x, strength_x), (ny, strength), (nz, strength)):
        resp = response(length, e)
        kappa /= math.sqrt(np.mean(resp * resp))
    z_tables = split_table(filter_matrix(nz, strength))
    y_tables = split_table(kappa * filter_matrix(ny, strength))

    f_old, f_now, a_late, a_now = forward_old[0], forward_now[0], adjoint_late[0], adjoint_now[0]
    f_halo = swap(boundary(f_now, even))
    a_halo = swap(boundary(a_now, even))
    accel, nxt, mid, src, rec = step_one(
        first, src_cell, src_sign, wavelet, rec_cell, rec_data, courant, f_old, f_now, a_late, a_now, bands
    )
    c0, c1, f0, f1 = correct(first, courant, (accel, nxt), f_halo)
    f_halo = swap((f0, f1))
    m0, m1 = correct(first, courant, (mid,), a_halo)
    a_halo = swap((m0, m1))
    send, keep, edge, by_f, by_a = step_two(
        first, courant, a_now, accel, nxt, mid, src, rec, (f0, f1, c0, c1, m0, m1), bands, shots
    )
    raw_shape = (rows, ny // shots, nz)
    keep, got = sum_groups(send, keep, shot)
    raw, *mains = depth(first, keep, got, z_tables, raw_shape, mp_count)
    mains = spread(mains, ratio)
    send, keep = finish(first, edge, by_f, by_a, f_halo, a_halo, shots)
    keep, got = sum_groups(send, keep, shot)
    raw, *edges = depth(first, keep, got, z_tables, raw_shape, mp_count, raw)
    edges = spread(edges, ratio)
    part, *ends = rows_filter(first, jnp.asarray(scan), mains, edges, y_tables, ratio, shots, rows)
    ends = [flip(end, j) for j, end in enumerate(ends, 1)]
    smooth = join(first, jnp.asarray(scan), jnp.asarray(carry), part, ends, y_tables)
    return raw, smooth


def solution(mesh):
    return jax.shard_map(
        per_device,
        mesh=mesh,
        in_specs=(
            P(("parts", "mp"), None, None),
            P(("parts", "shot"), "mp", None, None),
            P(("parts", "shot"), "mp", None, None),
            P(("parts", "shot"), "mp", None, None),
            P(("parts", "shot"), "mp", None, None),
            P(("parts", "shot"), None),
            P(("parts", "shot"), None),
            P(("parts", "shot"), None, None),
            P("parts"),
            P(("parts", "shot"), None, None),
        ),
        out_specs=(P(("parts", "mp"), "shot", None), P(("parts", "shot"), None, "mp")),
        check_vma=False,
    )
```

time: 406 us -> 168 us (0.41); the launches traced: 399 us -> 167 us
  other arithmetic: 228 us -> 1.69 us
  Pallas kernels: 0 us -> 71.3 us
  waiting for transfers between devices: 105 us -> 39.1 us
  starting transfers between devices: 22 us -> 42.7 us
  between operations: 16.6 us -> 1.05 us
  matrix products: 9.53 us -> 0 us
  local copies, waits for them, and re-layouts: 17.7 us -> 11.6 us
    add x7 -> x2, other arithmetic: 161 us -> 1.69 us  [sum_groups(): to_send = sum(part(1 - mine))]
    pallas_call x0 -> x9, Pallas kernels: none -> 71.3 us  [the longest x1 26.4 us: step_one(): pl.pallas_call(step_one_kernel, out_shape=(field, field, field, spikes, s...]
    reduce_scatter x1 -> x0, waiting for transfers between devices: 39.4 us -> none  [per_device(): lax.psum_scatter(group_term, 'shot', scatter_dimension=1, tiled=True)]
    scatter-add x4 -> x0, other arithmetic: 35.5 us -> none  [inject(): field.reshape(-1).at[target].add(values, mode='drop').reshape(field.shape)]
    ppermute x4 -> x23, starting transfers between devices: 13.4 us -> 42.7 us  [the longest x8 17.5 us: spread(): out.append(lax.ppermute(piece, ('mp', 'shot'), pairs))]
    all_to_all x2 -> x0, waiting for transfers between devices: 24.7 us -> none  [the longest x1 19.4 us: per_device(): lax.all_to_all(depth_done, 'mp', split_axis=2, concat_axis=0, tiled=True)]
    mul x3 -> x0, other arithmetic: 12.5 us -> none  [the longest x1 7.3 us: per_device(): accel_second = inject(courant * laps[0], cells, source_second, first_row)]
    dot_general x6 -> x0, matrix products: 9.53 us -> none  [the longest x3 3.88 us: filter_matrix(): jnp.dot(table * resp[None, :], table, precision=lax.Precision.HIGHEST)]
  transfers between devices with their start and end apart: 7 -> 23, of which waited for: 7 -> 7; matrix products, arithmetic and copies ran while one was open for 2% -> 2% of each run, Pallas kernels for 0% -> 22%
where the time goes in v1:
time: 168 us; the launch traced here: 167 us
  Pallas kernels  71.3 us (42%)
  starting transfers between devices  42.7 us (25%)
  waiting for transfers between devices  39.1 us (23%)
  local copies, waits for them, and re-layouts  11.6 us (7%)
  other arithmetic  1.69 us (1%)
    pallas_call x1, Pallas kernels, step_one(): pl.pallas_call(step_one_kernel, out_shape=(field, field, field, spikes, s...  26.4 us
    ppermute x8, waiting for transfers between devices, swap(): lax.ppermute(v, 'mp', neighbours(count, start))  20.1 us
    pallas_call x1, Pallas kernels, step_two(): pl.pallas_call(step_two_kernel, out_shape=(half, half, edge, edge, edge),...  18.3 us
    ppermute x8, starting transfers between devices, spread(): out.append(lax.ppermute(piece, ('mp', 'shot'), pairs))  17.5 us
    ppermute x7, waiting for transfers between devices, flip(): return lax.ppermute(value, 'shot', [(i, i ^ bit) for i in range(count)])  16 us
    ppermute x8, starting transfers between devices, swap(): lax.ppermute(v, 'mp', neighbours(count, start))  15.1 us
    ppermute x7, starting transfers between devices, flip(): return lax.ppermute(value, 'shot', [(i, i ^ bit) for i in range(count)])  10.1 us
    unnamed x51, local copies, waits for them, and re-layouts  8.47 us
  transfers between devices with their start and end apart: 23, of which 7 were waited for; matrix products, arithmetic and copies ran while one was open for 2% of the time, Pallas kernels for 22%

profile of v1, /device:TPU:0, one launch (start us, length us, event | category | flops | bytes accessed | tf_op | source)
XLA Modules:
  0.0 167.4 jit_solution(16348580701353517037)
XLA Ops:
  0.7 1.3 dynamic-slice_bitcast_fusion
  1.9 3.1 %collective-permute-start.2 = (f32[4,256,128]{2,1,0:T(8,128)S(1)}, f32[4,256,128]{2,1,0:T(8,128)S(1)}, u32[]{:S(2)}, u32[]{:S(2)}) collective-permute-start(f32[4,256,128]{2,1,0:T(8,128)S(1)} %get-tuple-element.69), channel_id=1, source_target_pairs={{0,4},{8,12},{4,0},{12,8},{1,5},{9,13},{5,1},{13,9},{2,6},{10,14},... | collective-permute-start | bytes 1572872 | tf_op jit(solution)/shard_map/ppermute | solution.py:666
  5.0 0.7 collective-permute-start.3
  5.7 1.3 dynamic-slice_bitcast_fusion.2
  7.0 4.4 %collective-permute-start = (f32[4,256,128]{2,1,0:T(8,128)S(1)}, f32[4,256,128]{2,1,0:T(8,128)}, u32[]{:S(2)}, u32[]{:S(2)}) collective-permute-start(f32[4,256,128]{2,1,0:T(8,128)S(1)} %get-tuple-element.71), channel_id=1, source_target_pairs={{0,4},{8,12},{4,0},{12,8},{1,5},{9,13},{5,1},{13,9},{2,6},{10,14},... | collective-permute-start | bytes 1572872 | tf_op jit(solution)/shard_map/ppermute | solution.py:666
  11.4 1.5 collective-permute-start.1
  12.9 0.6 stack.24.first_ref
  13.5 26.4 %step_one.1 = (f32[24,256,128]{2,1,0:T(8,128)}, f32[24,256,128]{2,1,0:T(8,128)}, f32[24,256,128]{2,1,0:T(8,128)}, f32[768,8,128]{2,1,0:T(8,128)}, f32[768,8,128]{2,1,0:T(8,128)}) custom-call(s32[8]{0:T(128)} %stack.24.first_ref, s32[1,64]{1,0:T(1,128)} %src_cell.1, s32[1,64]{1,0:T(1,128)} %src_sign.1, f32[1,2,64]{2,1,0:T(2,128)} %wavelet.1, s32[2048]{0:T(1024)} %rec_cell.1, ...), custom_call_target="tpu_custom_call" | custom-call | flops 10000000000 | bytes 41943040 | tf_op jit(solution)/shard_map/step_one/pallas_call | solution.py:246
  40.0 0.8 copy-done.3
  40.9 3.7 %correct.3 = (f32[4,256,128]{2,1,0:T(8,128)}, f32[4,256,128]{2,1,0:T(8,128)}) custom-call(s32[8]{0:T(128)} %stack.24.first_ref, f32[24,256,128]{2,1,0:T(8,128)} %courant.3, f32[24,256,128]{2,1,0:T(8,128)} %get-tuple-element.36.refs_1_.mid_in, f32[4,256,128]{2,1,0:T(8,128)} %copy-done.3, f32[4,256,128]{2,1,0:T(8,128)} %copy-done.4), custom_call_target="tpu_custom_call" | custom-call | flops 10000000 | bytes 6291456 | tf_op jit(solution)/shard_map/correct/pallas_call | solution.py:311
  44.7 4.3 %correct.2 = (f32[4,256,128]{2,1,0:T(8,128)}, f32[4,256,128]{2,1,0:T(8,128)}, f32[4,256,128]{2,1,0:T(8,128)}, f32[4,256,128]{2,1,0:T(8,128)}) custom-call(s32[8]{0:T(128)} %stack.24.first_ref, f32[24,256,128]{2,1,0:T(8,128)} %courant.3, f32[24,256,128]{2,1,0:T(8,128)} %get-tuple-element.34.refs_1_.accel_in, ...), custom_call_target="tpu_custom_call" | custom-call | flops 10000000 | bytes 6291456 | tf_op jit(solution)/shard_map/correct/pallas_call | solution.py:311
  49.0 18.3 %step_two.1 = (f32[16,2,64,128]{3,2,1,0:T(8,128)}, f32[16,2,64,128]{3,2,1,0:T(8,128)}, f32[2,4,256,128]{3,2,1,0:T(8,128)}, f32[2,4,256,128]{3,2,1,0:T(8,128)}, f32[2,4,256,128]{3,2,1,0:T(8,128)}) custom-call(s32[8]{0:T(128)} %stack.24.first_ref, f32[24,256,128]{2,1,0:T(8,128)} %courant.3, f32[24,256,128]{2,1,0:T(8,128)} %bitcast.19, ...), custom_call_target="tpu_custom_call" | custom-call | flops 10000000000 | bytes 41943040 | tf_op jit(solution)/shard_map/step_two/pallas_call | solution.py:404
  67.4 0.5 collective-permute-start.6
  67.9 0.7 collective-permute-start.7
  68.6 3.6 %collective-permute-start.4 = (f32[4,256,128]{2,1,0:T(8,128)S(1)}, f32[4,256,128]{2,1,0:T(8,128)S(1)}, u32[]{:S(2)}, u32[]{:S(2)}) collective-permute-start(f32[4,256,128]{2,1,0:T(8,128)S(1)} %copy-done.24), channel_id=1, source_target_pairs={{0,4},{8,12},{4,0},{12,8},{1,5},{9,13},{5,1},{13,9},{2,6},{10,14},... | collective-permute-start | bytes 1572872 | tf_op jit(solution)/shard_map/ppermute | solution.py:666
  72.2 0.7 collective-permute-start.5
  72.9 9.3 %collective-permute-done.6.a0 = f32[4,256,128]{2,1,0:T(8,128)S(1)} collective-permute-done((f32[4,256,128]{2,1,0:T(8,128)S(1)}, f32[4,256,128]{2,1,0:T(8,128)S(1)}, u32[]{:S(2)}, u32[]{:S(2)}) %collective-permute-start.6) | collective-permute-done | bytes 524320 | tf_op jit(solution)/shard_map/ppermute | solution.py:666
  82.2 10.8 %collective-permute-done.4.f0 = f32[4,256,128]{2,1,0:T(8,128)S(1)} collective-permute-done((f32[4,256,128]{2,1,0:T(8,128)S(1)}, f32[4,256,128]{2,1,0:T(8,128)S(1)}, u32[]{:S(2)}, u32[]{:S(2)}) %collective-permute-start.4) | collective-permute-done | bytes 524320 | tf_op jit(solution)/shard_map/ppermute | solution.py:666
  93.0 0.8 copy-done.7
  93.9 4.0 %finish.1 = (f32[8,2,64,128]{3,2,1,0:T(8,128)}, f32[8,2,64,128]{3,2,1,0:T(8,128)}) custom-call(s32[8]{0:T(128)} %stack.24.first_ref, f32[2,4,256,128]{3,2,1,0:T(8,128)} %get-tuple-element.45.edge, f32[2,4,256,128]{3,2,1,0:T(8,128)} %get-tuple-element.46.by_f, f32[2,4,256,128]{3,2,1,0:T(8,128)} %get-tuple-element.47.by_a, f32[4,256,128]{2,1,0:T(8,128)} %copy-done.7, ...), custom_call_target="tpu_custom_call" | custom-call | flops 10000000 | bytes 7340032 | tf_op jit(solution)/shard_map/finish/pallas_call | solution.py:447
  98.1 0.9 dynamic-slice_add_fusion
  99.0 1.5 collective-permute-start.11
  100.5 0.8 dynamic-slice_add_fusion.2
  101.3 1.1 collective-permute-start.9
  102.4 11.4 %collective-permute-done.11.got = f32[16,1,64,128]{3,2,1,0:T(8,128)S(1)} collective-permute-done((f32[16,1,64,128]{3,2,1,0:T(8,128)S(1)}, f32[16,1,64,128]{3,2,1,0:T(8,128)S(1)}, u32[]{:S(2)}, u32[]{:S(2)}) %collective-permute-start.11) | collective-permute-done | bytes 524320 | tf_op jit(solution)/shard_map/ppermute | solution.py:678
  113.7 0.8 copy-done.1
  114.5 3.2 %depth.2 = (f32[24,64,128]{2,1,0:T(8,128)}, f32[8,32,128]{2,1,0:T(8,128)}, f32[8,32,128]{2,1,0:T(8,128)}, f32[8,32,128]{2,1,0:T(8,128)}, f32[8,32,128]{2,1,0:T(8,128)}) custom-call(s32[8]{0:T(128)} %stack.24.first_ref, f32[16,1,64,128]{3,2,1,0:T(8,128)} %get-tuple-element.73.keep, f32[16,1,64,128]{3,2,1,0:T(8,128)} %copy-done.1, ...), custom_call_target="tpu_custom_call" | custom-call | flops 100000000 | bytes 2097152 | tf_op jit(solution)/shard_map/depth/pallas_call | solution.py:501
  117.7 1.2 collective-permute-done.9.got
  118.9 0.7 copy-done.9
  119.6 2.5 %depth.3 = (f32[24,64,128]{2,1,0:T(8,128)}, f32[4,32,128]{2,1,0:T(8,128)}, f32[4,32,128]{2,1,0:T(8,128)}, f32[4,32,128]{2,1,0:T(8,128)}, f32[4,32,128]{2,1,0:T(8,128)}) custom-call(s32[8]{0:T(128)} %stack.24.first_ref, f32[8,1,64,128]{3,2,1,0:T(8,128)} %get-tuple-element.75.keep, f32[8,1,64,128]{3,2,1,0:T(8,128)} %copy-done.9, ...), custom_call_target="tpu_custom_call", output_to_operand_aliasing={{0}: (5, {})} | custom-call | flops 100000000 | bytes 2097152 | tf_op jit(solution)/shard_map/depth/pallas_call | solution.py:501
  122.1 1.5 collective-permute-start.16
  123.6 4.0 %collective-permute-start.17 = (f32[4,32,128]{2,1,0:T(8,128)}, f32[4,32,128]{2,1,0:T(8,128)S(1)}, u32[]{:S(2)}, u32[]{:S(2)}) collective-permute-start(f32[4,32,128]{2,1,0:T(8,128)} %get-tuple-element.59), channel_id=1, source_target_pairs={{0,4},{1,8},{2,12},{3,0},{4,5},{5,9},{6,13},{7,1},{8,6},{9,10},{10... | collective-permute-start | bytes 196616 | tf_op jit(solution)/shard_map/ppermute | solution.py:709
  127.6 2.4 %collective-permute-start.18 = (f32[4,32,128]{2,1,0:T(8,128)}, f32[4,32,128]{2,1,0:T(8,128)S(1)}, u32[]{:S(2)}, u32[]{:S(2)}) collective-permute-start(f32[4,32,128]{2,1,0:T(8,128)} %get-tuple-element.60), channel_id=1, source_target_pairs={{0,8},{1,12},{2,0},{3,4},{4,9},{5,13},{6,1},{7,5},{8,10},{9,14},{1... | collective-permute-start | bytes 196616 | tf_op jit(solution)/shard_map/ppermute | solution.py:709
  130.0 1.6 collective-permute-start.12
  131.6 2.3 %collective-permute-start.13 = (f32[8,32,128]{2,1,0:T(8,128)}, f32[8,32,128]{2,1,0:T(8,128)S(1)}, u32[]{:S(2)}, u32[]{:S(2)}) collective-permute-start(f32[8,32,128]{2,1,0:T(8,128)} %get-tuple-element.55), channel_id=1, source_target_pairs={{0,4},{1,8},{2,12},{3,0},{4,5},{5,9},{6,13},{7,1},{8,6},{9,10},{10... | collective-permute-start | bytes 393224 | tf_op jit(solution)/shard_map/ppermute | solution.py:709
  133.9 0.9 collective-permute-start.14
  134.8 2.8 %collective-permute-start.15 = (f32[8,32,128]{2,1,0:T(8,128)}, f32[8,32,128]{2,1,0:T(8,128)S(1)}, u32[]{:S(2)}, u32[]{:S(2)}) collective-permute-start(f32[8,32,128]{2,1,0:T(8,128)} %get-tuple-element.57), channel_id=1, source_target_pairs={{0,12},{1,0},{2,4},{3,8},{4,13},{5,1},{6,5},{7,9},{8,14},{9,2},{10... | collective-permute-start | bytes 393224 | tf_op jit(solution)/shard_map/ppermute | solution.py:709
  137.6 2.0 %collective-permute-start.19 = (f32[4,32,128]{2,1,0:T(8,128)}, f32[4,32,128]{2,1,0:T(8,128)S(1)}, u32[]{:S(2)}, u32[]{:S(2)}) collective-permute-start(f32[4,32,128]{2,1,0:T(8,128)} %get-tuple-element.61), channel_id=1, source_target_pairs={{0,12},{1,0},{2,4},{3,8},{4,13},{5,1},{6,5},{7,9},{8,14},{9,2},{10... | collective-permute-start | bytes 196616 | tf_op jit(solution)/shard_map/ppermute | solution.py:709
  139.6 2.9 %collective-permute-done.19.refs_7_ = f32[4,32,128]{2,1,0:T(8,128)S(1)} collective-permute-done((f32[4,32,128]{2,1,0:T(8,128)}, f32[4,32,128]{2,1,0:T(8,128)S(1)}, u32[]{:S(2)}, u32[]{:S(2)}) %collective-permute-start.19) | collective-permute-done | bytes 65568 | tf_op jit(solution)/shard_map/ppermute | solution.py:709
  142.6 0.5 copy-done.17
  143.3 0.7 copy-done.13
  144.0 4.9 %rows.1 = (f32[24,32,256]{2,1,0:T(8,128)}, f32[32,256]{1,0:T(8,128)}, f32[32,256]{1,0:T(8,128)}, f32[32,256]{1,0:T(8,128)}) custom-call(s32[8]{0:T(128)} %stack.24.first_ref, f32[5,96]{1,0:T(8,128)} %constant.116.clone.scan, f32[8,32,128]{2,1,0:T(8,128)} %copy-done.10, f32[8,32,128]{2,1,0:T(8,128)} %copy-done.11, f32[8,32,128]{2,1,0:T(8,128)} %copy-done.12, ...), custom_call_target="tpu_custom_call" | custom-call | flops 100000000 | bytes 2097152 | tf_op jit(solution)/shard_map/rows/pallas_call | solution.py:607
  148.9 7.2 %collective-permute-start.21 = (f32[32,256]{1,0:T(8,128)}, f32[32,256]{1,0:T(8,128)S(1)}, u32[]{:S(2)}, u32[]{:S(2)}) collective-permute-start(f32[32,256]{1,0:T(8,128)} %get-tuple-element.64), channel_id=1, source_target_pairs={{0,2},{1,3},{2,0},{3,1},{4,6},{5,7},{6,4},{7,5},{8,10},{9,11},{10,... | collective-permute-start | bytes 98312 | tf_op jit(solution)/shard_map/ppermute | solution.py:678
  156.2 2.1 %collective-permute-done.21.refs_1_ = f32[32,256]{1,0:T(8,128)S(1)} collective-permute-done((f32[32,256]{1,0:T(8,128)}, f32[32,256]{1,0:T(8,128)S(1)}, u32[]{:S(2)}, u32[]{:S(2)}) %collective-permute-start.21) | collective-permute-done | bytes 32800 | tf_op jit(solution)/shard_map/ppermute | solution.py:678
  158.4 1.4 collective-permute-done.22.refs_2_
  159.7 0.6 copy-done.20
  160.3 4.0 %join.1 = f32[24,256,32]{2,1,0:T(8,128)} custom-call(s32[8]{0:T(128)} %stack.24.first_ref, f32[5,96]{1,0:T(8,128)} %constant.116.clone.scan, f32[4,4]{1,0:T(4,128)} %constant.117.clone.carry, f32[24,32,256]{2,1,0:T(8,128)} %get-tuple-element.62.part, f32[32,256]{1,0:T(8,128)} %copy-done.18, f32[32,256]{1,0:T(8,128)} %copy-done.19, f32[32,256]{1,0:T(8,128)} %copy-done.20, ...), custom_call_target="tpu_custom_call" | custom-call | flops 100000000 | bytes 2097152 | tf_op jit(solution)/shard_map/join/pallas_call | solution.py:648
  164.3 3.1 %copy.21 = f32[24,256,32]{1,2,0:T(8,128)} copy(f32[24,256,32]{2,1,0:T(8,128)} %join.1) | data formatting | bytes 1572864
  (63 shorter events, 0.9 us)
Async XLA Ops:
  1.9 38.0 %collective-permute-start.2 = (f32[4,256,128]{2,1,0:T(8,128)S(1)}, f32[4,256,128]{2,1,0:T(8,128)S(1)}, u32[]{:S(2)}, u32[]{:S(2)}) collective-permute-start(f32[4,256,128]{2,1,0:T(8,128)S(1)} %get-tuple-element.69), channel_id=1, source_target_pairs={{0,4},{8,12},{4,0},{12,8},{1,5},{9,13},{5,1},{13,9},{2,6},{10,14},... | collective-permute-start | bytes 1572872 | tf_op jit(solution)/shard_map/ppermute | solution.py:666
  5.0 34.9 %collective-permute-start.3 = (f32[4,256,128]{2,1,0:T(8,128)S(1)}, f32[4,256,128]{2,1,0:T(8,128)S(1)}, u32[]{:S(2)}, u32[]{:S(2)}) collective-permute-start(f32[4,256,128]{2,1,0:T(8,128)S(1)} %get-tuple-element.68), channel_id=1, source_target_pairs={{4,8},{8,4},{5,9},{9,5},{6,10},{10,6},{7,11},{11,7},{20,24},{24,20... | collective-permute-start | bytes 1572872 | tf_op jit(solution)/shard_map/ppermute | solution.py:666
  7.0 37.6 %collective-permute-start = (f32[4,256,128]{2,1,0:T(8,128)S(1)}, f32[4,256,128]{2,1,0:T(8,128)}, u32[]{:S(2)}, u32[]{:S(2)}) collective-permute-start(f32[4,256,128]{2,1,0:T(8,128)S(1)} %get-tuple-element.71), channel_id=1, source_target_pairs={{0,4},{8,12},{4,0},{12,8},{1,5},{9,13},{5,1},{13,9},{2,6},{10,14},... | collective-permute-start | bytes 1572872 | tf_op jit(solution)/shard_map/ppermute | solution.py:666
  11.4 33.2 %collective-permute-start.1 = (f32[4,256,128]{2,1,0:T(8,128)S(1)}, f32[4,256,128]{2,1,0:T(8,128)}, u32[]{:S(2)}, u32[]{:S(2)}) collective-permute-start(f32[4,256,128]{2,1,0:T(8,128)S(1)} %get-tuple-element.70), channel_id=1, source_target_pairs={{4,8},{8,4},{5,9},{9,5},{6,10},{10,6},{7,11},{11,7},{20,24},{24,20... | collective-permute-start | bytes 1572872 | tf_op jit(solution)/shard_map/ppermute | solution.py:666
  39.9 0.8 copy-start.3
  39.9 0.9 copy-start.4
  49.0 18.4 %copy-start.22 = (f32[4,256,128]{2,1,0:T(8,128)S(1)}, f32[4,256,128]{2,1,0:T(8,128)}, u32[]{:S(2)}) copy-start(f32[4,256,128]{2,1,0:T(8,128)} %get-tuple-element.43.m0) | copy-start | bytes 1572868
  49.0 18.9 %copy-start.21 = (f32[4,256,128]{2,1,0:T(8,128)S(1)}, f32[4,256,128]{2,1,0:T(8,128)}, u32[]{:S(2)}) copy-start(f32[4,256,128]{2,1,0:T(8,128)} %get-tuple-element.44.m1) | copy-start | bytes 1572868
  49.0 19.6 %copy-start.24 = (f32[4,256,128]{2,1,0:T(8,128)S(1)}, f32[4,256,128]{2,1,0:T(8,128)}, u32[]{:S(2)}) copy-start(f32[4,256,128]{2,1,0:T(8,128)} %get-tuple-element.39.f0) | copy-start | bytes 1572868
  49.0 23.2 %copy-start.23 = (f32[4,256,128]{2,1,0:T(8,128)S(1)}, f32[4,256,128]{2,1,0:T(8,128)}, u32[]{:S(2)}) copy-start(f32[4,256,128]{2,1,0:T(8,128)} %get-tuple-element.40.f1) | copy-start | bytes 1572868
  67.3 30.8 %copy-start = (f32[16,2,64,128]{3,2,1,0:T(8,128)S(1)}, f32[16,2,64,128]{3,2,1,0:T(8,128)}, u32[]{:S(2)}) copy-start(f32[16,2,64,128]{3,2,1,0:T(8,128)} %get-tuple-element.50) | copy-start | bytes 3145732
  67.3 30.8 %collective-permute-start.10 = (f32[16,2,64,128]{3,2,1,0:T(8,128)}, f32[16,2,64,128]{3,2,1,0:T(8,128)S(1)}, u32[]{:S(2)}, u32[]{:S(2)}) collective-permute-start(f32[16,2,64,128]{3,2,1,0:T(8,128)} %get-tuple-element.51), channel_id=1, source_target_pairs={{0,1},{1,0},{2,3},{3,2},{4,5},{5,4},{6,7},{7,6},{8,9},{9,8},{10,11... | collective-permute-start | bytes 3145736 | tf_op jit(solution)/shard_map/ppermute | solution.py:678
  67.4 14.8 %collective-permute-start.6 = (f32[4,256,128]{2,1,0:T(8,128)S(1)}, f32[4,256,128]{2,1,0:T(8,128)S(1)}, u32[]{:S(2)}, u32[]{:S(2)}) collective-permute-start(f32[4,256,128]{2,1,0:T(8,128)S(1)} %copy-done.22), channel_id=1, source_target_pairs={{0,4},{8,12},{4,0},{12,8},{1,5},{9,13},{5,1},{13,9},{2,6},{10,14},... | collective-permute-start | bytes 1572872 | tf_op jit(solution)/shard_map/ppermute | solution.py:666
  67.9 14.3 %collective-permute-start.7 = (f32[4,256,128]{2,1,0:T(8,128)S(1)}, f32[4,256,128]{2,1,0:T(8,128)S(1)}, u32[]{:S(2)}, u32[]{:S(2)}) collective-permute-start(f32[4,256,128]{2,1,0:T(8,128)S(1)} %copy-done.21), channel_id=1, source_target_pairs={{4,8},{8,4},{5,9},{9,5},{6,10},{10,6},{7,11},{11,7},{20,24},{24,20... | collective-permute-start | bytes 1572872 | tf_op jit(solution)/shard_map/ppermute | solution.py:666
  68.6 24.4 %collective-permute-start.4 = (f32[4,256,128]{2,1,0:T(8,128)S(1)}, f32[4,256,128]{2,1,0:T(8,128)S(1)}, u32[]{:S(2)}, u32[]{:S(2)}) collective-permute-start(f32[4,256,128]{2,1,0:T(8,128)S(1)} %copy-done.24), channel_id=1, source_target_pairs={{0,4},{8,12},{4,0},{12,8},{1,5},{9,13},{5,1},{13,9},{2,6},{10,14},... | collective-permute-start | bytes 1572872 | tf_op jit(solution)/shard_map/ppermute | solution.py:666
  72.2 20.8 %collective-permute-start.5 = (f32[4,256,128]{2,1,0:T(8,128)S(1)}, f32[4,256,128]{2,1,0:T(8,128)S(1)}, u32[]{:S(2)}, u32[]{:S(2)}) collective-permute-start(f32[4,256,128]{2,1,0:T(8,128)S(1)} %copy-done.23), channel_id=1, source_target_pairs={{4,8},{8,4},{5,9},{9,5},{6,10},{10,6},{7,11},{11,7},{20,24},{24,20... | collective-permute-start | bytes 1572872 | tf_op jit(solution)/shard_map/ppermute | solution.py:666
  82.2 10.8 %copy-start.5 = (f32[4,256,128]{2,1,0:T(8,128)}, f32[4,256,128]{2,1,0:T(8,128)S(1)}, u32[]{:S(2)}) copy-start(f32[4,256,128]{2,1,0:T(8,128)S(1)} %collective-permute-done.6.a0) | copy-start | bytes 1572868
  82.2 10.8 %copy-start.6 = (f32[4,256,128]{2,1,0:T(8,128)}, f32[4,256,128]{2,1,0:T(8,128)S(1)}, u32[]{:S(2)}) copy-start(f32[4,256,128]{2,1,0:T(8,128)S(1)} %collective-permute-done.7.a1) | copy-start | bytes 1572868
  93.0 0.8 copy-start.7
  93.0 1.0 copy-start.8
  97.9 2.6 %copy-start.2 = (f32[8,2,64,128]{3,2,1,0:T(8,128)S(1)}, f32[8,2,64,128]{3,2,1,0:T(8,128)}, u32[]{:S(2)}) copy-start(f32[8,2,64,128]{3,2,1,0:T(8,128)} %get-tuple-element.48) | copy-start | bytes 1572868
  97.9 2.6 %collective-permute-start.8 = (f32[8,2,64,128]{3,2,1,0:T(8,128)}, f32[8,2,64,128]{3,2,1,0:T(8,128)S(1)}, u32[]{:S(2)}, u32[]{:S(2)}) collective-permute-start(f32[8,2,64,128]{3,2,1,0:T(8,128)} %get-tuple-element.49), channel_id=1, source_target_pairs={{0,1},{1,0},{2,3},{3,2},{4,5},{5,4},{6,7},{7,6},{8,9},{9,8},{10,11... | collective-permute-start | bytes 1572872 | tf_op jit(solution)/shard_map/ppermute | solution.py:678
  99.0 14.7 %collective-permute-start.11 = (f32[16,1,64,128]{3,2,1,0:T(8,128)S(1)}, f32[16,1,64,128]{3,2,1,0:T(8,128)S(1)}, u32[]{:S(2)}, u32[]{:S(2)}) collective-permute-start(f32[16,1,64,128]{3,2,1,0:T(8,128)S(1)} %get-tuple-element.72), channel_id=1, source_target_pairs={{0,2},{1,3},{2,0},{3,1},{4,6},{5,7},{6,4},{7,5},{8,10},{9,11},{10,... | collective-permute-start | bytes 1572872 | tf_op jit(solution)/shard_map/ppermute | solution.py:678
  101.3 17.6 %collective-permute-start.9 = (f32[8,1,64,128]{3,2,1,0:T(8,128)S(1)}, f32[8,1,64,128]{3,2,1,0:T(8,128)S(1)}, u32[]{:S(2)}, u32[]{:S(2)}) collective-permute-start(f32[8,1,64,128]{3,2,1,0:T(8,128)S(1)} %get-tuple-element.74), channel_id=1, source_target_pairs={{0,2},{1,3},{2,0},{3,1},{4,6},{5,7},{6,4},{7,5},{8,10},{9,11},{10,... | collective-permute-start | bytes 786440 | tf_op jit(solution)/shard_map/ppermute | solution.py:678
  113.7 0.8 copy-start.1
  118.9 0.7 copy-start.9
  122.1 11.7 %collective-permute-start.16 = (f32[4,32,128]{2,1,0:T(8,128)}, f32[4,32,128]{2,1,0:T(8,128)S(1)}, u32[]{:S(2)}, u32[]{:S(2)}) collective-permute-start(f32[4,32,128]{2,1,0:T(8,128)} %get-tuple-element.58), channel_id=1, source_target_pairs={{0,0},{1,4},{2,8},{3,12},{4,1},{5,5},{6,9},{7,13},{8,2},{9,6},{10,... | collective-permute-start | bytes 196616 | tf_op jit(solution)/shard_map/ppermute | solution.py:709
  123.6 11.1 %collective-permute-start.17 = (f32[4,32,128]{2,1,0:T(8,128)}, f32[4,32,128]{2,1,0:T(8,128)S(1)}, u32[]{:S(2)}, u32[]{:S(2)}) collective-permute-start(f32[4,32,128]{2,1,0:T(8,128)} %get-tuple-element.59), channel_id=1, source_target_pairs={{0,4},{1,8},{2,12},{3,0},{4,5},{5,9},{6,13},{7,1},{8,6},{9,10},{10... | collective-permute-start | bytes 196616 | tf_op jit(solution)/shard_map/ppermute | solution.py:709
  127.6 10.0 %collective-permute-start.18 = (f32[4,32,128]{2,1,0:T(8,128)}, f32[4,32,128]{2,1,0:T(8,128)S(1)}, u32[]{:S(2)}, u32[]{:S(2)}) collective-permute-start(f32[4,32,128]{2,1,0:T(8,128)} %get-tuple-element.60), channel_id=1, source_target_pairs={{0,8},{1,12},{2,0},{3,4},{4,9},{5,13},{6,1},{7,5},{8,10},{9,14},{1... | collective-permute-start | bytes 196616 | tf_op jit(solution)/shard_map/ppermute | solution.py:709
  130.0 12.5 %collective-permute-start.12 = (f32[8,32,128]{2,1,0:T(8,128)}, f32[8,32,128]{2,1,0:T(8,128)S(1)}, u32[]{:S(2)}, u32[]{:S(2)}) collective-permute-start(f32[8,32,128]{2,1,0:T(8,128)} %get-tuple-element.54), channel_id=1, source_target_pairs={{0,0},{1,4},{2,8},{3,12},{4,1},{5,5},{6,9},{7,13},{8,2},{9,6},{10,... | collective-permute-start | bytes 393224 | tf_op jit(solution)/shard_map/ppermute | solution.py:709
  131.6 11.0 %collective-permute-start.13 = (f32[8,32,128]{2,1,0:T(8,128)}, f32[8,32,128]{2,1,0:T(8,128)S(1)}, u32[]{:S(2)}, u32[]{:S(2)}) collective-permute-start(f32[8,32,128]{2,1,0:T(8,128)} %get-tuple-element.55), channel_id=1, source_target_pairs={{0,4},{1,8},{2,12},{3,0},{4,5},{5,9},{6,13},{7,1},{8,6},{9,10},{10... | collective-permute-start | bytes 393224 | tf_op jit(solution)/shard_map/ppermute | solution.py:709
  133.9 8.8 %copy-start.14 = (f32[4,32,128]{2,1,0:T(8,128)}, f32[4,32,128]{2,1,0:T(8,128)S(1)}, u32[]{:S(2)}) copy-start(f32[4,32,128]{2,1,0:T(8,128)S(1)} %collective-permute-done.16.refs_4_) | copy-start | bytes 196612
  133.9 8.7 %collective-permute-start.14 = (f32[8,32,128]{2,1,0:T(8,128)}, f32[8,32,128]{2,1,0:T(8,128)S(1)}, u32[]{:S(2)}, u32[]{:S(2)}) collective-permute-start(f32[8,32,128]{2,1,0:T(8,128)} %get-tuple-element.56), channel_id=1, source_target_pairs={{0,8},{1,12},{2,0},{3,4},{4,9},{5,13},{6,1},{7,5},{8,10},{9,14},{1... | collective-permute-start | bytes 393224 | tf_op jit(solution)/shard_map/ppermute | solution.py:709
  134.8 7.9 %copy-start.15 = (f32[4,32,128]{2,1,0:T(8,128)}, f32[4,32,128]{2,1,0:T(8,128)S(1)}, u32[]{:S(2)}) copy-start(f32[4,32,128]{2,1,0:T(8,128)S(1)} %collective-permute-done.17.refs_5_) | copy-start | bytes 196612
  134.8 7.8 %collective-permute-start.15 = (f32[8,32,128]{2,1,0:T(8,128)}, f32[8,32,128]{2,1,0:T(8,128)S(1)}, u32[]{:S(2)}, u32[]{:S(2)}) collective-permute-start(f32[8,32,128]{2,1,0:T(8,128)} %get-tuple-element.57), channel_id=1, source_target_pairs={{0,12},{1,0},{2,4},{3,8},{4,13},{5,1},{6,5},{7,9},{8,14},{9,2},{10... | collective-permute-start | bytes 393224 | tf_op jit(solution)/shard_map/ppermute | solution.py:709
  137.6 5.0 %copy-start.16 = (f32[4,32,128]{2,1,0:T(8,128)}, f32[4,32,128]{2,1,0:T(8,128)S(1)}, u32[]{:S(2)}) copy-start(f32[4,32,128]{2,1,0:T(8,128)S(1)} %collective-permute-done.18.refs_6_) | copy-start | bytes 196612
  137.6 5.0 %collective-permute-start.19 = (f32[4,32,128]{2,1,0:T(8,128)}, f32[4,32,128]{2,1,0:T(8,128)S(1)}, u32[]{:S(2)}, u32[]{:S(2)}) collective-permute-start(f32[4,32,128]{2,1,0:T(8,128)} %get-tuple-element.61), channel_id=1, source_target_pairs={{0,12},{1,0},{2,4},{3,8},{4,13},{5,1},{6,5},{7,9},{8,14},{9,2},{10... | collective-permute-start | bytes 196616 | tf_op jit(solution)/shard_map/ppermute | solution.py:709
  142.5 0.6 copy-start.17
  142.6 0.7 copy-start.10
  142.6 0.7 copy-start.11
  142.6 0.7 copy-start.12
  143.3 0.7 copy-start.13
  148.8 7.4 %collective-permute-start.20 = (f32[32,256]{1,0:T(8,128)}, f32[32,256]{1,0:T(8,128)S(1)}, u32[]{:S(2)}, u32[]{:S(2)}) collective-permute-start(f32[32,256]{1,0:T(8,128)} %get-tuple-element.63), channel_id=1, source_target_pairs={{0,1},{1,0},{2,3},{3,2},{4,5},{5,4},{6,7},{7,6},{8,9},{9,8},{10,11... | collective-permute-start | bytes 98312 | tf_op jit(solution)/shard_map/ppermute | solution.py:678
  148.9 9.4 %collective-permute-start.21 = (f32[32,256]{1,0:T(8,128)}, f32[32,256]{1,0:T(8,128)S(1)}, u32[]{:S(2)}, u32[]{:S(2)}) collective-permute-start(f32[32,256]{1,0:T(8,128)} %get-tuple-element.64), channel_id=1, source_target_pairs={{0,2},{1,3},{2,0},{3,1},{4,6},{5,7},{6,4},{7,5},{8,10},{9,11},{10,... | collective-permute-start | bytes 98312 | tf_op jit(solution)/shard_map/ppermute | solution.py:678
  156.2 3.6 %collective-permute-start.22 = (f32[32,256]{1,0:T(8,128)}, f32[32,256]{1,0:T(8,128)S(1)}, u32[]{:S(2)}, u32[]{:S(2)}) collective-permute-start(f32[32,256]{1,0:T(8,128)} %get-tuple-element.65), channel_id=1, source_target_pairs={{0,3},{1,2},{2,1},{3,0},{4,7},{5,6},{6,5},{7,4},{8,11},{9,10},{10,... | collective-permute-start | bytes 98312 | tf_op jit(solution)/shard_map/ppermute | solution.py:678
  156.2 3.5 %copy-start.18 = (f32[32,256]{1,0:T(8,128)}, f32[32,256]{1,0:T(8,128)S(1)}, u32[]{:S(2)}) copy-start(f32[32,256]{1,0:T(8,128)S(1)} %collective-permute-done.20.refs_0_) | copy-start | bytes 98308
  158.4 1.4 copy-start.19
  159.7 0.6 copy-start.20

commit v2 on v1

v2 whole, which is shorter than its diff:
```python
import functools
import math

import jax
import jax.numpy as jnp
import ml_dtypes
import numpy as np
from jax import lax
from jax.experimental import pallas as pl
from jax.experimental.pallas import tpu as pltpu
from jax.sharding import PartitionSpec as P

SMOOTH_X = 32
SMOOTH_YZ = 4

COEFS = (8.0 / 5.0, -1.0 / 5.0, 8.0 / 315.0, -1.0 / 560.0)
CENTER = -205.0 / 72.0
REACH = len(COEFS)
SCALE = 5040.0
WHOLE = tuple(float(round(SCALE * a)) for a in COEFS)

LANES = 128
BF16 = jnp.bfloat16
F32 = jnp.float32
ANY = pl.BlockSpec(memory_space=pl.ANY)
VMEM = pl.BlockSpec(memory_space=pltpu.VMEM)
SMEM = pl.BlockSpec(memory_space=pltpu.SMEM)


def band(length):
    table = np.zeros((length, length), np.float32)
    for k, weight in enumerate(WHOLE, 1):
        near = np.arange(length - k)
        table[near, near + k] = weight
        table[near + k, near] = weight
    return table


def response(length, strength):
    counter = np.arange(1, length + 1, dtype=np.float64)
    half_sine = np.sin(np.pi * counter / (2 * (length + 1)))
    return 1.0 / (1.0 + strength * 4.0 * half_sine * half_sine)


def filter_matrix(length, strength):
    counter = np.arange(1, length + 1, dtype=np.float64)
    table = np.sin(np.pi * counter[:, None] * counter[None, :] / (length + 1))
    return 2.0 / (length + 1) * (table * response(length, strength)[None, :]) @ table


def scan_tables(length, strength, block):
    rate = math.acosh(1.0 + 0.5 / strength)
    index = np.arange(1, length + 1, dtype=np.float64)
    rise = np.sinh(rate * index)
    fall = np.sinh(rate * (length + 1 - index))
    whole = strength * math.sinh(rate) * math.sinh(rate * (length + 1))
    diag = rise * fall / whole
    left = np.concatenate([[0.0], rise[:-1] / rise[1:]])
    right = np.concatenate([fall[1:] / fall[:-1], [0.0]])
    first = (np.arange(length) // block) * block
    last = first + block - 1
    from_left = np.where(first > 0, rise[np.maximum(first - 1, 0)], 0.0) / rise
    from_right = np.where(last + 1 < length, fall[np.minimum(last + 1, length - 1)], 0.0) / fall
    rows = np.stack([diag, left, right, diag * from_left, diag * from_right])
    blocks = length // block
    carry = np.zeros((blocks, blocks))
    for here in range(blocks):
        for there in range(blocks):
            if there < here:
                carry[here, there] = rise[there * block + block - 1] / rise[here * block - 1]
            elif there > here:
                carry[here, there] = fall[there * block] / fall[here * block + block]
    return rows.astype(np.float32), carry.astype(np.float32)


def split_table(table):
    high = table.astype(np.float32).astype(ml_dtypes.bfloat16)
    low = (table - high.astype(np.float64)).astype(np.float32).astype(ml_dtypes.bfloat16)
    return jnp.asarray(high), jnp.asarray(low)


def split(value):
    high = value.astype(BF16)
    low = (value - high.astype(F32)).astype(BF16)
    return high, low


def dot(a, b):
    return jnp.dot(a, b, preferred_element_type=F32)


def dot_t(a, b):
    return lax.dot_general(a, b, (((1,), (1,)), ((), ())), preferred_element_type=F32)


def laplace_plane(field, p, band_y, band_z):
    here = field[p]
    width = here.shape[1]
    both = jnp.concatenate(split(here), axis=1)
    along_y = dot(band_y[...], both)
    along_z = dot(both, band_z[...])
    total = (3.0 * SCALE * CENTER) * here
    for k, weight in enumerate(WHOLE, 1):
        total += weight * (field[p + k] + field[p - k])
    return total + (along_y[:, :width] + along_y[:, width:]) + along_z


def divmod_fixed(value, size):
    if size & (size - 1) == 0:
        return lax.shift_right_logical(value, size.bit_length() - 1), value & (size - 1)
    return lax.div(value, size), lax.rem(value, size)


class Copies:
    def __init__(self, sems):
        self.sems, self.used = sems, 0

    def start(self, source, target):
        copy = pltpu.make_async_copy(source, target, self.sems.at[self.used])
        self.used += 1
        copy.start()
        return copy


def wait_all(copies):
    for copy in copies:
        copy.wait()


def chunk_bounds(rows):
    step = max(2 * REACH, -(-rows // 3))
    return [(low, min(low + step, rows)) for low in range(0, rows, step)]


def put_blocks(copies, buf, planes, shot, outs):
    return [copies.start(buf.at[planes, shot ^ j], out) for j, out in enumerate(outs)]


def step_one_kernel(
    first_ref, src_cell, src_sign, wavelet, rec_tile, rec_cell, rec_data,
    courant, f_old, f_now, a_late, a_now, band_y, band_z,
    c_buf, acc_buf, f_next, a_mid, a_base, s_second, near_out, keep_out,
    f_pad, a_pad, s_first, r_first, r_second, gt_buf, slot_buf, slots, found, slot_sem, sems,
):
    rows, ny, nz = courant.shape
    copies = Copies(sems)
    bounds = chunk_bounds(rows)

    def chunks(source, target, offset=0):
        return [
            copies.start(source.at[pl.ds(low, high - low)], target.at[pl.ds(low + offset, high - low)])
            for low, high in bounds
        ]

    loads = [chunks(f_now, f_pad, REACH), chunks(courant, c_buf), chunks(f_old, f_next, REACH)]
    late_loads = [chunks(a_now, a_pad, REACH), chunks(a_late, a_mid, REACH)]
    edge = jnp.zeros((REACH, ny, nz), F32)
    for pad in (f_pad, a_pad, f_next, a_mid):
        pad[:REACH] = edge
        pad[REACH + rows :] = edge

    group = ny // 8

    def clear(p, _):
        blank = jnp.zeros((group, 8, nz), F32)
        for ref in (s_first, r_first, s_second, r_second):
            ref[pl.ds(p * group, group)] = blank
        return 0

    lax.fori_loop(0, rows, clear, 0)

    start = first_ref[0]
    size = rows * ny * nz
    flat = lax.broadcasted_iota(jnp.int32, (8, nz), 0) * nz + lax.broadcasted_iota(jnp.int32, (8, nz), 1)

    def put(refs, local, values):
        tile, within = divmod_fixed(local, 8 * nz)
        spot = flat == within
        for ref, value in zip(refs, values, strict=True):
            ref[tile] = ref[tile] + jnp.where(spot, value, 0.0)

    nsrc = src_cell.shape[1]

    def one_source(i, _):
        local = src_cell[0, i] - start
        mine = (local >= 0) & (local < size)
        local = jnp.where(mine, local, 0)
        sign = jnp.where(mine, (2 * src_sign[0, i] - 1).astype(F32), 0.0)
        put((s_first, s_second), local, (sign * wavelet[0, 0, i], sign * wavelet[0, 1, i]))
        return 0

    lax.fori_loop(0, nsrc, one_source, 0, unroll=8 if nsrc % 8 == 0 else 1)

    nrec = rec_cell.shape[0]

    tiles = rec_tile.shape[0]
    local = rec_tile[...] - start
    inside = (local >= 0) & (local < size)
    marks = jnp.where(inside, 1.0, 0.0).astype(BF16)
    row, col = (lax.broadcasted_iota(jnp.int32, (LANES, LANES), d) for d in (0, 1))
    before = dot(marks, jnp.where(row < col, 1.0, 0.0).astype(BF16))
    sums = dot(marks, jnp.ones((LANES, LANES), BF16))
    row, col = (lax.broadcasted_iota(jnp.int32, (tiles, tiles), d) for d in (0, 1))
    above = dot(jnp.where(col < row, 1.0, 0.0).astype(BF16), sums.astype(BF16))
    count = jnp.sum(jnp.where(inside, 1.0, 0.0)).astype(jnp.int32)
    slot_buf[...] = jnp.where(inside, (before + above).astype(jnp.int32), nrec)
    fetch = pltpu.make_async_copy(slot_buf, slots, slot_sem)
    fetch.start()
    fetch.wait()
    batch = 32

    def look(g, _):
        tile = lax.div(g * batch, LANES)
        at = g * batch - tile * LANES
        places = [slots[tile, at + e] for e in range(batch)]
        for e, place in enumerate(places):
            found[place] = g * batch + e
        return 0

    lax.fori_loop(0, nrec // batch, look, 0)

    def receivers(g, valid):
        items = []
        for e in range(8):
            j = found[g * 8 + e]
            if valid is not None:
                j = jnp.where(e < valid, j, 0)
            items.append((rec_cell[j], rec_data[0, 0, j], rec_data[0, 1, j]))
        for e, (cell, first, second) in enumerate(items):
            place = cell - start
            if valid is not None:
                place = jnp.where(e < valid, place, 0)
                first = jnp.where(e < valid, first, 0.0)
                second = jnp.where(e < valid, second, 0.0)
            put((r_first, r_second), place, (first, second))
        return 0

    groups = lax.div(count, 8)
    lax.fori_loop(0, groups, lambda g, _: receivers(g, None), 0)
    receivers(groups, count - groups * 8)

    def forward(p, _):
        courant_here = c_buf[p] * (1.0 / SCALE)
        c_buf[p] = courant_here
        spike = s_first[pl.ds(p * group, group)].reshape(ny, nz)
        accel = courant_here * laplace_plane(f_pad, p + REACH, band_y, band_z) + spike
        acc_buf[p] = accel
        f_next[p + REACH] = (2.0 * f_pad[p + REACH] - f_next[p + REACH]) + accel
        return 0

    loads[0][0].wait()
    for i, (low, high) in enumerate(bounds):
        if i + 1 < len(bounds):
            loads[0][i + 1].wait()
        loads[1][i].wait()
        loads[2][i].wait()
        lax.fori_loop(low, high, forward, 0)

    def adjoint(p, _):
        spike = r_first[pl.ds(p * group, group)].reshape(ny, nz)
        change = c_buf[p] * laplace_plane(a_pad, p + REACH, band_y, band_z) + spike
        mid = (2.0 * a_pad[p + REACH] - a_mid[p + REACH]) + change
        a_mid[p + REACH] = mid
        later = r_second[pl.ds(p * group, group)].reshape(ny, nz)
        a_base[p] = (2.0 * mid - a_pad[p + REACH]) + later
        return 0

    late_loads[0][0].wait()
    for i, (low, high) in enumerate(bounds):
        if i + 1 < len(bounds):
            late_loads[0][i + 1].wait()
        late_loads[1][i].wait()
        lax.fori_loop(low, high, adjoint, 0)

    blocks = gt_buf.shape[1]

    def inner(i, _):
        p = i + 2 * REACH
        c = c_buf[p]
        here = pl.ds(p * group, group)
        mid = a_mid[p + REACH]
        accel = c * laplace_plane(f_next, p + REACH, band_y, band_z) + s_second[here].reshape(ny, nz)
        first = a_base[p] + c * laplace_plane(a_mid, p + REACH, band_y, band_z)
        gt_buf[i] = (first * acc_buf[p] + mid * accel).reshape(blocks, ny // blocks, nz)
        return 0

    lax.fori_loop(0, rows - 4 * REACH, inner, 0)
    bit = first_ref[2]
    stores = []
    for j in range(blocks // 2):
        stores.append(copies.start(gt_buf.at[:, 2 * j + 1 - bit], near_out.at[:, j]))
        stores.append(copies.start(gt_buf.at[:, 2 * j + bit], keep_out.at[:, j]))
    wait_all(stores)


def cheap(megabytes):
    return pltpu.CompilerParams(vmem_limit_bytes=megabytes * 2**20)


COST = pl.CostEstimate(flops=1000, bytes_accessed=1000, transcendentals=0)
LONG = pl.CostEstimate(flops=10**12, bytes_accessed=1000, transcendentals=0)


def held(*shape):
    return pltpu.VMEM(shape, F32)


def in_hbm(arrays):
    return [pltpu.with_memory_space_constraint(array, pltpu.HBM) for array in arrays]


def keep_held(arrays):
    return [pltpu.with_memory_space_constraint(array, pltpu.VMEM) for array in arrays]


def step_one(first, src_cell, src_sign, wavelet, rec_cell, rec_data, courant, f_old, f_now, a_late, a_now, bands, shots):
    rows, ny, nz = courant.shape
    half = jax.ShapeDtypeStruct((rows - 4 * REACH, shots // 2, ny // shots, nz), F32)
    whole, padded, sparse = (rows, ny, nz), (rows + 2 * REACH, ny, nz), (rows * ny // 8, 8, nz)
    nrec = rec_cell.shape[0]
    return pl.pallas_call(
        step_one_kernel,
        out_shape=tuple(held(*shape) for shape in (whole, whole, padded, padded, whole, sparse)) + (half, half),
        in_specs=[SMEM] * 4 + [VMEM] + [SMEM] * 2 + [ANY] * 5 + [VMEM] * 2,
        out_specs=(VMEM,) * 6 + (ANY,) * 2,
        scratch_shapes=[
            held(*padded), held(*padded), held(*sparse), held(*sparse), held(*sparse),
            held(rows - 4 * REACH, shots, ny // shots, nz),
            pltpu.VMEM((nrec // LANES, LANES), jnp.int32),
            pltpu.SMEM((nrec // LANES, LANES), jnp.int32),
            pltpu.SMEM((nrec + 16,), jnp.int32),
            pltpu.SemaphoreType.DMA,
            pltpu.SemaphoreType.DMA((5 * len(chunk_bounds(rows)) + shots,)),
        ],
        compiler_params=cheap(22),
        cost_estimate=LONG,
        name="step_one",
    )(
        first, src_cell, src_sign, wavelet, rec_cell.reshape(-1, LANES), rec_cell, rec_data,
        *in_hbm((courant, f_old, f_now, a_late, a_now)), *bands,
    )


def sides(first_ref, rows):
    even = first_ref[1] == 0
    high = rows - REACH
    return (jnp.where(even, high, 0), even), (jnp.where(even, 0, high), jnp.logical_not(even))


def halo_sum(halo, q, upper):
    total = None
    for k, weight in enumerate(WHOLE, 1):
        if q + k >= REACH:
            h = q + k - REACH
            term = weight * halo[jnp.where(upper, h, REACH - 1 - h)]
            total = term if total is None else total + term
    return total


def pick_kernel(first_ref, f_now, a_now, *refs):
    outs, sems = refs[:2], refs[2]
    copies = Copies(sems)
    wait_all([
        copies.start(field.at[pl.ds(base, REACH)], outs[s].at[i])
        for s, (base, _) in enumerate(sides(first_ref, f_now.shape[0]))
        for i, field in enumerate((f_now, a_now))
    ])


def pick(first, f_now, a_now):
    _, ny, nz = f_now.shape
    both = jax.ShapeDtypeStruct((2, REACH, ny, nz), F32)
    return pl.pallas_call(
        pick_kernel,
        out_shape=(both, both),
        in_specs=[SMEM] + [ANY] * 2,
        out_specs=(VMEM,) * 2,
        scratch_shapes=[pltpu.SemaphoreType.DMA((4,))],
        compiler_params=cheap(8),
        cost_estimate=COST,
        name="pick",
    )(first, *in_hbm((f_now, a_now)))


def correct_kernel(
    first_ref, c_buf, acc_in, next_in, mid_in, base_in, halo0, halo1, keep, near, acc_buf, f_next, a_mid, a_base, *refs
):
    edges, terms, sems = refs[:2], refs[2:-1], refs[-1]
    rows = c_buf.shape[0]
    copies = Copies(sems)
    shot = first_ref[6]
    stores = []
    for s, (base, upper) in enumerate(sides(first_ref, rows)):
        halo = (halo0, halo1)[s]
        for q in range(REACH):
            here = base + jnp.where(upper, q, REACH - 1 - q)
            c = c_buf[here]
            change = c * halo_sum(halo.at[0], q, upper)
            acc_buf[here] = acc_in[here] + change
            f_next[here + REACH] = next_in[here + REACH] + change
            change = c * halo_sum(halo.at[1], q, upper)
            a_mid[here + REACH] = mid_in[here + REACH] + change
            a_base[here] = base_in[here] + 2.0 * change
        inside = pl.ds(base + REACH, REACH)
        stores.append(copies.start(f_next.at[inside], edges[s].at[0]))
        stores.append(copies.start(a_mid.at[inside], edges[s].at[1]))
    for i, term in enumerate(terms):
        block = lax.div(shot ^ (2 * i), 2)
        term[...] = keep[:, block] + near[:, block]
    wait_all(stores)


def correct(first, c, accel, nxt, mid, a_base, halos, keep, near):
    rows, ny, nz = c.shape
    both = jax.ShapeDtypeStruct((2, REACH, ny, nz), F32)
    planes, blocks, yb, _ = keep.shape
    term = jax.ShapeDtypeStruct((planes, yb, nz), F32)
    return pl.pallas_call(
        correct_kernel,
        out_shape=tuple(held(*array.shape) for array in (accel, nxt, mid, a_base)) + (both, both) + (term,) * blocks,
        in_specs=[SMEM] + [VMEM] * 9,
        out_specs=(VMEM,) * 4 + (ANY,) * 2 + (VMEM,) * blocks,
        scratch_shapes=[pltpu.SemaphoreType.DMA((4,))],
        input_output_aliases={2: 0, 3: 1, 4: 2, 5: 3},
        compiler_params=cheap(8),
        cost_estimate=COST,
        name="correct",
    )(first, *keep_held((c, accel, nxt, mid, a_base)), *halos, keep, near)


def step_two_kernel(waits, first_ref, c_buf, acc_buf, f_next, a_mid, a_base, s_buf, band_y, band_z, *refs):
    edge_out, by_f, by_a, *terms_out = refs[waits:-2]
    gt_buf, sems = refs[-2:]
    rows, ny, nz = c_buf.shape
    copies = Copies(sems)
    group = ny // 8
    blocks = gt_buf.shape[1]

    def plane(p, _):
        c = c_buf[p]
        here = pl.ds(p * group, group)
        mid = a_mid[p + REACH]
        accel = c * laplace_plane(f_next, p + REACH, band_y, band_z) + s_buf[here].reshape(ny, nz)
        first = a_base[p] + c * laplace_plane(a_mid, p + REACH, band_y, band_z)
        gt_buf[p] = (first * acc_buf[p] + mid * accel).reshape(blocks, ny // blocks, nz)
        return 0

    stores = []
    shot = first_ref[6]
    for i, low in enumerate((REACH, rows - 2 * REACH)):
        lax.fori_loop(low, low + REACH, plane, 0)
        outs = [out.at[pl.ds(i * REACH, REACH)] for out in terms_out]
        stores += put_blocks(copies, gt_buf, pl.ds(low, REACH), shot, outs)
    for low in (0, rows - REACH):
        lax.fori_loop(low, low + REACH, plane, 0)
    for s, (base, _) in enumerate(sides(first_ref, rows)):
        for q in range(REACH):
            c = c_buf[base + q]
            by_f[s, q] = c * a_mid[base + q + REACH]
            by_a[s, q] = c * acc_buf[base + q]
            edge_out[s, q] = gt_buf[base + q].reshape(ny, nz)
    wait_all(stores)


def step_two(first, arrays, bands, after, shots):
    rows, ny, nz = arrays[0].shape
    edge = jax.ShapeDtypeStruct((2, REACH, ny, nz), F32)
    term = jax.ShapeDtypeStruct((2 * REACH, ny // shots, nz), F32)
    return pl.pallas_call(
        functools.partial(step_two_kernel, len(after)),
        out_shape=(edge, edge, edge) + (term,) * shots,
        in_specs=[SMEM] + [VMEM] * 8 + [ANY] * len(after),
        out_specs=(VMEM,) * 3 + (ANY,) * shots,
        scratch_shapes=[held(rows, shots, ny // shots, nz), pltpu.SemaphoreType.DMA((2 * shots,))],
        compiler_params=cheap(12),
        cost_estimate=LONG,
        name="step_two",
    )(first, *keep_held(arrays), *bands, *after)


def finish_kernel(first_ref, edge, by_f, by_a, halo0, halo1, *refs):
    outs, buf = refs[:-1], refs[-1]
    blocks = buf.shape[1]
    _, reach, ny, nz = edge.shape
    for s, (_, upper) in enumerate(sides(first_ref, first_ref[3])):
        halo = (halo0, halo1)[s]
        for q in range(reach):
            here = jnp.where(upper, q, reach - 1 - q)
            total = edge[s, here] + by_f[s, here] * halo_sum(halo.at[0], q, upper)
            total += by_a[s, here] * halo_sum(halo.at[1], q, upper)
            buf[s * reach + here] = total.reshape(blocks, ny // blocks, nz)
    for j, out in enumerate(outs):
        out[...] = buf[:, first_ref[6] ^ j]


def finish(first, edge, by_f, by_a, halos, shots):
    _, reach, ny, nz = edge.shape
    term = jax.ShapeDtypeStruct((2 * reach, ny // shots, nz), F32)
    return pl.pallas_call(
        finish_kernel,
        out_shape=(term,) * shots,
        in_specs=[SMEM] + [VMEM] * 5,
        out_specs=(VMEM,) * shots,
        scratch_shapes=[pltpu.VMEM((2 * reach, shots, ny // shots, nz), F32)],
        compiler_params=cheap(16),
        cost_estimate=LONG,
        name="finish",
    )(first, edge, by_f, by_a, *halos)


def depth_kernel(layout, parts, pieces, first_ref, *refs):
    used = sum(len(offsets) for offsets in parts)
    terms, refs = refs[:used], refs[used:]
    z_high, z_low = refs[:2]
    raw_out, outs, (raw_buf, spectrum, sems) = refs[-pieces - 4], refs[-pieces - 3 : -3], refs[-3:]
    planes, yb, nz = raw_buf.shape
    shots = first_ref[4].astype(F32)
    copies = Copies(sems)
    low, at = 0, 0
    for chunk, offsets in zip(layout, parts, strict=True):
        size = sum(count for _, count in chunk)
        total = None
        for offset in offsets:
            term = terms[at][offset : offset + size]
            total = term if total is None else total + term
            at += 1
        raw_buf[low : low + size] = total / shots
        low += size
    stores, done = [], 0
    rows = raw_out.shape[0]
    for chunk in layout:
        for where, count in chunk:
            base = sides(first_ref, rows)[where][0] if isinstance(where, bool) else where
            stores.append(copies.start(raw_buf.at[pl.ds(done, count)], raw_out.at[pl.ds(base, count)]))
            done += count
    lanes = LANES // yb
    count = planes // lanes
    zb = nz // pieces
    for p in range(count):
        rows_here = jnp.concatenate([raw_buf[h * count + p] for h in range(lanes)], axis=0)
        high, low_part = split(rows_here)
        table = z_high[...]
        spectrum[p] = (dot_t(table, high) + dot_t(table, low_part) + dot_t(z_low[...], high)).reshape(pieces, zb, LANES)
    offset = first_ref[5]
    for k, out in enumerate(outs):
        out[...] = spectrum[:, lax.rem(offset + k, pieces)]
    wait_all(stores)


def depth(first, layout, terms, tables, raw_shape, pieces, after=(), previous=None):
    planes = sum(count for chunk in layout for _, count in chunk)
    _, yb, nz = raw_shape
    lanes = LANES // yb
    count = planes // lanes
    piece = jax.ShapeDtypeStruct((count, nz // pieces, LANES), F32)
    extra = (*after, *(() if previous is None else (previous,)))
    flat = [term for chunk in terms for term, _ in chunk]
    offsets = [[offset for _, offset in chunk] for chunk in terms]
    last = 1 + len(flat) + 2 + len(extra) - 1
    return pl.pallas_call(
        functools.partial(depth_kernel, layout, offsets, pieces),
        out_shape=(jax.ShapeDtypeStruct(raw_shape, F32),) + (piece,) * pieces,
        in_specs=[SMEM] + [VMEM] * (len(flat) + 2) + [ANY] * len(extra),
        out_specs=(ANY,) + (VMEM,) * pieces,
        scratch_shapes=[
            pltpu.VMEM((planes, yb, nz), F32),
            pltpu.VMEM((count, pieces, nz // pieces, LANES), F32),
            pltpu.SemaphoreType.DMA((sum(len(chunk) for chunk in layout),)),
        ],
        input_output_aliases={} if previous is None else {last: 0},
        compiler_params=cheap(16),
        cost_estimate=LONG,
        name="depth",
    )(first, *flat, *tables, *extra)


def gather_kernel(pieces, ratio, shots, count, plane_of, first_ref, *refs):
    parts, (y_high, y_low, out, buf, field, sems) = refs[:pieces], refs[pieces:]
    mp, shot = first_ref[7], first_ref[6]
    copies = Copies(sems)
    loads = []
    for k in range(pieces):
        q = lax.rem(mp - k + pieces, pieces)
        loads.append(copies.start(parts[k], buf.at[lax.rem(q, ratio), lax.div(q, ratio)]))
    wait_all(loads)
    _, zb, ny = field.shape
    yb = ny // shots
    lanes = LANES // yb
    slot_of = lax.broadcasted_iota(jnp.int32, (zb, LANES), 1) // yb
    for sub in range(ratio):
        for p in range(count):
            for h in range(lanes):
                x = sub * count * lanes + h * count + p
                for t in range(shots // lanes):
                    value = None
                    for e in range(lanes):
                        piece = buf[sub, t * lanes + e, p]
                        if e != h:
                            piece = pltpu.roll(piece, (e - h) * yb % LANES, 1)
                        value = piece if value is None else jnp.where(slot_of == e, piece, value)
                    field[x, :, pl.ds(t * LANES, LANES)] = value
    filter_second(field, out, y_high[...], y_low[...])


def filter_second(field, out, high_t, low_t):
    total, zb, ny = field.shape
    step = max(1, 256 // zb)
    while total % step:
        step -= 1
    for i in range(0, total, step):
        high, low = split(field[i : i + step].reshape(step * zb, ny))
        result = dot_t(high, high_t) + dot_t(low, high_t) + dot_t(high, low_t)
        out[i : i + step] = result.reshape(step, zb, ny)


def gather(first, parts, tables, ratio, shots):
    pieces = len(parts)
    count, zb, _ = parts[0].shape
    ny = tables[0].shape[0]
    total = ratio * count * (LANES * shots // ny)
    return pl.pallas_call(
        functools.partial(gather_kernel, pieces, ratio, shots, count, None),
        out_shape=jax.ShapeDtypeStruct((total, zb, ny), F32),
        in_specs=[SMEM] + [ANY] * pieces + [VMEM] * 2,
        out_specs=VMEM,
        scratch_shapes=[
            pltpu.VMEM((ratio, shots, count, zb, LANES), F32),
            pltpu.VMEM((total, zb, ny), F32),
            pltpu.SemaphoreType.DMA((pieces,)),
        ],
        compiler_params=cheap(16),
        cost_estimate=LONG,
        name="gather",
    )(first, *parts, *tables)


def scan_kernel(planes, rows, shots, first_ref, scan, mains, edges, out, *refs):
    sends, (field, ends) = refs[: shots - 1], refs[shots - 1 :]
    shot = first_ref[6]
    total, zb, ny = field.shape
    ratio = total // rows
    per_slab = len(planes)
    for sub in range(ratio):
        for i, x in enumerate(planes):
            field[sub * rows + x] = mains[sub * per_slab + i]
        even = lax.rem(shot * ratio + sub, 2) == 0
        for s, base in enumerate((jnp.where(even, rows - REACH, 0), jnp.where(even, 0, rows - REACH))):
            for q in range(REACH):
                field[sub * rows + base + q] = edges[sub * 2 * REACH + s * REACH + q]
    first_x = shot * total

    def up(x, carry):
        carry = field[x] + scan[1, first_x + x] * carry
        out[x] = carry
        return carry

    ends[0] = lax.fori_loop(0, total, up, jnp.zeros((zb, ny), F32))

    def down(i, carry):
        x = total - 1 - i
        out[x] = (out[x] + carry) * scan[0, first_x + x]
        return scan[2, first_x + x - 1] * (field[x] + carry)

    carry = lax.fori_loop(0, total - 1, down, jnp.zeros((zb, ny), F32))
    out[0] = (out[0] + carry) * scan[0, first_x]
    ends[1] = field[0] + carry
    for j, send in enumerate(sends, 1):
        send[...] = jnp.where((shot ^ j) > shot, ends[0], ends[1])


def scan_first(first, scan, mains, edges, planes, rows, shots):
    per_slab = len(planes)
    ratio = mains.shape[0] // per_slab
    _, zb, ny = mains.shape
    end = jax.ShapeDtypeStruct((zb, ny), F32)
    total = rows * ratio
    return pl.pallas_call(
        functools.partial(scan_kernel, planes, rows, shots),
        out_shape=(jax.ShapeDtypeStruct((total, zb, ny), F32),) + (end,) * (shots - 1),
        in_specs=[SMEM] * 2 + [VMEM] * 2,
        out_specs=(VMEM,) * shots,
        scratch_shapes=[pltpu.VMEM((total, zb, ny), F32), pltpu.VMEM((2, zb, ny), F32)],
        compiler_params=cheap(16),
        cost_estimate=COST,
        name="scan",
    )(first, scan, mains, edges)


def join_kernel(shots, first_ref, scan, carry, part, *refs):
    ends, out = refs[: shots - 1], refs[shots - 1]
    total, zb, ny = part.shape
    shot = first_ref[6]
    first_x = shot * total
    below = jnp.zeros((zb, ny), F32)
    above = jnp.zeros((zb, ny), F32)
    for j, end in enumerate(ends, 1):
        other = shot ^ j
        term = carry[shot, other] * end[...]
        below += jnp.where(other < shot, term, 0.0)
        above += jnp.where(other > shot, term, 0.0)
    for x in range(total):
        out[x] = part[x] + scan[3, first_x + x] * below + scan[4, first_x + x] * above


def join(first, scan, carry, part, ends):
    total, zb, ny = part.shape
    shots = len(ends) + 1
    return pl.pallas_call(
        functools.partial(join_kernel, shots),
        out_shape=jax.ShapeDtypeStruct((total, zb, ny), F32),
        in_specs=[SMEM] * 3 + [VMEM] * shots,
        out_specs=VMEM,
        compiler_params=cheap(16),
        cost_estimate=COST,
        name="join",
    )(first, scan, carry, part, *ends)


def neighbours(count, start):
    low = range(start, count - 1, 2)
    return [(i, i + 1) for i in low] + [(i + 1, i) for i in low]


def swap(values):
    count = lax.axis_size("mp")
    return tuple(lax.ppermute(v, "mp", neighbours(count, start)) for start, v in enumerate(values))


def flip(value, bit):
    count = lax.axis_size("shot")
    return lax.ppermute(value, "shot", [(i, i ^ bit) for i in range(count)])


def share(terms):
    return [terms[0]] + [flip(term, j) for j, term in enumerate(terms[1:], 1)]


def spread(pieces, ratio):
    mp, shots = lax.axis_size("mp"), lax.axis_size("shot")
    out = []
    for k, piece in enumerate(pieces):
        pairs = []
        for m in range(mp):
            for s in range(shots):
                target = (s * ratio + m % ratio + k) % mp
                pairs.append((m * shots + s, target * shots + m // ratio))
        out.append(lax.ppermute(piece, ("mp", "shot"), pairs))
    return out


def per_device(
    courant, forward_old, forward_now, adjoint_late, adjoint_now,
    src_cell, src_sign, wavelet, rec_cell, rec_data,
):
    mp_count, shots = lax.axis_size("mp"), lax.axis_size("shot")
    mp, shot = lax.axis_index("mp"), lax.axis_index("shot")
    rows, ny, nz = courant.shape
    ratio = mp_count // shots
    full_x = rows * mp_count
    first = jnp.stack(
        [
            mp * (rows * ny * nz), mp % 2, shot % 2, jnp.int32(rows), jnp.int32(shots),
            shot * ratio + mp % ratio, shot, mp,
        ]
    ).astype(jnp.int32)
    band_y, band_z = band(ny), band(nz)
    bands = (jnp.asarray(band_y, BF16), jnp.asarray(np.concatenate([band_z, band_z]), BF16))
    strength = float(SMOOTH_YZ * SMOOTH_YZ)
    strength_x = float(SMOOTH_X * SMOOTH_X)
    scan, carry = scan_tables(full_x, strength_x, rows * ratio)
    kappa = 1.0
    for length, e in ((full_x, strength_x), (ny, strength), (nz, strength)):
        resp = response(length, e)
        kappa /= math.sqrt(np.mean(resp * resp))
    z_tables = split_table(filter_matrix(nz, strength))
    y_tables = split_table(kappa * filter_matrix(ny, strength))

    f_old, f_now, a_late, a_now = forward_old[0], forward_now[0], adjoint_late[0], adjoint_now[0]
    halos = swap(pick(first, f_now, a_now))
    c, accel, nxt, mid, a_base, src, near, keep = step_one(
        first, src_cell, src_sign, wavelet, rec_cell, rec_data, courant, f_old, f_now, a_late, a_now, bands, shots
    )
    accel, nxt, mid, a_base, edge0, edge1, *inner = correct(
        first, c, accel, nxt, mid, a_base, halos, keep, flip(near, 1)
    )
    halos = swap((edge0, edge1))
    inner = [inner[0]] + [flip(term, 2 * i) for i, term in enumerate(inner[1:], 1)]
    edge, by_f, by_a, *outer = step_two(first, (c, accel, nxt, mid, a_base, src), bands, inner[1:], shots)
    outer = share(outer)
    last = share(finish(first, edge, by_f, by_a, halos, shots))
    raw_shape = (rows, ny // shots, nz)
    layout = [[(2 * REACH, rows - 4 * REACH)], [(REACH, REACH), (rows - 2 * REACH, REACH)]]
    terms = [[(term, 0) for term in inner], [(term, 0) for term in outer]]
    raw, *mains = depth(first, layout, terms, z_tables, raw_shape, mp_count)
    mains = gather(first, spread(mains, ratio), y_tables, ratio, shots)
    layout_edge = [[(False, REACH), (True, REACH)]]
    terms = [[(term, 0) for term in last]]
    raw, *edges = depth(first, layout_edge, terms, z_tables, raw_shape, mp_count, (), raw)
    edges = gather(first, spread(edges, ratio), y_tables, ratio, shots)
    planes = [low + i for chunk in layout for low, count in chunk for i in range(count)]
    part, *ends = scan_first(first, jnp.asarray(scan), mains, edges, planes, rows, shots)
    ends = [flip(end, j) for j, end in enumerate(ends, 1)]
    smooth = join(first, jnp.asarray(scan), jnp.asarray(carry), part, ends)
    smooth = jnp.transpose(smooth, (0, 2, 1))
    return raw, smooth


def solution(mesh):
    return jax.shard_map(
        per_device,
        mesh=mesh,
        in_specs=(
            P(("parts", "mp"), None, None),
            P(("parts", "shot"), "mp", None, None),
            P(("parts", "shot"), "mp", None, None),
            P(("parts", "shot"), "mp", None, None),
            P(("parts", "shot"), "mp", None, None),
            P(("parts", "shot"), None),
            P(("parts", "shot"), None),
            P(("parts", "shot"), None, None),
            P("parts"),
            P(("parts", "shot"), None, None),
        ),
        out_specs=(P(("parts", "mp"), "shot", None), P(("parts", "shot"), None, "mp")),
        check_vma=False,
    )
```

time: 168 us -> 119 us (0.71)
  waiting for transfers between devices: 39.1 us -> 18.6 us
  Pallas kernels: 71.3 us -> 57 us
  local copies, waits for them, and re-layouts: 11.6 us -> 0.15 us
  other arithmetic: 1.69 us -> 0 us
    pallas_call x8 -> x10, Pallas kernels: 67.3 us -> 55.3 us  [the longest x1 27.9 us: step_one(): pl.pallas_call(step_one_kernel, out_shape=tuple((held(*shape) for shape i...]
    ppermute x7 -> x11, waiting for transfers between devices: 16 us -> 6.38 us  [flip(): return lax.ppermute(value, 'shot', [(i, i ^ bit) for i in range(count)])]
    unnamed x51 -> x26, local copies, waits for them, and re-layouts: 8.47 us -> 0.07 us
    ppermute x8 -> x4, waiting for transfers between devices: 20.1 us -> 12.1 us  [swap(): lax.ppermute(v, 'mp', neighbours(count, start))]
    ppermute x8, starting transfers between devices: 17.5 us -> 24.9 us  [spread(): out.append(lax.ppermute(piece, ('mp', 'shot'), pairs))]
    ppermute x8 -> x4, starting transfers between devices: 15.1 us -> 10 us  [swap(): lax.ppermute(v, 'mp', neighbours(count, start))]
    ppermute x8, waiting for transfers between devices: 2.93 us -> 0.04 us  [spread(): out.append(lax.ppermute(piece, ('mp', 'shot'), pairs))]
    ppermute x7 -> x11, starting transfers between devices: 10.1 us -> 7.35 us  [flip(): return lax.ppermute(value, 'shot', [(i, i ^ bit) for i in range(count)])]
  transfers between devices with their start and end apart: 23 -> 23, of which waited for: 7 -> 5; matrix products, arithmetic and copies ran while one was open for 2% -> 0% of each run, Pallas kernels for 22% -> 38%
where the time goes in v2:
time: 119 us
  Pallas kernels  57 us (48%)
  starting transfers between devices  42.3 us (36%)
  waiting for transfers between devices  18.6 us (16%)
    pallas_call x1, Pallas kernels, step_one(): pl.pallas_call(step_one_kernel, out_shape=tuple((held(*shape) for shape i...  27.9 us
    ppermute x8, starting transfers between devices, spread(): out.append(lax.ppermute(piece, ('mp', 'shot'), pairs))  24.9 us
    ppermute x4, waiting for transfers between devices, swap(): lax.ppermute(v, 'mp', neighbours(count, start))  12.1 us
    ppermute x4, starting transfers between devices, swap(): lax.ppermute(v, 'mp', neighbours(count, start))  10 us
    ppermute x11, starting transfers between devices, flip(): return lax.ppermute(value, 'shot', [(i, i ^ bit) for i in range(count)])  7.35 us
    ppermute x11, waiting for transfers between devices, flip(): return lax.ppermute(value, 'shot', [(i, i ^ bit) for i in range(count)])  6.38 us
    pallas_call x1, Pallas kernels, step_two(): pl.pallas_call(functools.partial(step_two_kernel, len(after)), out_shape=...  6.23 us
    pallas_call x2, Pallas kernels, depth(): pl.pallas_call(functools.partial(depth_kernel, layout, offsets, pieces),...  6.12 us
  transfers between devices with their start and end apart: 23, of which 5 were waited for; matrix products, arithmetic and copies ran while one was open for 0% of the time, Pallas kernels for 38%

profile of v2, /device:TPU:0, one launch (start us, length us, event | category | flops | bytes accessed | tf_op | source)
XLA Modules:
  0.0 118.9 jit_solution(6383327650993294997)
XLA Ops:
  0.6 0.1 stack.24.first_ref
  0.7 0.0 copy-start.4
  0.8 0.0 copy-start.5
  0.8 0.0 copy-start.6
  0.8 0.0 copy-start.9
  0.8 0.0 copy-start.10
  0.8 3.4 %pick.1 = (f32[2,4,256,128]{3,2,1,0:T(8,128)}, f32[2,4,256,128]{3,2,1,0:T(8,128)}) custom-call(s32[8]{0:T(128)S(1)} %stack.24.first_ref, f32[24,256,128]{2,1,0:T(8,128)} %bitcast.12, f32[24,256,128]{2,1,0:T(8,128)} %bitcast.14), custom_call_target="tpu_custom_call" | custom-call | flops 1000 | bytes 1000 | tf_op jit(solution)/shard_map/pick/pallas_call | solution.py:373
  4.2 3.1 %collective-permute-start = (f32[2,4,256,128]{3,2,1,0:T(8,128)}, f32[2,4,256,128]{3,2,1,0:T(8,128)}, u32[]{:S(2)}, u32[]{:S(2)}) collective-permute-start(f32[2,4,256,128]{3,2,1,0:T(8,128)} %get-tuple-element.50), channel_id=1, source_target_pairs={{0,4},{8,12},{4,0},{12,8},{1,5},{9,13},{5,1},{13,9},{2,6},{10,14},... | collective-permute-start | bytes 3145736 | tf_op jit(solution)/shard_map/ppermute | solution.py:726
  7.3 1.6 %collective-permute-start.1 = (f32[2,4,256,128]{3,2,1,0:T(8,128)}, f32[2,4,256,128]{3,2,1,0:T(8,128)}, u32[]{:S(2)}, u32[]{:S(2)}) collective-permute-start(f32[2,4,256,128]{3,2,1,0:T(8,128)} %get-tuple-element.51), channel_id=1, source_target_pairs={{4,8},{8,4},{5,9},{9,5},{6,10},{10,6},{7,11},{11,7},{20,24},{24,20... | collective-permute-start | bytes 3145736 | tf_op jit(solution)/shard_map/ppermute | solution.py:726
  9.0 27.9 %step_one.1 = (f32[24,256,128]{2,1,0:T(8,128)S(1)}, f32[24,256,128]{2,1,0:T(8,128)S(1)}, f32[32,256,128]{2,1,0:T(8,128)S(1)}, f32[32,256,128]{2,1,0:T(8,128)S(1)...) custom-call(s32[8]{0:T(128)S(1)} %stack.24.first_ref, ...), custom_call_target="tpu_custom_call" | custom-call | flops 999999995904 | bytes 1000 | tf_op jit(solution)/shard_map/step_one/pallas_call | solution.py:321
  36.9 0.1 collective-permute-start.2
  37.0 1.9 %collective-permute-done.2.near = f32[8,2,64,128]{3,2,1,0:T(8,128)S(1)} collective-permute-done((f32[8,2,64,128]{3,2,1,0:T(8,128)S(1)}, f32[8,2,64,128]{3,2,1,0:T(8,128)S(1)}, u32[]{:S(2)}, u32[]{:S(2)}) %collective-permute-start.2) | collective-permute-done | bytes 524320 | tf_op jit(solution)/shard_map/ppermute | solution.py:731
  38.9 3.4 %correct.1 = (f32[24,256,128]{2,1,0:T(8,128)S(1)}, f32[32,256,128]{2,1,0:T(8,128)S(1)}, f32[32,256,128]{2,1,0:T(8,128)S(1)}, f32[24,256,128]{2,1,0:T(8,128)S(1)}...) custom-call(s32[8]{0:T(128)S(1)} %stack.24.first_ref, ...), custom_call_target="tpu_custom_call", output_to_operand_aliasing={{0}: (2, {}), {1}: (3, {}), {2}: (4, {}), {3}: (5, {})} | custom-call | flops 1000 | bytes 1000 | tf_op jit(solution)/shard_map/correct/pallas_call | solution.py:418
  42.3 1.6 %collective-permute-start.3 = (f32[8,64,128]{2,1,0:T(8,128)S(1)}, f32[8,64,128]{2,1,0:T(8,128)S(1)}, u32[]{:S(2)}, u32[]{:S(2)}) collective-permute-start(f32[8,64,128]{2,1,0:T(8,128)S(1)} %get-tuple-element.59), channel_id=1, source_target_pairs={{0,2},{1,3},{2,0},{3,1},{4,6},{5,7},{6,4},{7,5},{8,10},{9,11},{10,... | collective-permute-start | bytes 786440 | tf_op jit(solution)/shard_map/ppermute | solution.py:731
  43.8 3.7 %collective-permute-start.4 = (f32[2,4,256,128]{3,2,1,0:T(8,128)}, f32[2,4,256,128]{3,2,1,0:T(8,128)}, u32[]{:S(2)}, u32[]{:S(2)}) collective-permute-start(f32[2,4,256,128]{3,2,1,0:T(8,128)} %get-tuple-element.63), channel_id=1, source_target_pairs={{0,4},{8,12},{4,0},{12,8},{1,5},{9,13},{5,1},{13,9},{2,6},{10,14},... | collective-permute-start | bytes 3145736 | tf_op jit(solution)/shard_map/ppermute | solution.py:726
  47.5 1.6 %collective-permute-start.5 = (f32[2,4,256,128]{3,2,1,0:T(8,128)}, f32[2,4,256,128]{3,2,1,0:T(8,128)}, u32[]{:S(2)}, u32[]{:S(2)}) collective-permute-start(f32[2,4,256,128]{3,2,1,0:T(8,128)} %get-tuple-element.64), channel_id=1, source_target_pairs={{4,8},{8,4},{5,9},{9,5},{6,10},{10,6},{7,11},{11,7},{20,24},{24,20... | collective-permute-start | bytes 3145736 | tf_op jit(solution)/shard_map/ppermute | solution.py:726
  49.1 1.5 %collective-permute-done.3.refs_0_.refs_1_ = f32[8,64,128]{2,1,0:T(8,128)S(1)} collective-permute-done((f32[8,64,128]{2,1,0:T(8,128)S(1)}, f32[8,64,128]{2,1,0:T(8,128)S(1)}, u32[]{:S(2)}, u32[]{:S(2)}) %collective-permute-start.3) | collective-permute-done | bytes 262176 | tf_op jit(solution)/shard_map/ppermute | solution.py:731
  50.7 6.2 %step_two.1 = (f32[2,4,256,128]{3,2,1,0:T(8,128)S(1)}, f32[2,4,256,128]{3,2,1,0:T(8,128)S(1)}, f32[2,4,256,128]{3,2,1,0:T(8,128)S(1)}, f32[8,64,128]{2,1,0:T(8,1...) custom-call(s32[8]{0:T(128)S(1)} %stack.24.first_ref, ...), custom_call_target="tpu_custom_call" | custom-call | flops 999999995904 | bytes 1000 | tf_op jit(solution)/shard_map/step_two/pallas_call | solution.py:469
  56.9 0.1 collective-permute-start.9
  57.0 1.6 %collective-permute-start.10 = (f32[8,64,128]{2,1,0:T(8,128)}, f32[8,64,128]{2,1,0:T(8,128)}, u32[]{:S(2)}, u32[]{:S(2)}) collective-permute-start(f32[8,64,128]{2,1,0:T(8,128)} %get-tuple-element.72), channel_id=1, source_target_pairs={{0,2},{1,3},{2,0},{3,1},{4,6},{5,7},{6,4},{7,5},{8,10},{9,11},{10,... | collective-permute-start | bytes 786440 | tf_op jit(solution)/shard_map/ppermute | solution.py:731
  58.6 0.3 collective-permute-start.11
  58.9 12.1 %collective-permute-done.4.halo0 = f32[2,4,256,128]{3,2,1,0:T(8,128)} collective-permute-done((f32[2,4,256,128]{3,2,1,0:T(8,128)}, f32[2,4,256,128]{3,2,1,0:T(8,128)}, u32[]{:S(2)}, u32[]{:S(2)}) %collective-permute-start.4) | collective-permute-done | bytes 1048608 | tf_op jit(solution)/shard_map/ppermute | solution.py:726
  71.0 3.1 %finish.1 = (f32[8,64,128]{2,1,0:T(8,128)S(1)}, f32[8,64,128]{2,1,0:T(8,128)}, f32[8,64,128]{2,1,0:T(8,128)}, f32[8,64,128]{2,1,0:T(8,128)}) custom-call(s32[8]{0:T(128)S(1)} %stack.24.first_ref, f32[2,4,256,128]{3,2,1,0:T(8,128)S(1)} %get-tuple-element.60.edge, f32[2,4,256,128]{3,2,1,0:T(8,128)S(1)} %get-tuple-element.61.by_f, ...), custom_call_target="tpu_custom_call" | custom-call | flops 999999995904 | bytes 1000 | tf_op jit(solution)/shard_map/finish/pallas_call | solution.py:499
  74.1 0.0 collective-permute-start.6
  74.1 0.5 collective-permute-start.7
  74.6 1.3 %collective-permute-start.8 = (f32[8,64,128]{2,1,0:T(8,128)}, f32[8,64,128]{2,1,0:T(8,128)}, u32[]{:S(2)}, u32[]{:S(2)}) collective-permute-start(f32[8,64,128]{2,1,0:T(8,128)} %get-tuple-element.68), channel_id=1, source_target_pairs={{0,3},{1,2},{2,1},{3,0},{4,7},{5,6},{6,5},{7,4},{8,11},{9,10},{10,... | collective-permute-start | bytes 786440 | tf_op jit(solution)/shard_map/ppermute | solution.py:731
  76.0 3.3 %depth.2 = (f32[24,64,128]{2,1,0:T(8,128)}, f32[8,32,128]{2,1,0:T(8,128)}, f32[8,32,128]{2,1,0:T(8,128)}, f32[8,32,128]{2,1,0:T(8,128)}, f32[8,32,128]{2,1,0:T(8,128)}) custom-call(s32[8]{0:T(128)S(1)} %stack.24.first_ref, f32[8,64,128]{2,1,0:T(8,128)S(1)} %get-tuple-element.69.refs_0_, f32[8,64,128]{2,1,0:T(8,128)S(1)} %collective-permute-done.3.refs_0_.refs_1_, ...), custom_call_target="tpu_custom_call" | custom-call | flops 999999995904 | bytes 1000 | tf_op jit(solution)/shard_map/depth/pallas_call | solution.py:560
  79.3 2.2 %collective-permute-start.12 = (f32[8,32,128]{2,1,0:T(8,128)}, f32[8,32,128]{2,1,0:T(8,128)}, u32[]{:S(2)}, u32[]{:S(2)}) collective-permute-start(f32[8,32,128]{2,1,0:T(8,128)} %get-tuple-element.76), channel_id=1, source_target_pairs={{0,0},{1,4},{2,8},{3,12},{4,1},{5,5},{6,9},{7,13},{8,2},{9,6},{10,... | collective-permute-start | bytes 393224 | tf_op jit(solution)/shard_map/ppermute | solution.py:747
  81.4 3.5 %collective-permute-start.13 = (f32[8,32,128]{2,1,0:T(8,128)}, f32[8,32,128]{2,1,0:T(8,128)}, u32[]{:S(2)}, u32[]{:S(2)}) collective-permute-start(f32[8,32,128]{2,1,0:T(8,128)} %get-tuple-element.77), channel_id=1, source_target_pairs={{0,4},{1,8},{2,12},{3,0},{4,5},{5,9},{6,13},{7,1},{8,6},{9,10},{10... | collective-permute-start | bytes 393224 | tf_op jit(solution)/shard_map/ppermute | solution.py:747
  84.9 0.0 collective-permute-done.6.refs_1_
  84.9 2.5 %collective-permute-start.14 = (f32[8,32,128]{2,1,0:T(8,128)}, f32[8,32,128]{2,1,0:T(8,128)}, u32[]{:S(2)}, u32[]{:S(2)}) collective-permute-start(f32[8,32,128]{2,1,0:T(8,128)} %get-tuple-element.78), channel_id=1, source_target_pairs={{0,8},{1,12},{2,0},{3,4},{4,9},{5,13},{6,1},{7,5},{8,10},{9,14},{1... | collective-permute-start | bytes 393224 | tf_op jit(solution)/shard_map/ppermute | solution.py:747
  87.4 2.2 %collective-permute-start.15 = (f32[8,32,128]{2,1,0:T(8,128)}, f32[8,32,128]{2,1,0:T(8,128)}, u32[]{:S(2)}, u32[]{:S(2)}) collective-permute-start(f32[8,32,128]{2,1,0:T(8,128)} %get-tuple-element.79), channel_id=1, source_target_pairs={{0,12},{1,0},{2,4},{3,8},{4,13},{5,1},{6,5},{7,9},{8,14},{9,2},{10... | collective-permute-start | bytes 393224 | tf_op jit(solution)/shard_map/ppermute | solution.py:747
  89.6 2.9 %depth.3 = (f32[24,64,128]{2,1,0:T(8,128)}, f32[4,32,128]{2,1,0:T(8,128)}, f32[4,32,128]{2,1,0:T(8,128)}, f32[4,32,128]{2,1,0:T(8,128)}, f32[4,32,128]{2,1,0:T(8,128)}) custom-call(s32[8]{0:T(128)S(1)} %stack.24.first_ref, f32[8,64,128]{2,1,0:T(8,128)S(1)} %get-tuple-element.65.refs_0_, ...), custom_call_target="tpu_custom_call", output_to_operand_aliasing={{0}: (7, {})} | custom-call | flops 999999995904 | bytes 1000 | tf_op jit(solution)/shard_map/depth/pallas_call | solution.py:560
  92.5 2.1 %collective-permute-start.16 = (f32[4,32,128]{2,1,0:T(8,128)}, f32[4,32,128]{2,1,0:T(8,128)}, u32[]{:S(2)}, u32[]{:S(2)}) collective-permute-start(f32[4,32,128]{2,1,0:T(8,128)} %get-tuple-element.80), channel_id=1, source_target_pairs={{0,0},{1,4},{2,8},{3,12},{4,1},{5,5},{6,9},{7,13},{8,2},{9,6},{10,... | collective-permute-start | bytes 196616 | tf_op jit(solution)/shard_map/ppermute | solution.py:747
  94.6 5.5 %collective-permute-start.17 = (f32[4,32,128]{2,1,0:T(8,128)}, f32[4,32,128]{2,1,0:T(8,128)}, u32[]{:S(2)}, u32[]{:S(2)}) collective-permute-start(f32[4,32,128]{2,1,0:T(8,128)} %get-tuple-element.81), channel_id=1, source_target_pairs={{0,4},{1,8},{2,12},{3,0},{4,5},{5,9},{6,13},{7,1},{8,6},{9,10},{10... | collective-permute-start | bytes 196616 | tf_op jit(solution)/shard_map/ppermute | solution.py:747
  100.1 4.9 %collective-permute-start.18 = (f32[4,32,128]{2,1,0:T(8,128)}, f32[4,32,128]{2,1,0:T(8,128)}, u32[]{:S(2)}, u32[]{:S(2)}) collective-permute-start(f32[4,32,128]{2,1,0:T(8,128)} %get-tuple-element.82), channel_id=1, source_target_pairs={{0,8},{1,12},{2,0},{3,4},{4,9},{5,13},{6,1},{7,5},{8,10},{9,14},{1... | collective-permute-start | bytes 196616 | tf_op jit(solution)/shard_map/ppermute | solution.py:747
  104.9 2.1 %collective-permute-start.19 = (f32[4,32,128]{2,1,0:T(8,128)}, f32[4,32,128]{2,1,0:T(8,128)}, u32[]{:S(2)}, u32[]{:S(2)}) collective-permute-start(f32[4,32,128]{2,1,0:T(8,128)} %get-tuple-element.83), channel_id=1, source_target_pairs={{0,12},{1,0},{2,4},{3,8},{4,13},{5,1},{6,5},{7,9},{8,14},{9,2},{10... | collective-permute-start | bytes 196616 | tf_op jit(solution)/shard_map/ppermute | solution.py:747
  107.1 2.2 %gather.2.mains = f32[16,32,256]{2,1,0:T(8,128)S(1)} custom-call(s32[8]{0:T(128)S(1)} %stack.24.first_ref, f32[8,32,128]{2,1,0:T(8,128)} %collective-permute-done.12.refs_0_, f32[8,32,128]{2,1,0:T(8,128)} %collective-permute-done.13.refs_1_, f32[8,32,128]{2,1,0:T(8,128)} %collective-permute-done.14.refs_2_, f32[8,32,128]{2,1,0:T(8,128)} %collective-permute-done.15.refs_3_, ...), custom_call_target="tpu_custom_call" | custom-call | flops 999999995904 | bytes 1000 | tf_op jit(solution)/shard_map/gather/pallas_call | solution.py:621
  109.3 0.0 collective-permute-done.19.refs_3_
  109.3 0.0 copy-start.1
  109.3 1.8 %gather.3.edges = f32[8,32,256]{2,1,0:T(8,128)S(1)} custom-call(s32[8]{0:T(128)S(1)} %stack.24.first_ref, f32[4,32,128]{2,1,0:T(8,128)} %collective-permute-done.16.refs_0_, f32[4,32,128]{2,1,0:T(8,128)} %collective-permute-done.17.refs_1_, f32[4,32,128]{2,1,0:T(8,128)} %collective-permute-done.18.refs_2_, f32[4,32,128]{2,1,0:T(8,128)} %collective-permute-done.19.refs_3_, ...), custom_call_target="tpu_custom_call" | custom-call | flops 999999995904 | bytes 1000 | tf_op jit(solution)/shard_map/gather/pallas_call | solution.py:621
  111.2 1.2 scan.3
  112.4 0.1 collective-permute-start.20
  112.4 1.4 %collective-permute-start.21 = (f32[32,256]{1,0:T(8,128)S(1)}, f32[32,256]{1,0:T(8,128)S(1)}, u32[]{:S(2)}, u32[]{:S(2)}) collective-permute-start(f32[32,256]{1,0:T(8,128)S(1)} %get-tuple-element.86), channel_id=1, source_target_pairs={{0,2},{1,3},{2,0},{3,1},{4,6},{5,7},{6,4},{7,5},{8,10},{9,11},{10,... | collective-permute-start | bytes 98312 | tf_op jit(solution)/shard_map/ppermute | solution.py:731
  113.9 0.4 collective-permute-start.22
  114.3 2.1 %collective-permute-done.21.refs_1_ = f32[32,256]{1,0:T(8,128)S(1)} collective-permute-done((f32[32,256]{1,0:T(8,128)S(1)}, f32[32,256]{1,0:T(8,128)S(1)}, u32[]{:S(2)}, u32[]{:S(2)}) %collective-permute-start.21) | collective-permute-done | bytes 32800 | tf_op jit(solution)/shard_map/ppermute | solution.py:731
  116.4 0.8 collective-permute-done.22.refs_2_
  117.2 1.6 %join.1 = f32[24,32,256]{2,1,0:T(8,128)} custom-call(s32[8]{0:T(128)S(1)} %stack.24.first_ref, f32[5,96]{1,0:T(8,128)S(1)} %copy-done, f32[4,4]{1,0:T(4,128)S(1)} %copy-done.1, f32[24,32,256]{2,1,0:T(8,128)S(1)} %get-tuple-element.84.part, f32[32,256]{1,0:T(8,128)S(1)} %collective-permute-done.20.refs_0_, f32[32,256]{1,0:T(8,128)S(1)} %collective-permute-done.21.refs_1_, ...), custom_call_target="tpu_custom_call" | custom-call | flops 1000 | bytes 1000 | tf_op jit(solution)/shard_map/join/pallas_call | solution.py:708
  (36 shorter events, 0.1 us)
Async XLA Ops:
  0.7 8.2 %copy-start.2 = (f32[1,2,2048]{2,1,0:T(2,128)S(1)}, f32[1,2,2048]{2,1,0:T(2,128)}, u32[]{:S(2)}) copy-start(f32[1,2,2048]{2,1,0:T(2,128)} %rec_data.1) | copy-start | bytes 49156
  0.7 8.2 %copy-start.3 = (s32[2048]{0:T(1024)S(1)}, s32[2048]{0:T(1024)}, u32[]{:S(2)}) copy-start(s32[2048]{0:T(1024)} %rec_cell.1) | copy-start | bytes 24580
  0.7 8.2 %copy-start.4 = (f32[1,2,64]{2,1,0:T(2,128)S(1)}, f32[1,2,64]{2,1,0:T(2,128)}, u32[]{:S(2)}) copy-start(f32[1,2,64]{2,1,0:T(2,128)} %wavelet.1) | copy-start | bytes 1540
  0.8 8.2 %copy-start.5 = (s32[1,64]{1,0:T(1,128)S(1)}, s32[1,64]{1,0:T(1,128)}, u32[]{:S(2)}) copy-start(s32[1,64]{1,0:T(1,128)} %src_cell.1) | copy-start | bytes 772
  0.8 8.2 %copy-start.6 = (s32[1,64]{1,0:T(1,128)S(1)}, s32[1,64]{1,0:T(1,128)}, u32[]{:S(2)}) copy-start(s32[1,64]{1,0:T(1,128)} %src_sign.1) | copy-start | bytes 772
  0.8 8.2 %copy-start.9 = (bf16[256,256]{1,0:T(8,128)(2,1)S(1)}, bf16[256,256]{1,0:T(8,128)(2,1)}, u32[]{:S(2)}) copy-start(bf16[256,256]{1,0:T(8,128)(2,1)} %constant.55.clone.band_y) | copy-start | bytes 393220
  0.8 8.2 %copy-start.10 = (bf16[256,128]{1,0:T(8,128)(2,1)S(1)}, bf16[256,128]{1,0:T(8,128)(2,1)}, u32[]{:S(2)}) copy-start(bf16[256,128]{1,0:T(8,128)(2,1)} %constant.56.clone.band_z) | copy-start | bytes 196612
  4.2 34.7 %collective-permute-start = (f32[2,4,256,128]{3,2,1,0:T(8,128)}, f32[2,4,256,128]{3,2,1,0:T(8,128)}, u32[]{:S(2)}, u32[]{:S(2)}) collective-permute-start(f32[2,4,256,128]{3,2,1,0:T(8,128)} %get-tuple-element.50), channel_id=1, source_target_pairs={{0,4},{8,12},{4,0},{12,8},{1,5},{9,13},{5,1},{13,9},{2,6},{10,14},... | collective-permute-start | bytes 3145736 | tf_op jit(solution)/shard_map/ppermute | solution.py:726
  7.3 31.6 %collective-permute-start.1 = (f32[2,4,256,128]{3,2,1,0:T(8,128)}, f32[2,4,256,128]{3,2,1,0:T(8,128)}, u32[]{:S(2)}, u32[]{:S(2)}) collective-permute-start(f32[2,4,256,128]{3,2,1,0:T(8,128)} %get-tuple-element.51), channel_id=1, source_target_pairs={{4,8},{8,4},{5,9},{9,5},{6,10},{10,6},{7,11},{11,7},{20,24},{24,20... | collective-permute-start | bytes 3145736 | tf_op jit(solution)/shard_map/ppermute | solution.py:726
  36.9 2.0 %collective-permute-start.2 = (f32[8,2,64,128]{3,2,1,0:T(8,128)S(1)}, f32[8,2,64,128]{3,2,1,0:T(8,128)S(1)}, u32[]{:S(2)}, u32[]{:S(2)}) collective-permute-start(f32[8,2,64,128]{3,2,1,0:T(8,128)S(1)} %get-tuple-element.53), channel_id=1, source_target_pairs={{0,1},{1,0},{2,3},{3,2},{4,5},{5,4},{6,7},{7,6},{8,9},{9,8},{10,11... | collective-permute-start | bytes 1572872 | tf_op jit(solution)/shard_map/ppermute | solution.py:731
  42.3 8.4 %collective-permute-start.3 = (f32[8,64,128]{2,1,0:T(8,128)S(1)}, f32[8,64,128]{2,1,0:T(8,128)S(1)}, u32[]{:S(2)}, u32[]{:S(2)}) collective-permute-start(f32[8,64,128]{2,1,0:T(8,128)S(1)} %get-tuple-element.59), channel_id=1, source_target_pairs={{0,2},{1,3},{2,0},{3,1},{4,6},{5,7},{6,4},{7,5},{8,10},{9,11},{10,... | collective-permute-start | bytes 786440 | tf_op jit(solution)/shard_map/ppermute | solution.py:731
  43.8 27.2 %collective-permute-start.4 = (f32[2,4,256,128]{3,2,1,0:T(8,128)}, f32[2,4,256,128]{3,2,1,0:T(8,128)}, u32[]{:S(2)}, u32[]{:S(2)}) collective-permute-start(f32[2,4,256,128]{3,2,1,0:T(8,128)} %get-tuple-element.63), channel_id=1, source_target_pairs={{0,4},{8,12},{4,0},{12,8},{1,5},{9,13},{5,1},{13,9},{2,6},{10,14},... | collective-permute-start | bytes 3145736 | tf_op jit(solution)/shard_map/ppermute | solution.py:726
  47.5 23.5 %collective-permute-start.5 = (f32[2,4,256,128]{3,2,1,0:T(8,128)}, f32[2,4,256,128]{3,2,1,0:T(8,128)}, u32[]{:S(2)}, u32[]{:S(2)}) collective-permute-start(f32[2,4,256,128]{3,2,1,0:T(8,128)} %get-tuple-element.64), channel_id=1, source_target_pairs={{4,8},{8,4},{5,9},{9,5},{6,10},{10,6},{7,11},{11,7},{20,24},{24,20... | collective-permute-start | bytes 3145736 | tf_op jit(solution)/shard_map/ppermute | solution.py:726
  56.9 17.7 %collective-permute-start.9 = (f32[8,64,128]{2,1,0:T(8,128)}, f32[8,64,128]{2,1,0:T(8,128)}, u32[]{:S(2)}, u32[]{:S(2)}) collective-permute-start(f32[8,64,128]{2,1,0:T(8,128)} %get-tuple-element.71), channel_id=1, source_target_pairs={{0,1},{1,0},{2,3},{3,2},{4,5},{5,4},{6,7},{7,6},{8,9},{9,8},{10,11... | collective-permute-start | bytes 786440 | tf_op jit(solution)/shard_map/ppermute | solution.py:731
  57.0 19.0 %collective-permute-start.10 = (f32[8,64,128]{2,1,0:T(8,128)}, f32[8,64,128]{2,1,0:T(8,128)}, u32[]{:S(2)}, u32[]{:S(2)}) collective-permute-start(f32[8,64,128]{2,1,0:T(8,128)} %get-tuple-element.72), channel_id=1, source_target_pairs={{0,2},{1,3},{2,0},{3,1},{4,6},{5,7},{6,4},{7,5},{8,10},{9,11},{10,... | collective-permute-start | bytes 786440 | tf_op jit(solution)/shard_map/ppermute | solution.py:731
  58.6 17.4 %collective-permute-start.11 = (f32[8,64,128]{2,1,0:T(8,128)}, f32[8,64,128]{2,1,0:T(8,128)}, u32[]{:S(2)}, u32[]{:S(2)}) collective-permute-start(f32[8,64,128]{2,1,0:T(8,128)} %get-tuple-element.73), channel_id=1, source_target_pairs={{0,3},{1,2},{2,1},{3,0},{4,7},{5,6},{6,5},{7,4},{8,11},{9,10},{10,... | collective-permute-start | bytes 786440 | tf_op jit(solution)/shard_map/ppermute | solution.py:731
  71.0 5.0 %copy-start.11 = (bf16[128,128]{1,0:T(8,128)(2,1)S(1)}, bf16[128,128]{1,0:T(8,128)(2,1)}, u32[]{:S(2)}) copy-start(bf16[128,128]{1,0:T(8,128)(2,1)} %constant.58.clone.refs_7_.refs_5_) | copy-start | bytes 98308
  71.0 5.0 %copy-start.12 = (bf16[128,128]{1,0:T(8,128)(2,1)S(1)}, bf16[128,128]{1,0:T(8,128)(2,1)}, u32[]{:S(2)}) copy-start(bf16[128,128]{1,0:T(8,128)(2,1)} %constant.57.clone.refs_6_.refs_4_) | copy-start | bytes 98308
  74.1 10.8 %collective-permute-start.6 = (f32[8,64,128]{2,1,0:T(8,128)}, f32[8,64,128]{2,1,0:T(8,128)}, u32[]{:S(2)}, u32[]{:S(2)}) collective-permute-start(f32[8,64,128]{2,1,0:T(8,128)} %get-tuple-element.66), channel_id=1, source_target_pairs={{0,1},{1,0},{2,3},{3,2},{4,5},{5,4},{6,7},{7,6},{8,9},{9,8},{10,11... | collective-permute-start | bytes 786440 | tf_op jit(solution)/shard_map/ppermute | solution.py:731
  74.1 13.3 %collective-permute-start.7 = (f32[8,64,128]{2,1,0:T(8,128)}, f32[8,64,128]{2,1,0:T(8,128)}, u32[]{:S(2)}, u32[]{:S(2)}) collective-permute-start(f32[8,64,128]{2,1,0:T(8,128)} %get-tuple-element.67), channel_id=1, source_target_pairs={{0,2},{1,3},{2,0},{3,1},{4,6},{5,7},{6,4},{7,5},{8,10},{9,11},{10,... | collective-permute-start | bytes 786440 | tf_op jit(solution)/shard_map/ppermute | solution.py:731
  74.6 15.0 %collective-permute-start.8 = (f32[8,64,128]{2,1,0:T(8,128)}, f32[8,64,128]{2,1,0:T(8,128)}, u32[]{:S(2)}, u32[]{:S(2)}) collective-permute-start(f32[8,64,128]{2,1,0:T(8,128)} %get-tuple-element.68), channel_id=1, source_target_pairs={{0,3},{1,2},{2,1},{3,0},{4,7},{5,6},{6,5},{7,4},{8,11},{9,10},{10,... | collective-permute-start | bytes 786440 | tf_op jit(solution)/shard_map/ppermute | solution.py:731
  79.3 15.3 %collective-permute-start.12 = (f32[8,32,128]{2,1,0:T(8,128)}, f32[8,32,128]{2,1,0:T(8,128)}, u32[]{:S(2)}, u32[]{:S(2)}) collective-permute-start(f32[8,32,128]{2,1,0:T(8,128)} %get-tuple-element.76), channel_id=1, source_target_pairs={{0,0},{1,4},{2,8},{3,12},{4,1},{5,5},{6,9},{7,13},{8,2},{9,6},{10,... | collective-permute-start | bytes 393224 | tf_op jit(solution)/shard_map/ppermute | solution.py:747
  81.4 18.7 %collective-permute-start.13 = (f32[8,32,128]{2,1,0:T(8,128)}, f32[8,32,128]{2,1,0:T(8,128)}, u32[]{:S(2)}, u32[]{:S(2)}) collective-permute-start(f32[8,32,128]{2,1,0:T(8,128)} %get-tuple-element.77), channel_id=1, source_target_pairs={{0,4},{1,8},{2,12},{3,0},{4,5},{5,9},{6,13},{7,1},{8,6},{9,10},{10... | collective-permute-start | bytes 393224 | tf_op jit(solution)/shard_map/ppermute | solution.py:747
  84.9 20.1 %collective-permute-start.14 = (f32[8,32,128]{2,1,0:T(8,128)}, f32[8,32,128]{2,1,0:T(8,128)}, u32[]{:S(2)}, u32[]{:S(2)}) collective-permute-start(f32[8,32,128]{2,1,0:T(8,128)} %get-tuple-element.78), channel_id=1, source_target_pairs={{0,8},{1,12},{2,0},{3,4},{4,9},{5,13},{6,1},{7,5},{8,10},{9,14},{1... | collective-permute-start | bytes 393224 | tf_op jit(solution)/shard_map/ppermute | solution.py:747
  87.4 19.7 %collective-permute-start.15 = (f32[8,32,128]{2,1,0:T(8,128)}, f32[8,32,128]{2,1,0:T(8,128)}, u32[]{:S(2)}, u32[]{:S(2)}) collective-permute-start(f32[8,32,128]{2,1,0:T(8,128)} %get-tuple-element.79), channel_id=1, source_target_pairs={{0,12},{1,0},{2,4},{3,8},{4,13},{5,1},{6,5},{7,9},{8,14},{9,2},{10... | collective-permute-start | bytes 393224 | tf_op jit(solution)/shard_map/ppermute | solution.py:747
  89.6 17.5 %copy-start.7 = (bf16[256,256]{1,0:T(8,128)(2,1)S(1)}, bf16[256,256]{1,0:T(8,128)(2,1)}, u32[]{:S(2)}) copy-start(bf16[256,256]{1,0:T(8,128)(2,1)} %constant.60.clone.refs_5_) | copy-start | bytes 393220
  89.6 17.5 %copy-start.8 = (bf16[256,256]{1,0:T(8,128)(2,1)S(1)}, bf16[256,256]{1,0:T(8,128)(2,1)}, u32[]{:S(2)}) copy-start(bf16[256,256]{1,0:T(8,128)(2,1)} %constant.59.clone.refs_4_) | copy-start | bytes 393220
  92.5 16.8 %collective-permute-start.16 = (f32[4,32,128]{2,1,0:T(8,128)}, f32[4,32,128]{2,1,0:T(8,128)}, u32[]{:S(2)}, u32[]{:S(2)}) collective-permute-start(f32[4,32,128]{2,1,0:T(8,128)} %get-tuple-element.80), channel_id=1, source_target_pairs={{0,0},{1,4},{2,8},{3,12},{4,1},{5,5},{6,9},{7,13},{8,2},{9,6},{10,... | collective-permute-start | bytes 196616 | tf_op jit(solution)/shard_map/ppermute | solution.py:747
  94.6 14.7 %collective-permute-start.17 = (f32[4,32,128]{2,1,0:T(8,128)}, f32[4,32,128]{2,1,0:T(8,128)}, u32[]{:S(2)}, u32[]{:S(2)}) collective-permute-start(f32[4,32,128]{2,1,0:T(8,128)} %get-tuple-element.81), channel_id=1, source_target_pairs={{0,4},{1,8},{2,12},{3,0},{4,5},{5,9},{6,13},{7,1},{8,6},{9,10},{10... | collective-permute-start | bytes 196616 | tf_op jit(solution)/shard_map/ppermute | solution.py:747
  100.1 9.2 %collective-permute-start.18 = (f32[4,32,128]{2,1,0:T(8,128)}, f32[4,32,128]{2,1,0:T(8,128)}, u32[]{:S(2)}, u32[]{:S(2)}) collective-permute-start(f32[4,32,128]{2,1,0:T(8,128)} %get-tuple-element.82), channel_id=1, source_target_pairs={{0,8},{1,12},{2,0},{3,4},{4,9},{5,13},{6,1},{7,5},{8,10},{9,14},{1... | collective-permute-start | bytes 196616 | tf_op jit(solution)/shard_map/ppermute | solution.py:747
  104.9 4.4 %collective-permute-start.19 = (f32[4,32,128]{2,1,0:T(8,128)}, f32[4,32,128]{2,1,0:T(8,128)}, u32[]{:S(2)}, u32[]{:S(2)}) collective-permute-start(f32[4,32,128]{2,1,0:T(8,128)} %get-tuple-element.83), channel_id=1, source_target_pairs={{0,12},{1,0},{2,4},{3,8},{4,13},{5,1},{6,5},{7,9},{8,14},{9,2},{10... | collective-permute-start | bytes 196616 | tf_op jit(solution)/shard_map/ppermute | solution.py:747
  109.3 1.9 %copy-start = (f32[5,96]{1,0:T(8,128)S(1)}, f32[5,96]{1,0:T(8,128)}, u32[]{:S(2)}) copy-start(f32[5,96]{1,0:T(8,128)} %constant.61.clone.scan) | copy-start | bytes 5764
  109.3 7.9 %copy-start.1 = (f32[4,4]{1,0:T(4,128)S(1)}, f32[4,4]{1,0:T(4,128)}, u32[]{:S(2)}) copy-start(f32[4,4]{1,0:T(4,128)} %constant.62.clone.carry) | copy-start | bytes 196
  112.4 1.9 %collective-permute-start.20 = (f32[32,256]{1,0:T(8,128)S(1)}, f32[32,256]{1,0:T(8,128)S(1)}, u32[]{:S(2)}, u32[]{:S(2)}) collective-permute-start(f32[32,256]{1,0:T(8,128)S(1)} %get-tuple-element.85), channel_id=1, source_target_pairs={{0,1},{1,0},{2,3},{3,2},{4,5},{5,4},{6,7},{7,6},{8,9},{9,8},{10,11... | collective-permute-start | bytes 98312 | tf_op jit(solution)/shard_map/ppermute | solution.py:731
  112.4 4.0 %collective-permute-start.21 = (f32[32,256]{1,0:T(8,128)S(1)}, f32[32,256]{1,0:T(8,128)S(1)}, u32[]{:S(2)}, u32[]{:S(2)}) collective-permute-start(f32[32,256]{1,0:T(8,128)S(1)} %get-tuple-element.86), channel_id=1, source_target_pairs={{0,2},{1,3},{2,0},{3,1},{4,6},{5,7},{6,4},{7,5},{8,10},{9,11},{10,... | collective-permute-start | bytes 98312 | tf_op jit(solution)/shard_map/ppermute | solution.py:731
  113.9 3.3 %collective-permute-start.22 = (f32[32,256]{1,0:T(8,128)S(1)}, f32[32,256]{1,0:T(8,128)S(1)}, u32[]{:S(2)}, u32[]{:S(2)}) collective-permute-start(f32[32,256]{1,0:T(8,128)S(1)} %get-tuple-element.87), channel_id=1, source_target_pairs={{0,3},{1,2},{2,1},{3,0},{4,7},{5,6},{6,5},{7,4},{8,11},{9,10},{10,... | collective-permute-start | bytes 98312 | tf_op jit(solution)/shard_map/ppermute | solution.py:731

commit v3 on v2

v3 whole, which is shorter than its diff:
```python
import functools
import math

import jax
import jax.numpy as jnp
import ml_dtypes
import numpy as np
from jax import lax
from jax.experimental import pallas as pl
from jax.experimental.pallas import tpu as pltpu
from jax.sharding import PartitionSpec as P

SMOOTH_X = 32
SMOOTH_YZ = 4

COEFS = (8.0 / 5.0, -1.0 / 5.0, 8.0 / 315.0, -1.0 / 560.0)
CENTER = -205.0 / 72.0
REACH = len(COEFS)
SCALE = 5040.0
WHOLE = tuple(float(round(SCALE * a)) for a in COEFS)

LANES = 128
BF16 = jnp.bfloat16
F32 = jnp.float32
ANY = pl.BlockSpec(memory_space=pl.ANY)
VMEM = pl.BlockSpec(memory_space=pltpu.VMEM)
SMEM = pl.BlockSpec(memory_space=pltpu.SMEM)


def band(length):
    table = np.zeros((length, length), np.float32)
    for k, weight in enumerate(WHOLE, 1):
        near = np.arange(length - k)
        table[near, near + k] = weight
        table[near + k, near] = weight
    return table


def response(length, strength):
    counter = np.arange(1, length + 1, dtype=np.float64)
    half_sine = np.sin(np.pi * counter / (2 * (length + 1)))
    return 1.0 / (1.0 + strength * 4.0 * half_sine * half_sine)


def filter_matrix(length, strength):
    counter = np.arange(1, length + 1, dtype=np.float64)
    table = np.sin(np.pi * counter[:, None] * counter[None, :] / (length + 1))
    return 2.0 / (length + 1) * (table * response(length, strength)[None, :]) @ table


def scan_tables(length, strength, block):
    rate = math.acosh(1.0 + 0.5 / strength)
    index = np.arange(1, length + 1, dtype=np.float64)
    rise = np.sinh(rate * index)
    fall = np.sinh(rate * (length + 1 - index))
    whole = strength * math.sinh(rate) * math.sinh(rate * (length + 1))
    diag = rise * fall / whole
    left = np.concatenate([[0.0], rise[:-1] / rise[1:]])
    right = np.concatenate([fall[1:] / fall[:-1], [0.0]])
    first = (np.arange(length) // block) * block
    last = first + block - 1
    from_left = np.where(first > 0, rise[np.maximum(first - 1, 0)], 0.0) / rise
    from_right = np.where(last + 1 < length, fall[np.minimum(last + 1, length - 1)], 0.0) / fall
    rows = np.stack([diag, left, right, diag * from_left, diag * from_right])
    blocks = length // block
    carry = np.zeros((blocks, blocks))
    for here in range(blocks):
        for there in range(blocks):
            if there < here:
                carry[here, there] = rise[there * block + block - 1] / rise[here * block - 1]
            elif there > here:
                carry[here, there] = fall[there * block] / fall[here * block + block]
    return rows.astype(np.float32), carry.astype(np.float32)


def split_table(table):
    high = table.astype(np.float32).astype(ml_dtypes.bfloat16)
    low = (table - high.astype(np.float64)).astype(np.float32).astype(ml_dtypes.bfloat16)
    return jnp.asarray(high), jnp.asarray(low)


def split(value):
    high = value.astype(BF16)
    low = (value - high.astype(F32)).astype(BF16)
    return high, low


def dot(a, b):
    return jnp.dot(a, b, preferred_element_type=F32)


def dot_t(a, b):
    return lax.dot_general(a, b, (((1,), (1,)), ((), ())), preferred_element_type=F32)


def laplace_plane(field, p, band_y, band_z):
    here = field[p]
    width = here.shape[1]
    both = jnp.concatenate(split(here), axis=1)
    along_y = dot(band_y[...], both)
    along_z = dot(both, band_z[...])
    total = (3.0 * SCALE * CENTER) * here
    for k, weight in enumerate(WHOLE, 1):
        total += weight * (field[p + k] + field[p - k])
    return total + (along_y[:, :width] + along_y[:, width:]) + along_z


def divmod_fixed(value, size):
    if size & (size - 1) == 0:
        return lax.shift_right_logical(value, size.bit_length() - 1), value & (size - 1)
    return lax.div(value, size), lax.rem(value, size)


class Copies:
    def __init__(self, sems):
        self.sems, self.used = sems, 0

    def start(self, source, target):
        copy = pltpu.make_async_copy(source, target, self.sems.at[self.used])
        self.used += 1
        copy.start()
        return copy


def wait_all(copies):
    for copy in copies:
        copy.wait()


def chunk_bounds(rows):
    step = max(2 * REACH, -(-rows // 3))
    return [(low, min(low + step, rows)) for low in range(0, rows, step)]


def put_blocks(copies, buf, planes, shot, outs):
    return [copies.start(buf.at[planes, shot ^ j], out) for j, out in enumerate(outs)]


def step_one_kernel(
    src_cell, src_sign, wavelet, rec_tile, data_tile,
    courant, f_old, f_now, a_late, a_now, band_y, band_z,
    c_buf, acc_buf, f_next, a_mid, a_base, s_second,
    *refs,
):
    terms_out = refs[:-15]
    (
        f_pad, a_pad, s_first, r_first, r_second, gt_buf,
        place_buf, value_buf, count_buf, places, values, counts, list_sems, term_sems, sems,
    ) = refs[-15:]
    rows, ny, nz = courant.shape
    copies = Copies(sems)
    bounds = chunk_bounds(rows)

    def chunks(source, target, offset=0):
        return [
            copies.start(source.at[pl.ds(low, high - low)], target.at[pl.ds(low + offset, high - low)])
            for low, high in bounds
        ]

    loads = [chunks(f_now, f_pad, REACH), chunks(courant, c_buf), chunks(f_old, f_next, REACH)]
    late_loads = [chunks(a_now, a_pad, REACH), chunks(a_late, a_mid, REACH)]
    edge = jnp.zeros((REACH, ny, nz), F32)
    for pad in (f_pad, a_pad, f_next, a_mid):
        pad[:REACH] = edge
        pad[REACH + rows :] = edge

    group = ny // 8

    def clear(p, _):
        blank = jnp.zeros((group, 8, nz), F32)
        for ref in (s_first, r_first, s_second, r_second):
            ref[pl.ds(p * group, group)] = blank
        return 0

    lax.fori_loop(0, rows, clear, 0)

    size = rows * ny * nz
    start = lax.axis_index("mp") * size
    flat = lax.broadcasted_iota(jnp.int32, (8, nz), 0) * nz + lax.broadcasted_iota(jnp.int32, (8, nz), 1)

    def put(refs, local, values):
        tile, within = divmod_fixed(local, 8 * nz)
        spot = flat == within
        for ref, value in zip(refs, values, strict=True):
            ref[tile] = ref[tile] + jnp.where(spot, value, 0.0)

    nsrc = src_cell.shape[1]

    def one_source(i, _):
        local = src_cell[0, i] - start
        mine = (local >= 0) & (local < size)
        local = jnp.where(mine, local, 0)
        sign = jnp.where(mine, (2 * src_sign[0, i] - 1).astype(F32), 0.0)
        put((s_first, s_second), local, (sign * wavelet[0, 0, i], sign * wavelet[0, 1, i]))
        return 0

    lax.fori_loop(0, nsrc, one_source, 0, unroll=8 if nsrc % 8 == 0 else 1)


    tiles = rec_tile.shape[0]
    local = rec_tile[...] - start
    inside = (local >= 0) & (local < size)
    marks = jnp.where(inside, 1.0, 0.0).astype(BF16)
    row, col = (lax.broadcasted_iota(jnp.int32, (LANES, LANES), d) for d in (0, 1))
    before = jnp.where(inside, dot(marks, jnp.where(row < col, 1.0, 0.0).astype(BF16)).astype(jnp.int32), -1)
    thirds = []
    for value in (jnp.where(inside, local, 0).astype(F32), data_tile[0], data_tile[1]):
        for _ in range(3):
            part = value.astype(BF16)
            value = value - part.astype(F32)
            thirds.append(part)
    for t in range(tiles):
        moves = jnp.where(row == before[t : t + 1], 1.0, 0.0).astype(BF16)
        stacked = jnp.concatenate([part[t : t + 1] for part in thirds] + [thirds[0][:7]], axis=0)
        moved = dot_t(stacked, moves)
        place_buf[t : t + 1] = (moved[0:1] + moved[1:2] + moved[2:3]).astype(jnp.int32)
        value_buf[0, t : t + 1] = moved[3:4] + moved[4:5] + moved[5:6]
        value_buf[1, t : t + 1] = moved[6:7] + moved[7:8] + moved[8:9]
    count_buf[...] = dot(marks, jnp.ones((LANES, LANES), BF16)).astype(jnp.int32)
    fetches = [
        pltpu.make_async_copy(source, target, list_sems.at[i])
        for i, (source, target) in enumerate(((place_buf, places), (value_buf, values), (count_buf, counts)))
    ]
    for fetch in fetches:
        fetch.start()
    wait_all(fetches)

    def receivers(t, _):
        def some(g, _):
            items = []
            for e in range(8):
                i = g * 8 + e
                items.append((places[t, i], values[0, t, i], values[1, t, i]))
            for place, first, second in items:
                put((r_first, r_second), place, (first, second))
            return 0

        return lax.fori_loop(0, lax.div(counts[t, 0] + 7, 8), some, 0)

    lax.fori_loop(0, tiles, receivers, 0)

    def forward(p, _):
        courant_here = c_buf[p] * (1.0 / SCALE)
        c_buf[p] = courant_here
        spike = s_first[pl.ds(p * group, group)].reshape(ny, nz)
        accel = courant_here * laplace_plane(f_pad, p + REACH, band_y, band_z) + spike
        acc_buf[p] = accel
        f_next[p + REACH] = (2.0 * f_pad[p + REACH] - f_next[p + REACH]) + accel
        return 0

    for group_loads in loads:
        wait_all(group_loads)
    lax.fori_loop(0, rows, forward, 0, unroll=2)

    def adjoint(p, _):
        spike = r_first[pl.ds(p * group, group)].reshape(ny, nz)
        change = c_buf[p] * laplace_plane(a_pad, p + REACH, band_y, band_z) + spike
        mid = (2.0 * a_pad[p + REACH] - a_mid[p + REACH]) + change
        a_mid[p + REACH] = mid
        later = r_second[pl.ds(p * group, group)].reshape(ny, nz)
        a_base[p] = (2.0 * mid - a_pad[p + REACH]) + later
        return 0

    for group_loads in late_loads:
        wait_all(group_loads)
    lax.fori_loop(0, rows, adjoint, 0, unroll=2)

    blocks = gt_buf.shape[1]

    def inner(i, _):
        p = i + 2 * REACH
        c = c_buf[p]
        here = pl.ds(p * group, group)
        accel = c * laplace_plane(f_next, p + REACH, band_y, band_z) + s_second[here].reshape(ny, nz)
        first = a_base[p] + c * laplace_plane(a_mid, p + REACH, band_y, band_z)
        gt_buf[i] = (first * acc_buf[p] + a_mid[p + REACH] * accel).reshape(blocks, ny // blocks, nz)
        return 0

    lax.fori_loop(0, rows - 4 * REACH, inner, 0)
    wait_all(put_blocks(Copies(term_sems), gt_buf, slice(None), lax.axis_index("shot"), terms_out))


def cheap(megabytes):
    return pltpu.CompilerParams(vmem_limit_bytes=megabytes * 2**20)


COST = pl.CostEstimate(flops=1000, bytes_accessed=1000, transcendentals=0)
LONG = pl.CostEstimate(flops=10**12, bytes_accessed=1000, transcendentals=0)


def held(*shape):
    return pltpu.VMEM(shape, F32)


def in_hbm(arrays):
    return [pltpu.with_memory_space_constraint(array, pltpu.HBM) for array in arrays]


def keep_held(arrays):
    return [pltpu.with_memory_space_constraint(array, pltpu.VMEM) for array in arrays]


def step_one(src_cell, src_sign, wavelet, rec_cell, rec_data, courant, f_old, f_now, a_late, a_now, bands, shots):
    rows, ny, nz = courant.shape
    term = held(rows - 4 * REACH, ny // shots, nz)
    whole, padded, sparse = (rows, ny, nz), (rows + 2 * REACH, ny, nz), (rows * ny // 8, 8, nz)
    tiles = rec_cell.shape[0] // LANES
    return pl.pallas_call(
        step_one_kernel,
        out_shape=tuple(held(*shape) for shape in (whole, whole, padded, padded, whole, sparse)) + (term,) * shots,
        in_specs=[SMEM] * 3 + [VMEM] * 2 + [ANY] * 5 + [VMEM] * 2,
        out_specs=(VMEM,) * (6 + shots),
        scratch_shapes=[
            held(*padded), held(*padded), held(*sparse), held(*sparse), held(*sparse),
            held(rows - 4 * REACH, shots, ny // shots, nz),
            pltpu.VMEM((tiles, LANES), jnp.int32),
            pltpu.VMEM((2, tiles, LANES), F32),
            pltpu.VMEM((tiles, LANES), jnp.int32),
            pltpu.SMEM((tiles, LANES), jnp.int32),
            pltpu.SMEM((2, tiles, LANES), F32),
            pltpu.SMEM((tiles, LANES), jnp.int32),
            pltpu.SemaphoreType.DMA((3,)),
            pltpu.SemaphoreType.DMA((shots,)),
            pltpu.SemaphoreType.DMA((5 * len(chunk_bounds(rows)),)),
        ],
        compiler_params=cheap(24),
        cost_estimate=LONG,
        name="step_one",
    )(
        src_cell, src_sign, wavelet, rec_cell.reshape(-1, LANES), rec_data.reshape(2, -1, LANES),
        *in_hbm((courant, f_old, f_now, a_late, a_now)), *bands,
    )


def sides(rows):
    even = lax.rem(lax.axis_index("mp"), 2) == 0
    high = rows - REACH
    return (jnp.where(even, high, 0), even), (jnp.where(even, 0, high), jnp.logical_not(even))


STRIP = 32


def halo_sums(halo, upper):
    planes = [halo(jnp.where(upper, h, REACH - 1 - h)) for h in range(REACH)]
    return [sum(WHOLE[h + REACH - q - 1] * planes[h] for h in range(q + 1)) for q in range(REACH)]


def strips(count, body):
    def step(i, _):
        body(pl.ds(pl.multiple_of(i * STRIP, STRIP), STRIP))
        return 0

    lax.fori_loop(0, count // STRIP, step, 0)


def pick_kernel(f_now, a_now, *refs):
    outs, sems = refs[:2], refs[2]
    copies = Copies(sems)
    wait_all([
        copies.start(field.at[pl.ds(base, REACH)], outs[s].at[i])
        for s, (base, _) in enumerate(sides(f_now.shape[0]))
        for i, field in enumerate((f_now, a_now))
    ])


def pick(f_now, a_now):
    _, ny, nz = f_now.shape
    both = held(2, REACH, ny, nz)
    return pl.pallas_call(
        pick_kernel,
        out_shape=(both, both),
        in_specs=[ANY] * 2,
        out_specs=(VMEM,) * 2,
        scratch_shapes=[pltpu.SemaphoreType.DMA((4,))],
        compiler_params=cheap(8),
        cost_estimate=COST,
        name="pick",
    )(*in_hbm((f_now, a_now)))


def correct_kernel(
    c_buf, acc_in, next_in, mid_in, base_in, halo0, halo1, acc_buf, f_next, a_mid, a_base, edge0, edge1
):
    edges = (edge0, edge1)
    rows, ny, _ = c_buf.shape

    def strip(part):
        for s, (base, upper) in enumerate(sides(rows)):
            halo = (halo0, halo1)[s]
            forward = halo_sums(lambda h, halo=halo: halo[0, h, part], upper)
            adjoint = halo_sums(lambda h, halo=halo: halo[1, h, part], upper)
            for q in range(REACH):
                place = jnp.where(upper, q, REACH - 1 - q)
                here = base + place
                c = c_buf[here, part]
                change = c * forward[q]
                acc_buf[here, part] = acc_in[here, part] + change
                value = next_in[here + REACH, part] + change
                f_next[here + REACH, part] = value
                edges[s][0, place, part] = value
                change = c * adjoint[q]
                value = mid_in[here + REACH, part] + change
                a_mid[here + REACH, part] = value
                edges[s][1, place, part] = value
                a_base[here, part] = base_in[here, part] + 2.0 * change

    strips(ny, strip)


def correct(c, accel, nxt, mid, a_base, halos):
    rows, ny, nz = c.shape
    both = held(2, REACH, ny, nz)
    return pl.pallas_call(
        correct_kernel,
        out_shape=tuple(held(*array.shape) for array in (accel, nxt, mid, a_base)) + (both, both),
        in_specs=[VMEM] * 7,
        out_specs=(VMEM,) * 6,
        input_output_aliases={1: 0, 2: 1, 3: 2, 4: 3},
        compiler_params=cheap(8),
        cost_estimate=COST,
        name="correct",
    )(*keep_held((c, accel, nxt, mid, a_base)), *halos)


def step_two_kernel(waits, c_buf, acc_buf, f_next, a_mid, a_base, s_buf, band_y, band_z, *refs):
    edge_out, by_f, by_a, *terms_out, gt_buf, sems = refs[waits:]
    rows, ny, nz = c_buf.shape
    copies = Copies(sems)
    group = ny // 8
    blocks = gt_buf.shape[1]

    def plane(p, _):
        c = c_buf[p]
        here = pl.ds(p * group, group)
        mid = a_mid[p + REACH]
        accel = c * laplace_plane(f_next, p + REACH, band_y, band_z) + s_buf[here].reshape(ny, nz)
        first = a_base[p] + c * laplace_plane(a_mid, p + REACH, band_y, band_z)
        gt_buf[p] = (first * acc_buf[p] + mid * accel).reshape(blocks, ny // blocks, nz)
        return 0

    def inner(i, _):
        return plane(jnp.where(i < REACH, i + REACH, i + rows - 3 * REACH), 0)

    lax.fori_loop(0, 2 * REACH, inner, 0)
    stores = []
    for i, low in enumerate((REACH, rows - 2 * REACH)):
        outs = [out.at[pl.ds(i * REACH, REACH)] for out in terms_out]
        stores += put_blocks(copies, gt_buf, pl.ds(low, REACH), lax.axis_index("shot"), outs)

    bases = [base for base, _ in sides(rows)]

    def outer(i, _):
        s, q = lax.div(i, REACH), lax.rem(i, REACH)
        p = jnp.where(s == 0, bases[0], bases[1]) + q
        plane(p, 0)
        c = c_buf[p]
        by_f[s, q] = c * a_mid[p + REACH]
        by_a[s, q] = c * acc_buf[p]
        edge_out[s, q] = gt_buf[p].reshape(ny, nz)
        return 0

    lax.fori_loop(0, 2 * REACH, outer, 0)
    wait_all(stores)


def step_two(arrays, bands, after, shots):
    rows, ny, nz = arrays[0].shape
    edge = held(2, REACH, ny, nz)
    term = held(2 * REACH, ny // shots, nz)
    return pl.pallas_call(
        functools.partial(step_two_kernel, len(after)),
        out_shape=(edge, edge, edge) + (term,) * shots,
        in_specs=[VMEM] * (8 + len(after)),
        out_specs=(VMEM,) * (3 + shots),
        scratch_shapes=[held(rows, shots, ny // shots, nz), pltpu.SemaphoreType.DMA((2 * shots,))],
        compiler_params=cheap(12),
        cost_estimate=LONG,
        name="step_two",
    )(*keep_held(arrays), *bands, *after)


def add_up_kernel(shots, *refs):
    terms, out = refs[:shots], refs[2 * shots]
    total = terms[0][...]
    for term in terms[1:]:
        total += term[...]
    out[...] = total


def add_up(terms, passed):
    shots = len(terms)
    outs = pl.pallas_call(
        functools.partial(add_up_kernel, shots),
        out_shape=tuple(held(*array.shape) for array in (terms[0], *passed)),
        in_specs=[VMEM] * shots + [ANY] * shots,
        out_specs=(VMEM,) + (ANY,) * shots,
        input_output_aliases={shots + i: 1 + i for i in range(shots)},
        compiler_params=cheap(8),
        cost_estimate=COST,
        name="add_up",
    )(*keep_held((*terms, *passed)))
    return outs[0], outs[1:]


def finish_kernel(edge, by_f, by_a, halo0, halo1, near_out, keep_out):
    _, blocks, yb, _ = near_out.shape
    bit = lax.rem(lax.axis_index("shot"), 2)
    width = math.gcd(yb, STRIP)

    def strip(i, _):
        for out, mine in ((near_out, 1 - bit), (keep_out, bit)):
            for j in range(blocks):
                inside = pl.ds(pl.multiple_of(i * width, width), width)
                part = pl.ds(pl.multiple_of((2 * j + mine) * yb + i * width, width), width)
                for s, (_, upper) in enumerate(sides(2 * REACH)):
                    halo = (halo0, halo1)[s]
                    forward = halo_sums(lambda h, halo=halo: halo[0, h, part], upper)
                    adjoint = halo_sums(lambda h, halo=halo: halo[1, h, part], upper)
                    for q in range(REACH):
                        place = jnp.where(upper, q, REACH - 1 - q)
                        total = edge[s, place, part] + by_f[s, place, part] * forward[q]
                        out[s * REACH + place, j, inside] = total + by_a[s, place, part] * adjoint[q]
        return 0

    lax.fori_loop(0, yb // width, strip, 0)


def finish(edge, by_f, by_a, halos, shots):
    _, reach, ny, nz = edge.shape
    half = held(2 * reach, shots // 2, ny // shots, nz)
    return pl.pallas_call(
        finish_kernel,
        out_shape=(half, half),
        in_specs=[VMEM] * 5,
        out_specs=(VMEM,) * 2,
        compiler_params=cheap(16),
        cost_estimate=LONG,
        name="finish",
    )(edge, by_f, by_a, *halos)


def depth_kernel(layout, parts, pieces, *refs):
    used = sum(len(offsets) for offsets in parts)
    terms, refs = refs[:used], refs[used:]
    z_high, z_low = refs[:2]
    raw_out, outs, (raw_buf, spectrum, sems) = refs[-pieces - 4], refs[-pieces - 3 : -3], refs[-3:]
    planes, yb, nz = raw_buf.shape
    shots = lax.axis_size("shot")
    copies = Copies(sems)
    low, at = 0, 0
    for chunk, offsets in zip(layout, parts, strict=True):
        size = sum(count for _, count in chunk)
        total = None
        for offset in offsets:
            term = terms[at][offset : offset + size]
            total = term if total is None else total + term
            at += 1
        raw_buf[low : low + size] = total / shots
        low += size
    stores, done = [], 0
    rows = raw_out.shape[0]
    for chunk in layout:
        for where, count in chunk:
            base = sides(rows)[where][0] if isinstance(where, bool) else where
            stores.append(copies.start(raw_buf.at[pl.ds(done, count)], raw_out.at[pl.ds(base, count)]))
            done += count
    lanes = LANES // yb
    count = planes // lanes
    zb = nz // pieces

    def turn(p, _):
        rows_here = jnp.concatenate([raw_buf[h * count + p] for h in range(lanes)], axis=0)
        high, low_part = split(rows_here)
        table = z_high[...]
        spectrum[p] = (dot_t(table, high) + dot_t(table, low_part) + dot_t(z_low[...], high)).reshape(pieces, zb, LANES)
        return 0

    lax.fori_loop(0, count, turn, 0, unroll=2)
    offset = piece_offset()
    for k, out in enumerate(outs):
        out[...] = spectrum[:, lax.rem(offset + k, pieces)]
    wait_all(stores)


def depth(layout, terms, tables, raw_shape, pieces, after=(), previous=None):
    planes = sum(count for chunk in layout for _, count in chunk)
    _, yb, nz = raw_shape
    lanes = LANES // yb
    count = planes // lanes
    piece = held(count, nz // pieces, LANES)
    extra = (*after, *(() if previous is None else (previous,)))
    flat = [term for chunk in terms for term, _ in chunk]
    offsets = [[offset for _, offset in chunk] for chunk in terms]
    last = len(flat) + 2 + len(extra) - 1
    return pl.pallas_call(
        functools.partial(depth_kernel, layout, offsets, pieces),
        out_shape=(jax.ShapeDtypeStruct(raw_shape, F32),) + (piece,) * pieces,
        in_specs=[VMEM] * (len(flat) + 2) + [ANY] * len(extra),
        out_specs=(ANY,) + (VMEM,) * pieces,
        scratch_shapes=[
            pltpu.VMEM((planes, yb, nz), F32),
            pltpu.VMEM((count, pieces, nz // pieces, LANES), F32),
            pltpu.SemaphoreType.DMA((sum(len(chunk) for chunk in layout),)),
        ],
        input_output_aliases={} if previous is None else {last: 0},
        compiler_params=cheap(16),
        cost_estimate=LONG,
        name="depth",
    )(*flat, *tables, *extra)


def piece_offset():
    ratio = lax.axis_size("mp") // lax.axis_size("shot")
    return lax.axis_index("shot") * ratio + lax.rem(lax.axis_index("mp"), ratio)


def depth_edge_kernel(pieces, keep, near, z_high, z_low, own, *refs):
    far, outs, (total, spectrum) = refs[: -pieces - 2], refs[-pieces - 2 : -2], refs[-2:]
    planes, blocks, yb, nz = keep.shape
    total[...] = (keep[...] + near[...]) / lax.axis_size("shot")
    for i, term in enumerate((own, *far)):
        term[...] = total[:, lax.div(lax.axis_index("shot") ^ (2 * i), 2)]

    def turn(p, _):
        high, low = split(total[p].reshape(blocks * yb, nz))
        table = z_high[...]
        both = dot_t(table, high) + dot_t(table, low) + dot_t(z_low[...], high)
        spectrum[p] = both.reshape(pieces, nz // pieces, blocks * yb)
        return 0

    lax.fori_loop(0, planes, turn, 0, unroll=2)
    for k, out in enumerate(outs):
        out[...] = spectrum[:, lax.rem(piece_offset() + k, pieces)]


def depth_edge(keep, near, tables, pieces):
    planes, blocks, yb, nz = keep.shape
    term = held(planes, yb, nz)
    piece = held(planes, nz // pieces, blocks * yb)
    outs = pl.pallas_call(
        functools.partial(depth_edge_kernel, pieces),
        out_shape=(term,) * blocks + (piece,) * pieces,
        in_specs=[VMEM] * 4,
        out_specs=(VMEM,) * (blocks + pieces),
        scratch_shapes=[
            pltpu.VMEM(keep.shape, F32),
            pltpu.VMEM((planes, pieces, nz // pieces, blocks * yb), F32),
        ],
        compiler_params=cheap(12),
        cost_estimate=LONG,
        name="depth_edge",
    )(keep, near, *tables)
    return outs[:blocks], outs[blocks:]


def raw_edge_kernel(*refs):
    terms, (raw_out, buf, sems) = refs[:-4], refs[-3:]
    total = terms[0][...]
    for term in terms[1:]:
        total += term[...]
    buf[...] = total
    copies = Copies(sems)
    wait_all([
        copies.start(buf.at[pl.ds(s * REACH, REACH)], raw_out.at[pl.ds(base, REACH)])
        for s, (base, _) in enumerate(sides(raw_out.shape[0]))
    ])


def raw_edge(terms, raw):
    return pl.pallas_call(
        raw_edge_kernel,
        out_shape=jax.ShapeDtypeStruct(raw.shape, F32),
        in_specs=[VMEM] * len(terms) + [ANY],
        out_specs=ANY,
        scratch_shapes=[pltpu.VMEM(terms[0].shape, F32), pltpu.SemaphoreType.DMA((2,))],
        input_output_aliases={len(terms): 0},
        compiler_params=cheap(8),
        cost_estimate=COST,
        name="raw_edge",
    )(*terms, raw)


def gather_planes(ratio, shots, parts, buf, field, sems):
    pieces = len(parts)
    mp = lax.axis_index("mp")
    copies = Copies(sems)
    loads = []
    for k, part in enumerate(parts):
        q = lax.rem(mp - k + pieces, pieces)
        loads.append(copies.start(part, buf.at[lax.rem(q, ratio), lax.div(q, ratio)]))
    wait_all(loads)
    count = buf.shape[2]
    _, zb, ny = field.shape
    yb = ny // shots
    lanes = LANES // yb
    slot_of = lax.broadcasted_iota(jnp.int32, (zb, LANES), 1) // yb
    for sub in range(ratio):
        for p in range(count):
            for h in range(lanes):
                x = sub * count * lanes + h * count + p
                for t in range(shots // lanes):
                    value = None
                    for e in range(lanes):
                        piece = buf[sub, t * lanes + e, p]
                        if e != h:
                            piece = pltpu.roll(piece, (e - h) * yb % LANES, 1)
                        value = piece if value is None else jnp.where(slot_of == e, piece, value)
                    field[x, :, pl.ds(t * LANES, LANES)] = value


def gather_halves(ratio, shots, parts, buf, field, sems):
    pieces = len(parts)
    copies = Copies(sems)
    loads = []
    for k, part in enumerate(parts):
        q = lax.rem(lax.axis_index("mp") - k + pieces, pieces)
        loads.append(copies.start(part, buf.at[lax.rem(q, ratio), lax.div(q, ratio)]))
    wait_all(loads)
    _, _, count, zb, half = buf.shape
    ny = field.shape[2]
    yb = ny // shots
    lanes = LANES // yb
    slot_of = lax.broadcasted_iota(jnp.int32, (zb, LANES), 1) // yb
    for sub in range(ratio):
        for p in range(count):
            cores = [sum(buf[sub, s, p] for s in range(core, shots, 2)) for core in (0, 1)]
            for t in range(ny // LANES):
                value = None
                for e in range(lanes):
                    core, place = (t * lanes + e) % 2, (t * lanes + e) // 2
                    low = place // lanes * LANES
                    piece = cores[core][:, low : low + LANES]
                    if e != place % lanes:
                        piece = pltpu.roll(piece, (e - place % lanes) * yb % LANES, 1)
                    value = piece if value is None else jnp.where(slot_of == e, piece, value)
                field[sub * count + p, :, pl.ds(t * LANES, LANES)] = value


def gather_kernel(ratio, shots, *refs):
    parts, (y_high, y_low, out, buf, field, sems) = refs[:-6], refs[-6:]
    gather_planes(ratio, shots, parts, buf, field, sems)
    filter_second(field, out, y_high[...], y_low[...])


def filter_second(field, out, high_t, low_t):
    total, zb, ny = field.shape
    step = max(1, 256 // zb)
    while total % step:
        step -= 1
    for i in range(0, total, step):
        high, low = split(field[i : i + step].reshape(step * zb, ny))
        result = dot_t(high, high_t) + dot_t(low, high_t) + dot_t(high, low_t)
        out[i : i + step] = result.reshape(step, zb, ny)


def gather(parts, tables, ratio, shots):
    pieces = len(parts)
    count, zb, _ = parts[0].shape
    ny = tables[0].shape[0]
    total = ratio * count * (LANES * shots // ny)
    return pl.pallas_call(
        functools.partial(gather_kernel, ratio, shots),
        out_shape=held(total, zb, ny),
        in_specs=[VMEM] * (pieces + 2),
        out_specs=VMEM,
        scratch_shapes=[
            pltpu.VMEM((ratio, shots, count, zb, LANES), F32),
            pltpu.VMEM((total, zb, ny), F32),
            pltpu.SemaphoreType.DMA((pieces,)),
        ],
        compiler_params=cheap(16),
        cost_estimate=LONG,
        name="gather",
    )(*parts, *tables)


def scan_kernel(planes, rows, ratio, shots, scan, mains, *refs):
    refs, (buf, field, edges, ends, sems) = refs[:-5], refs[-5:]
    parts, (y_high, y_low, out), sends = refs[: -shots - 2], refs[-shots - 2 : -shots + 1], refs[-shots + 1 :]
    gather_halves(ratio, shots, parts, buf, edges, sems)
    filter_second(edges, edges, y_high[...], y_low[...])
    shot = lax.axis_index("shot")
    total, zb, ny = field.shape
    per_slab = len(planes)
    for sub in range(ratio):
        for i, x in enumerate(planes):
            field[sub * rows + x] = mains[sub * per_slab + i]
        even = lax.rem(shot * ratio + sub, 2) == 0
        for s, base in enumerate((jnp.where(even, rows - REACH, 0), jnp.where(even, 0, rows - REACH))):
            for q in range(REACH):
                field[sub * rows + base + q] = edges[sub * 2 * REACH + s * REACH + q]
    first_x = shot * total

    def up(x, carry):
        carry = field[x] + scan[1, first_x + x] * carry
        out[x] = carry
        return carry

    ends[0] = lax.fori_loop(0, total, up, jnp.zeros((zb, ny), F32))

    def down(i, carry):
        x = total - 1 - i
        out[x] = (out[x] + carry) * scan[0, first_x + x]
        return scan[2, first_x + x - 1] * (field[x] + carry)

    carry = lax.fori_loop(0, total - 1, down, jnp.zeros((zb, ny), F32))
    out[0] = (out[0] + carry) * scan[0, first_x]
    ends[1] = field[0] + carry
    for j, send in enumerate(sends, 1):
        send[...] = jnp.where((shot ^ j) > shot, ends[0], ends[1])


def scan_first(scan, mains, parts, tables, planes, rows, shots):
    per_slab = len(planes)
    ratio = mains.shape[0] // per_slab
    _, zb, ny = mains.shape
    end = held(zb, ny)
    total = rows * ratio
    pieces, count = len(parts), parts[0].shape[0]
    return pl.pallas_call(
        functools.partial(scan_kernel, planes, rows, ratio, shots),
        out_shape=(held(total, zb, ny),) + (end,) * (shots - 1),
        in_specs=[SMEM] + [VMEM] * (pieces + 3),
        out_specs=(VMEM,) * shots,
        scratch_shapes=[
            pltpu.VMEM((ratio, shots, count, zb, ny // 2), F32),
            pltpu.VMEM((total, zb, ny), F32),
            pltpu.VMEM((2 * REACH * ratio, zb, ny), F32),
            pltpu.VMEM((2, zb, ny), F32),
            pltpu.SemaphoreType.DMA((pieces,)),
        ],
        compiler_params=cheap(16),
        cost_estimate=COST,
        name="scan",
    )(scan, mains, *parts, *tables)


def join_kernel(shots, scan, carry, part, *refs):
    ends, out = refs[: shots - 1], refs[shots]
    total, zb, ny = part.shape
    shot = lax.axis_index("shot")
    first_x = shot * total
    below = jnp.zeros((zb, ny), F32)
    above = jnp.zeros((zb, ny), F32)
    for j, end in enumerate(ends, 1):
        other = shot ^ j
        term = carry[shot, other] * end[...]
        below += jnp.where(other < shot, term, 0.0)
        above += jnp.where(other > shot, term, 0.0)
    for x in range(total):
        out[x] = part[x] + scan[3, first_x + x] * below + scan[4, first_x + x] * above


def join(scan, carry, part, ends, after):
    total, zb, ny = part.shape
    shots = len(ends) + 1
    return pl.pallas_call(
        functools.partial(join_kernel, shots),
        out_shape=jax.ShapeDtypeStruct((total, zb, ny), F32),
        in_specs=[SMEM] * 2 + [VMEM] * shots + [ANY],
        out_specs=VMEM,
        compiler_params=cheap(16),
        cost_estimate=COST,
        name="join",
    )(scan, carry, part, *ends, *in_hbm((after,)))


def neighbours(count, start):
    low = range(start, count - 1, 2)
    return [(i, i + 1) for i in low] + [(i + 1, i) for i in low]


def swap(values):
    count = lax.axis_size("mp")
    return keep_held(lax.ppermute(v, "mp", neighbours(count, start)) for start, v in enumerate(values))


def flip(value, bit):
    count = lax.axis_size("shot")
    got = lax.ppermute(value, "shot", [(i, i ^ bit) for i in range(count)])
    return keep_held((got,))[0]


def share(terms, step):
    return [terms[0]] + [flip(term, step * i) for i, term in enumerate(terms[1:], 1)]


def spread(pieces, ratio):
    mp, shots = lax.axis_size("mp"), lax.axis_size("shot")
    out = []
    for k, piece in enumerate(pieces):
        pairs = []
        for m in range(mp):
            for s in range(shots):
                target = (s * ratio + m % ratio + k) % mp
                pairs.append((m * shots + s, target * shots + m // ratio))
        out.append(lax.ppermute(piece, ("mp", "shot"), pairs))
    return keep_held(out)


def per_device(
    courant, forward_old, forward_now, adjoint_late, adjoint_now,
    src_cell, src_sign, wavelet, rec_cell, rec_data,
):
    mp_count, shots = lax.axis_size("mp"), lax.axis_size("shot")
    rows, ny, nz = courant.shape
    ratio = mp_count // shots
    full_x = rows * mp_count
    band_y, band_z = band(ny), band(nz)
    bands = (jnp.asarray(band_y, BF16), jnp.asarray(np.concatenate([band_z, band_z]), BF16))
    strength = float(SMOOTH_YZ * SMOOTH_YZ)
    strength_x = float(SMOOTH_X * SMOOTH_X)
    scan, carry = scan_tables(full_x, strength_x, rows * ratio)
    kappa = 1.0
    for length, e in ((full_x, strength_x), (ny, strength), (nz, strength)):
        resp = response(length, e)
        kappa /= math.sqrt(np.mean(resp * resp))
    z_tables = split_table(filter_matrix(nz, strength))
    y_tables = split_table(kappa * filter_matrix(ny, strength))

    f_old, f_now, a_late, a_now = forward_old[0], forward_now[0], adjoint_late[0], adjoint_now[0]
    halos = swap(pick(f_now, a_now))
    c, accel, nxt, mid, a_base, src, *inner = step_one(
        src_cell, src_sign, wavelet, rec_cell, rec_data, courant, f_old, f_now, a_late, a_now, bands, shots
    )
    accel, nxt, mid, a_base, edge0, edge1 = correct(c, accel, nxt, mid, a_base, halos)
    halos = swap((edge0, edge1))
    inner = share(inner, 1)
    edge, by_f, by_a, *outer = step_two((c, accel, nxt, mid, a_base, src), bands, (), shots)
    inner, outer = add_up(inner, outer)
    outer = share(outer, 1)
    near, keep = finish(edge, by_f, by_a, halos, shots)
    raw_shape = (rows, ny // shots, nz)
    layout = [[(2 * REACH, rows - 4 * REACH)], [(REACH, REACH), (rows - 2 * REACH, REACH)]]
    terms = [[(term, 0) for term in chunk] for chunk in ((inner,), outer)]
    raw, *mains = depth(layout, terms, z_tables, raw_shape, mp_count)
    mains = gather(spread(mains, ratio), y_tables, ratio, shots)
    last, edges = depth_edge(keep, flip(near, 1), z_tables, mp_count)
    raw = raw_edge(share(last, 2), raw)
    edges = spread(edges, ratio)
    planes = [low + i for chunk in layout for low, count in chunk for i in range(count)]
    part, *ends = scan_first(jnp.asarray(scan), mains, edges, y_tables, planes, rows, shots)
    ends = [flip(end, j) for j, end in enumerate(ends, 1)]
    smooth = join(jnp.asarray(scan), jnp.asarray(carry), part, ends, raw)
    smooth = jnp.transpose(smooth, (0, 2, 1))
    return raw, smooth


def solution(mesh):
    return jax.shard_map(
        per_device,
        mesh=mesh,
        in_specs=(
            P(("parts", "mp"), None, None),
            P(("parts", "shot"), "mp", None, None),
            P(("parts", "shot"), "mp", None, None),
            P(("parts", "shot"), "mp", None, None),
            P(("parts", "shot"), "mp", None, None),
            P(("parts", "shot"), None),
            P(("parts", "shot"), None),
            P(("parts", "shot"), None, None),
            P("parts"),
            P(("parts", "shot"), None, None),
        ),
        out_specs=(P(("parts", "mp"), "shot", None), P(("parts", "shot"), None, "mp")),
        check_vma=False,
    )
```

time: 119 us -> 108 us (0.908)
  Pallas kernels: 57 us -> 52.3 us
  waiting for transfers between devices: 18.6 us -> 14.9 us
  starting transfers between devices: 42.3 us -> 39.3 us
    ppermute x8, starting transfers between devices: 24.9 us -> 16.7 us  [spread(): out.append(lax.ppermute(piece, ('mp', 'shot'), pairs))]
    pallas_call x1, Pallas kernels: 27.9 us -> 20.1 us  [step_one(): pl.pallas_call(step_one_kernel, out_shape=tuple((held(*shape) for shape i...]
    pallas_call x5 -> x7, Pallas kernels: 11.7 us -> 16.8 us  [the longest x1 3.17 us: depth_edge(): pl.pallas_call(functools.partial(depth_edge_kernel, pieces), out_shape=(t...]
    ppermute x11, waiting for transfers between devices: 6.38 us -> 1.58 us  [flip(): got = lax.ppermute(value, 'shot', [(i, i ^ bit) for i in range(count)])]
    ppermute x11, starting transfers between devices: 7.35 us -> 11.7 us  [flip(): got = lax.ppermute(value, 'shot', [(i, i ^ bit) for i in range(count)])]
    pallas_call x2 -> x1, Pallas kernels: 6.12 us -> 3.12 us  [depth(): pl.pallas_call(functools.partial(depth_kernel, layout, offsets, pieces),...]
    ppermute x8, waiting for transfers between devices: 0.04 us -> 2.03 us  [spread(): out.append(lax.ppermute(piece, ('mp', 'shot'), pairs))]
  transfers between devices with their start and end apart: 23 -> 23, of which waited for: 5 -> 4; matrix products, arithmetic and copies ran while one was open for 0% -> 0% of each run, Pallas kernels for 38% -> 44%
where the time goes in v3:
time: 108 us; the launch traced here: 107 us
  Pallas kernels  52.3 us (48%)
  starting transfers between devices  39.3 us (36%)
  waiting for transfers between devices  14.9 us (14%)
    pallas_call x1, Pallas kernels, step_one(): pl.pallas_call(step_one_kernel, out_shape=tuple((held(*shape) for shape i...  20.1 us
    ppermute x8, starting transfers between devices, spread(): out.append(lax.ppermute(piece, ('mp', 'shot'), pairs))  16.7 us
    ppermute x11, starting transfers between devices, flip(): got = lax.ppermute(value, 'shot', [(i, i ^ bit) for i in range(count)])  11.7 us
    ppermute x4, waiting for transfers between devices, swap(): lax.ppermute(v, 'mp', neighbours(count, start))  11.2 us
    ppermute x4, starting transfers between devices, swap(): lax.ppermute(v, 'mp', neighbours(count, start))  10.8 us
    pallas_call x1, Pallas kernels, step_two(): pl.pallas_call(functools.partial(step_two_kernel, len(after)), out_shape=...  6.92 us
    pallas_call x1, Pallas kernels, correct(): pl.pallas_call(correct_kernel, out_shape=tuple((held(*array.shape) for ar...  3.65 us
    pallas_call x1, Pallas kernels, depth_edge(): pl.pallas_call(functools.partial(depth_edge_kernel, pieces), out_shape=(t...  3.17 us
  transfers between devices with their start and end apart: 23, of which 4 were waited for; matrix products, arithmetic and copies ran while one was open for 0% of the time, Pallas kernels for 44%

profile of v3, /device:TPU:0, one launch (start us, length us, event | category | flops | bytes accessed | tf_op | source)
XLA Modules:
  0.0 107.4 jit_solution(12518384350255327542)
XLA Ops:
  0.7 0.0 copy-start.8
  0.7 0.0 copy-start.9
  0.7 3.0 %pick.1 = (f32[2,4,256,128]{3,2,1,0:T(8,128)}, f32[2,4,256,128]{3,2,1,0:T(8,128)}) custom-call(f32[24,256,128]{2,1,0:T(8,128)} %bitcast.13, f32[24,256,128]{2,1,0:T(8,128)} %bitcast.15), custom_call_target="tpu_custom_call" | custom-call | flops 1000 | bytes 1000 | tf_op jit(solution)/shard_map/pick/pallas_call | solution.py:370
  3.7 3.1 %collective-permute-start = (f32[2,4,256,128]{3,2,1,0:T(8,128)}, f32[2,4,256,128]{3,2,1,0:T(8,128)}, u32[]{:S(2)}, u32[]{:S(2)}) collective-permute-start(f32[2,4,256,128]{3,2,1,0:T(8,128)} %get-tuple-element.54), channel_id=1, source_target_pairs={{0,4},{8,12},{4,0},{12,8},{1,5},{9,13},{5,1},{13,9},{2,6},{10,14},... | collective-permute-start | bytes 3145736 | tf_op jit(solution)/shard_map/ppermute | solution.py:876
  6.8 1.6 %collective-permute-start.1 = (f32[2,4,256,128]{3,2,1,0:T(8,128)}, f32[2,4,256,128]{3,2,1,0:T(8,128)}, u32[]{:S(2)}, u32[]{:S(2)}) collective-permute-start(f32[2,4,256,128]{3,2,1,0:T(8,128)} %get-tuple-element.55), channel_id=1, source_target_pairs={{4,8},{8,4},{5,9},{9,5},{6,10},{10,6},{7,11},{11,7},{20,24},{24,20... | collective-permute-start | bytes 3145736 | tf_op jit(solution)/shard_map/ppermute | solution.py:876
  8.5 20.1 %step_one.1 = (f32[24,256,128]{2,1,0:T(8,128)S(1)}, f32[24,256,128]{2,1,0:T(8,128)S(1)}, f32[32,256,128]{2,1,0:T(8,128)S(1)}, f32[32,256,128]{2,1,0:T(8,128)S(1)...) custom-call(s32[1,64]{1,0:T(1,128)S(1)} %copy-done.6, ...), custom_call_target="tpu_custom_call" | custom-call | flops 999999995904 | bytes 1000 | tf_op jit(solution)/shard_map/step_one/pallas_call | solution.py:308
  28.6 0.1 collective-permute-start.6
  28.7 1.6 %collective-permute-start.7 = (f32[8,64,128]{2,1,0:T(8,128)}, f32[8,64,128]{2,1,0:T(8,128)}, u32[]{:S(2)}, u32[]{:S(2)}) collective-permute-start(f32[8,64,128]{2,1,0:T(8,128)} %get-tuple-element.72), channel_id=1, source_target_pairs={{0,2},{1,3},{2,0},{3,1},{4,6},{5,7},{6,4},{7,5},{8,10},{9,11},{10,... | collective-permute-start | bytes 786440 | tf_op jit(solution)/shard_map/ppermute | solution.py:881
  30.3 0.3 collective-permute-start.8
  30.6 3.7 %correct.1 = (f32[24,256,128]{2,1,0:T(8,128)S(1)}, f32[32,256,128]{2,1,0:T(8,128)S(1)}, f32[32,256,128]{2,1,0:T(8,128)S(1)}, f32[24,256,128]{2,1,0:T(8,128)S(1)}...) custom-call(f32[24,256,128]{2,1,0:T(8,128)S(1)} %get-tuple-element.4, ...), custom_call_target="tpu_custom_call", output_to_operand_aliasing={{0}: (1, {}), {1}: (2, {}), {2}: (3, {}), {3}: (4, {})} | custom-call | flops 1000 | bytes 1000 | tf_op jit(solution)/shard_map/correct/pallas_call | solution.py:414
  34.2 4.5 %collective-permute-start.2 = (f32[2,4,256,128]{3,2,1,0:T(8,128)}, f32[2,4,256,128]{3,2,1,0:T(8,128)}, u32[]{:S(2)}, u32[]{:S(2)}) collective-permute-start(f32[2,4,256,128]{3,2,1,0:T(8,128)} %get-tuple-element.64), channel_id=1, source_target_pairs={{0,4},{8,12},{4,0},{12,8},{1,5},{9,13},{5,1},{13,9},{2,6},{10,14},... | collective-permute-start | bytes 3145736 | tf_op jit(solution)/shard_map/ppermute | solution.py:876
  38.7 1.6 %collective-permute-start.3 = (f32[2,4,256,128]{3,2,1,0:T(8,128)}, f32[2,4,256,128]{3,2,1,0:T(8,128)}, u32[]{:S(2)}, u32[]{:S(2)}) collective-permute-start(f32[2,4,256,128]{3,2,1,0:T(8,128)} %get-tuple-element.65), channel_id=1, source_target_pairs={{4,8},{8,4},{5,9},{9,5},{6,10},{10,6},{7,11},{11,7},{20,24},{24,20... | collective-permute-start | bytes 3145736 | tf_op jit(solution)/shard_map/ppermute | solution.py:876
  40.3 6.9 %step_two.1 = (f32[2,4,256,128]{3,2,1,0:T(8,128)S(1)}, f32[2,4,256,128]{3,2,1,0:T(8,128)S(1)}, f32[2,4,256,128]{3,2,1,0:T(8,128)S(1)}, f32[8,64,128]{2,1,0:T(8,1...) custom-call(f32[24,256,128]{2,1,0:T(8,128)S(1)} %get-tuple-element.49.c_buf, ...), custom_call_target="tpu_custom_call" | custom-call | flops 999999995904 | bytes 1000 | tf_op jit(solution)/shard_map/step_two/pallas_call | solution.py:471
  47.3 0.0 collective-permute-done.6.refs_1_
  47.3 0.0 collective-permute-done.7.refs_2_
  47.3 1.2 %add_up.1 = (f32[8,64,128]{2,1,0:T(8,128)S(1)}, f32[8,64,128]{2,1,0:T(8,128)S(1)}, f32[8,64,128]{2,1,0:T(8,128)}, f32[8,64,128]{2,1,0:T(8,128)}, f32[8,64,128]{2,1,0:T(8,128)}) custom-call(f32[8,64,128]{2,1,0:T(8,128)S(1)} %get-tuple-element.70.refs_0_, ...), custom_call_target="tpu_custom_call", output_to_operand_aliasing={{1}: (4, {}), {2}: (5, {}), {3}: (6, {}), {4}: (7, {})} | custom-call | flops 1000 | bytes 1000 | tf_op jit(solution)/shard_map/add_up/pallas_call | solution.py:493
  48.5 0.1 collective-permute-start.9
  48.5 1.6 %collective-permute-start.10 = (f32[8,64,128]{2,1,0:T(8,128)}, f32[8,64,128]{2,1,0:T(8,128)}, u32[]{:S(2)}, u32[]{:S(2)}) collective-permute-start(f32[8,64,128]{2,1,0:T(8,128)} %get-tuple-element.81), channel_id=1, source_target_pairs={{0,2},{1,3},{2,0},{3,1},{4,6},{5,7},{6,4},{7,5},{8,10},{9,11},{10,... | collective-permute-start | bytes 786440 | tf_op jit(solution)/shard_map/ppermute | solution.py:881
  50.1 0.3 collective-permute-start.11
  50.4 11.2 %collective-permute-done.2.halo0 = f32[2,4,256,128]{3,2,1,0:T(8,128)} collective-permute-done((f32[2,4,256,128]{3,2,1,0:T(8,128)}, f32[2,4,256,128]{3,2,1,0:T(8,128)}, u32[]{:S(2)}, u32[]{:S(2)}) %collective-permute-start.2) | collective-permute-done | bytes 1048608 | tf_op jit(solution)/shard_map/ppermute | solution.py:876
  61.6 0.0 collective-permute-done.3.halo1
  61.6 2.8 %finish.1 = (f32[8,2,64,128]{3,2,1,0:T(8,128)}, f32[8,2,64,128]{3,2,1,0:T(8,128)S(1)}) custom-call(f32[2,4,256,128]{3,2,1,0:T(8,128)S(1)} %get-tuple-element.61.edge, f32[2,4,256,128]{3,2,1,0:T(8,128)S(1)} %get-tuple-element.62.by_f, f32[2,4,256,128]{3,2,1,0:T(8,128)S(1)} %get-tuple-element.63.by_a, f32[2,4,256,128]{3,2,1,0:T(8,128)} %collective-permute-done.2.halo0, ...), custom_call_target="tpu_custom_call" | custom-call | flops 999999995904 | bytes 1000 | tf_op jit(solution)/shard_map/finish/pallas_call | solution.py:532
  64.5 0.0 collective-permute-start.4
  64.5 0.0 collective-permute-done.9.refs_2_
  64.5 0.0 collective-permute-done.10.refs_3_
  64.5 0.0 collective-permute-done.11.refs_4_
  64.5 3.1 %depth.1 = (f32[24,64,128]{2,1,0:T(8,128)}, f32[8,32,128]{2,1,0:T(8,128)}, f32[8,32,128]{2,1,0:T(8,128)}, f32[8,32,128]{2,1,0:T(8,128)}, f32[8,32,128]{2,1,0:T(8,128)}) custom-call(f32[8,64,128]{2,1,0:T(8,128)S(1)} %get-tuple-element.78.refs_0_, f32[8,64,128]{2,1,0:T(8,128)S(1)} %get-tuple-element.79.refs_1_, f32[8,64,128]{2,1,0:T(8,128)} %collective-permute-done.9.refs_2_, ...), custom_call_target="tpu_custom_call" | custom-call | flops 999999995904 | bytes 1000 | tf_op jit(solution)/shard_map/depth/pallas_call | solution.py:596
  67.6 2.2 %collective-permute-start.12 = (f32[8,32,128]{2,1,0:T(8,128)}, f32[8,32,128]{2,1,0:T(8,128)}, u32[]{:S(2)}, u32[]{:S(2)}) collective-permute-start(f32[8,32,128]{2,1,0:T(8,128)} %get-tuple-element.84), channel_id=1, source_target_pairs={{0,0},{1,4},{2,8},{3,12},{4,1},{5,5},{6,9},{7,13},{8,2},{9,6},{10,... | collective-permute-start | bytes 393224 | tf_op jit(solution)/shard_map/ppermute | solution.py:898
  69.8 3.5 %collective-permute-start.13 = (f32[8,32,128]{2,1,0:T(8,128)}, f32[8,32,128]{2,1,0:T(8,128)}, u32[]{:S(2)}, u32[]{:S(2)}) collective-permute-start(f32[8,32,128]{2,1,0:T(8,128)} %get-tuple-element.85), channel_id=1, source_target_pairs={{0,4},{1,8},{2,12},{3,0},{4,5},{5,9},{6,13},{7,1},{8,6},{9,10},{10... | collective-permute-start | bytes 393224 | tf_op jit(solution)/shard_map/ppermute | solution.py:898
  73.3 3.5 %collective-permute-start.14 = (f32[8,32,128]{2,1,0:T(8,128)}, f32[8,32,128]{2,1,0:T(8,128)}, u32[]{:S(2)}, u32[]{:S(2)}) collective-permute-start(f32[8,32,128]{2,1,0:T(8,128)} %get-tuple-element.86), channel_id=1, source_target_pairs={{0,8},{1,12},{2,0},{3,4},{4,9},{5,13},{6,1},{7,5},{8,10},{9,14},{1... | collective-permute-start | bytes 393224 | tf_op jit(solution)/shard_map/ppermute | solution.py:898
  76.8 2.0 %collective-permute-start.15 = (f32[8,32,128]{2,1,0:T(8,128)}, f32[8,32,128]{2,1,0:T(8,128)}, u32[]{:S(2)}, u32[]{:S(2)}) collective-permute-start(f32[8,32,128]{2,1,0:T(8,128)} %get-tuple-element.87), channel_id=1, source_target_pairs={{0,12},{1,0},{2,4},{3,8},{4,13},{5,1},{6,5},{7,9},{8,14},{9,2},{10... | collective-permute-start | bytes 393224 | tf_op jit(solution)/shard_map/ppermute | solution.py:898
  78.8 0.0 collective-permute-done.4.near
  78.8 3.2 %depth_edge.1 = (f32[8,64,128]{2,1,0:T(8,128)S(1)}, f32[8,64,128]{2,1,0:T(8,128)}, f32[8,32,128]{2,1,0:T(8,128)}, f32[8,32,128]{2,1,0:T(8,128)}, f32[8,32,128]{2,1,0:T(8,128)}, /*index=5*/f32[8,32,128]{2,1,0:T(8,128)}) custom-call(f32[8,2,64,128]{3,2,1,0:T(8,128)S(1)} %get-tuple-element.66.keep, f32[8,2,64,128]{3,2,1,0:T(8,128)} %collective-permute-done.4.near, ...), custom_call_target="tpu_custom_call" | custom-call | flops 999999995904 | bytes 1000 | tf_op jit(solution)/shard_map/depth_edge/pallas_call | solution.py:641
  81.9 2.2 %collective-permute-start.16 = (f32[8,32,128]{2,1,0:T(8,128)}, f32[8,32,128]{2,1,0:T(8,128)}, u32[]{:S(2)}, u32[]{:S(2)}) collective-permute-start(f32[8,32,128]{2,1,0:T(8,128)} %get-tuple-element.88), channel_id=1, source_target_pairs={{0,0},{1,4},{2,8},{3,12},{4,1},{5,5},{6,9},{7,13},{8,2},{9,6},{10,... | collective-permute-start | bytes 393224 | tf_op jit(solution)/shard_map/ppermute | solution.py:898
  84.1 2.9 %collective-permute-start.18 = (f32[8,32,128]{2,1,0:T(8,128)}, f32[8,32,128]{2,1,0:T(8,128)}, u32[]{:S(2)}, u32[]{:S(2)}) collective-permute-start(f32[8,32,128]{2,1,0:T(8,128)} %get-tuple-element.90), channel_id=1, source_target_pairs={{0,8},{1,12},{2,0},{3,4},{4,9},{5,13},{6,1},{7,5},{8,10},{9,14},{1... | collective-permute-start | bytes 393224 | tf_op jit(solution)/shard_map/ppermute | solution.py:898
  87.0 0.6 collective-permute-start.19
  87.6 2.3 %collective-permute-start.5 = (f32[8,64,128]{2,1,0:T(8,128)}, f32[8,64,128]{2,1,0:T(8,128)}, u32[]{:S(2)}, u32[]{:S(2)}) collective-permute-start(f32[8,64,128]{2,1,0:T(8,128)} %get-tuple-element.69), channel_id=1, source_target_pairs={{0,2},{1,3},{2,0},{3,1},{4,6},{5,7},{6,4},{7,5},{8,10},{9,11},{10,... | collective-permute-start | bytes 786440 | tf_op jit(solution)/shard_map/ppermute | solution.py:881
  89.9 2.3 %gather.1.mains = f32[16,32,256]{2,1,0:T(8,128)S(1)} custom-call(f32[8,32,128]{2,1,0:T(8,128)} %collective-permute-done.12.refs_0_, f32[8,32,128]{2,1,0:T(8,128)} %collective-permute-done.13.refs_1_, f32[8,32,128]{2,1,0:T(8,128)} %collective-permute-done.14.refs_2_, f32[8,32,128]{2,1,0:T(8,128)} %collective-permute-done.15.refs_3_, ...), custom_call_target="tpu_custom_call" | custom-call | flops 999999995904 | bytes 1000 | tf_op jit(solution)/shard_map/gather/pallas_call | solution.py:762
  92.1 0.0 copy-start.3
  92.2 2.0 %collective-permute-done.18.refs_2_ = f32[8,32,128]{2,1,0:T(8,128)} collective-permute-done((f32[8,32,128]{2,1,0:T(8,128)}, f32[8,32,128]{2,1,0:T(8,128)}, u32[]{:S(2)}, u32[]{:S(2)}) %collective-permute-start.18) | collective-permute-done | bytes 131104 | tf_op jit(solution)/shard_map/ppermute | solution.py:898
  94.2 2.7 %scan.3 = (f32[24,32,256]{2,1,0:T(8,128)S(1)}, f32[32,256]{1,0:T(8,128)S(1)}, f32[32,256]{1,0:T(8,128)S(1)}, f32[32,256]{1,0:T(8,128)S(1)}) custom-call(f32[5,96]{1,0:T(8,128)S(1)} %copy-done.2, f32[16,32,256]{2,1,0:T(8,128)S(1)} %gather.1.mains, f32[8,32,128]{2,1,0:T(8,128)} %collective-permute-done.16.refs_0_, ...), custom_call_target="tpu_custom_call" | custom-call | flops 1000 | bytes 1000 | tf_op jit(solution)/shard_map/scan/pallas_call | solution.py:821
  96.9 3.2 %collective-permute-start.20 = (f32[32,256]{1,0:T(8,128)S(1)}, f32[32,256]{1,0:T(8,128)S(1)}, u32[]{:S(2)}, u32[]{:S(2)}) collective-permute-start(f32[32,256]{1,0:T(8,128)S(1)} %get-tuple-element.93), channel_id=1, source_target_pairs={{0,1},{1,0},{2,3},{3,2},{4,5},{5,4},{6,7},{7,6},{8,9},{9,8},{10,11... | collective-permute-start | bytes 98312 | tf_op jit(solution)/shard_map/ppermute | solution.py:881
  100.1 2.3 %collective-permute-start.21 = (f32[32,256]{1,0:T(8,128)S(1)}, f32[32,256]{1,0:T(8,128)S(1)}, u32[]{:S(2)}, u32[]{:S(2)}) collective-permute-start(f32[32,256]{1,0:T(8,128)S(1)} %get-tuple-element.94), channel_id=1, source_target_pairs={{0,2},{1,3},{2,0},{3,1},{4,6},{5,7},{6,4},{7,5},{8,10},{9,11},{10,... | collective-permute-start | bytes 98312 | tf_op jit(solution)/shard_map/ppermute | solution.py:881
  102.4 0.1 collective-permute-start.22
  102.5 1.7 %raw_edge.1.refs_3_ = f32[24,64,128]{2,1,0:T(8,128)} custom-call(f32[8,64,128]{2,1,0:T(8,128)S(1)} %get-tuple-element.68.refs_0_, f32[8,64,128]{2,1,0:T(8,128)} %collective-permute-done.5.refs_1_, f32[24,64,128]{2,1,0:T(8,128)} %get-tuple-element.83.refs_2_), custom_call_target="tpu_custom_call", output_to_operand_aliasing={{}: (2, {})} | custom-call | flops 1000 | bytes 1000 | tf_op jit(solution)/shard_map/raw_edge/pallas_call | solution.py:671
  104.2 0.2 collective-permute-done.21.refs_1_
  104.4 1.4 %collective-permute-done.22.refs_2_ = f32[32,256]{1,0:T(8,128)S(1)} collective-permute-done((f32[32,256]{1,0:T(8,128)S(1)}, f32[32,256]{1,0:T(8,128)S(1)}, u32[]{:S(2)}, u32[]{:S(2)}) %collective-permute-start.22) | collective-permute-done | bytes 32800 | tf_op jit(solution)/shard_map/ppermute | solution.py:881
  105.7 1.6 %join.1 = f32[24,32,256]{2,1,0:T(8,128)} custom-call(f32[5,96]{1,0:T(8,128)S(1)} %copy-done.2, f32[4,4]{1,0:T(4,128)S(1)} %copy-done.3, f32[24,32,256]{2,1,0:T(8,128)S(1)} %get-tuple-element.92.part, f32[32,256]{1,0:T(8,128)S(1)} %collective-permute-done.20.refs_0_, f32[32,256]{1,0:T(8,128)S(1)} %collective-permute-done.21.refs_1_, ...), custom_call_target="tpu_custom_call" | custom-call | flops 1000 | bytes 1000 | tf_op jit(solution)/shard_map/join/pallas_call | solution.py:858
  (37 shorter events, 0.1 us)
Async XLA Ops:
  0.6 7.8 %copy-start.12 = (f32[1,2,2048]{2,1,0:T(2,128)S(1)}, f32[1,2,2048]{2,1,0:T(2,128)}, u32[]{:S(2)}) copy-start(f32[1,2,2048]{2,1,0:T(2,128)} %param.27) | copy-start | bytes 49156
  0.6 7.8 %copy-start.4 = (s32[2048]{0:T(1024)S(1)}, s32[2048]{0:T(1024)}, u32[]{:S(2)}) copy-start(s32[2048]{0:T(1024)} %param.26) | copy-start | bytes 24580
  0.7 7.8 %copy-start.5 = (f32[1,2,64]{2,1,0:T(2,128)S(1)}, f32[1,2,64]{2,1,0:T(2,128)}, u32[]{:S(2)}) copy-start(f32[1,2,64]{2,1,0:T(2,128)} %wavelet.1) | copy-start | bytes 1540
  0.7 7.8 %copy-start.6 = (s32[1,64]{1,0:T(1,128)S(1)}, s32[1,64]{1,0:T(1,128)}, u32[]{:S(2)}) copy-start(s32[1,64]{1,0:T(1,128)} %src_cell.1) | copy-start | bytes 772
  0.7 7.8 %copy-start.7 = (s32[1,64]{1,0:T(1,128)S(1)}, s32[1,64]{1,0:T(1,128)}, u32[]{:S(2)}) copy-start(s32[1,64]{1,0:T(1,128)} %src_sign.1) | copy-start | bytes 772
  0.7 7.8 %copy-start.8 = (bf16[256,256]{1,0:T(8,128)(2,1)S(1)}, bf16[256,256]{1,0:T(8,128)(2,1)}, u32[]{:S(2)}) copy-start(bf16[256,256]{1,0:T(8,128)(2,1)} %constant.16.clone.band_y) | copy-start | bytes 393220
  0.7 7.8 %copy-start.9 = (bf16[256,128]{1,0:T(8,128)(2,1)S(1)}, bf16[256,128]{1,0:T(8,128)(2,1)}, u32[]{:S(2)}) copy-start(bf16[256,128]{1,0:T(8,128)(2,1)} %constant.17.clone.band_z) | copy-start | bytes 196612
  3.7 26.8 %collective-permute-start = (f32[2,4,256,128]{3,2,1,0:T(8,128)}, f32[2,4,256,128]{3,2,1,0:T(8,128)}, u32[]{:S(2)}, u32[]{:S(2)}) collective-permute-start(f32[2,4,256,128]{3,2,1,0:T(8,128)} %get-tuple-element.54), channel_id=1, source_target_pairs={{0,4},{8,12},{4,0},{12,8},{1,5},{9,13},{5,1},{13,9},{2,6},{10,14},... | collective-permute-start | bytes 3145736 | tf_op jit(solution)/shard_map/ppermute | solution.py:876
  6.8 23.8 %collective-permute-start.1 = (f32[2,4,256,128]{3,2,1,0:T(8,128)}, f32[2,4,256,128]{3,2,1,0:T(8,128)}, u32[]{:S(2)}, u32[]{:S(2)}) collective-permute-start(f32[2,4,256,128]{3,2,1,0:T(8,128)} %get-tuple-element.55), channel_id=1, source_target_pairs={{4,8},{8,4},{5,9},{9,5},{6,10},{10,6},{7,11},{11,7},{20,24},{24,20... | collective-permute-start | bytes 3145736 | tf_op jit(solution)/shard_map/ppermute | solution.py:876
  28.6 18.6 %collective-permute-start.6 = (f32[8,64,128]{2,1,0:T(8,128)}, f32[8,64,128]{2,1,0:T(8,128)}, u32[]{:S(2)}, u32[]{:S(2)}) collective-permute-start(f32[8,64,128]{2,1,0:T(8,128)} %get-tuple-element.71), channel_id=1, source_target_pairs={{0,1},{1,0},{2,3},{3,2},{4,5},{5,4},{6,7},{7,6},{8,9},{9,8},{10,11... | collective-permute-start | bytes 786440 | tf_op jit(solution)/shard_map/ppermute | solution.py:881
  28.7 18.6 %collective-permute-start.7 = (f32[8,64,128]{2,1,0:T(8,128)}, f32[8,64,128]{2,1,0:T(8,128)}, u32[]{:S(2)}, u32[]{:S(2)}) collective-permute-start(f32[8,64,128]{2,1,0:T(8,128)} %get-tuple-element.72), channel_id=1, source_target_pairs={{0,2},{1,3},{2,0},{3,1},{4,6},{5,7},{6,4},{7,5},{8,10},{9,11},{10,... | collective-permute-start | bytes 786440 | tf_op jit(solution)/shard_map/ppermute | solution.py:881
  30.3 17.0 %collective-permute-start.8 = (f32[8,64,128]{2,1,0:T(8,128)}, f32[8,64,128]{2,1,0:T(8,128)}, u32[]{:S(2)}, u32[]{:S(2)}) collective-permute-start(f32[8,64,128]{2,1,0:T(8,128)} %get-tuple-element.73), channel_id=1, source_target_pairs={{0,3},{1,2},{2,1},{3,0},{4,7},{5,6},{6,5},{7,4},{8,11},{9,10},{10,... | collective-permute-start | bytes 786440 | tf_op jit(solution)/shard_map/ppermute | solution.py:881
  34.2 27.4 %collective-permute-start.2 = (f32[2,4,256,128]{3,2,1,0:T(8,128)}, f32[2,4,256,128]{3,2,1,0:T(8,128)}, u32[]{:S(2)}, u32[]{:S(2)}) collective-permute-start(f32[2,4,256,128]{3,2,1,0:T(8,128)} %get-tuple-element.64), channel_id=1, source_target_pairs={{0,4},{8,12},{4,0},{12,8},{1,5},{9,13},{5,1},{13,9},{2,6},{10,14},... | collective-permute-start | bytes 3145736 | tf_op jit(solution)/shard_map/ppermute | solution.py:876
  38.7 22.9 %collective-permute-start.3 = (f32[2,4,256,128]{3,2,1,0:T(8,128)}, f32[2,4,256,128]{3,2,1,0:T(8,128)}, u32[]{:S(2)}, u32[]{:S(2)}) collective-permute-start(f32[2,4,256,128]{3,2,1,0:T(8,128)} %get-tuple-element.65), channel_id=1, source_target_pairs={{4,8},{8,4},{5,9},{9,5},{6,10},{10,6},{7,11},{11,7},{20,24},{24,20... | collective-permute-start | bytes 3145736 | tf_op jit(solution)/shard_map/ppermute | solution.py:876
  48.5 16.0 %collective-permute-start.9 = (f32[8,64,128]{2,1,0:T(8,128)}, f32[8,64,128]{2,1,0:T(8,128)}, u32[]{:S(2)}, u32[]{:S(2)}) collective-permute-start(f32[8,64,128]{2,1,0:T(8,128)} %get-tuple-element.80), channel_id=1, source_target_pairs={{0,1},{1,0},{2,3},{3,2},{4,5},{5,4},{6,7},{7,6},{8,9},{9,8},{10,11... | collective-permute-start | bytes 786440 | tf_op jit(solution)/shard_map/ppermute | solution.py:881
  48.5 16.0 %collective-permute-start.10 = (f32[8,64,128]{2,1,0:T(8,128)}, f32[8,64,128]{2,1,0:T(8,128)}, u32[]{:S(2)}, u32[]{:S(2)}) collective-permute-start(f32[8,64,128]{2,1,0:T(8,128)} %get-tuple-element.81), channel_id=1, source_target_pairs={{0,2},{1,3},{2,0},{3,1},{4,6},{5,7},{6,4},{7,5},{8,10},{9,11},{10,... | collective-permute-start | bytes 786440 | tf_op jit(solution)/shard_map/ppermute | solution.py:881
  50.1 14.4 %collective-permute-start.11 = (f32[8,64,128]{2,1,0:T(8,128)}, f32[8,64,128]{2,1,0:T(8,128)}, u32[]{:S(2)}, u32[]{:S(2)}) collective-permute-start(f32[8,64,128]{2,1,0:T(8,128)} %get-tuple-element.82), channel_id=1, source_target_pairs={{0,3},{1,2},{2,1},{3,0},{4,7},{5,6},{6,5},{7,4},{8,11},{9,10},{10,... | collective-permute-start | bytes 786440 | tf_op jit(solution)/shard_map/ppermute | solution.py:881
  61.6 2.9 %copy-start.10 = (bf16[128,128]{1,0:T(8,128)(2,1)S(1)}, bf16[128,128]{1,0:T(8,128)(2,1)}, u32[]{:S(2)}) copy-start(bf16[128,128]{1,0:T(8,128)(2,1)} %constant.19.clone.z_low.refs_6_) | copy-start | bytes 98308
  61.6 2.9 %copy-start.11 = (bf16[128,128]{1,0:T(8,128)(2,1)S(1)}, bf16[128,128]{1,0:T(8,128)(2,1)}, u32[]{:S(2)}) copy-start(bf16[128,128]{1,0:T(8,128)(2,1)} %constant.18.clone.z_high.refs_5_) | copy-start | bytes 98308
  64.5 14.3 %collective-permute-start.4 = (f32[8,2,64,128]{3,2,1,0:T(8,128)}, f32[8,2,64,128]{3,2,1,0:T(8,128)}, u32[]{:S(2)}, u32[]{:S(2)}) collective-permute-start(f32[8,2,64,128]{3,2,1,0:T(8,128)} %get-tuple-element.67), channel_id=1, source_target_pairs={{0,1},{1,0},{2,3},{3,2},{4,5},{5,4},{6,7},{7,6},{8,9},{9,8},{10,11... | collective-permute-start | bytes 1572872 | tf_op jit(solution)/shard_map/ppermute | solution.py:881
  67.6 16.5 %collective-permute-start.12 = (f32[8,32,128]{2,1,0:T(8,128)}, f32[8,32,128]{2,1,0:T(8,128)}, u32[]{:S(2)}, u32[]{:S(2)}) collective-permute-start(f32[8,32,128]{2,1,0:T(8,128)} %get-tuple-element.84), channel_id=1, source_target_pairs={{0,0},{1,4},{2,8},{3,12},{4,1},{5,5},{6,9},{7,13},{8,2},{9,6},{10,... | collective-permute-start | bytes 393224 | tf_op jit(solution)/shard_map/ppermute | solution.py:898
  69.8 14.3 %collective-permute-start.13 = (f32[8,32,128]{2,1,0:T(8,128)}, f32[8,32,128]{2,1,0:T(8,128)}, u32[]{:S(2)}, u32[]{:S(2)}) collective-permute-start(f32[8,32,128]{2,1,0:T(8,128)} %get-tuple-element.85), channel_id=1, source_target_pairs={{0,4},{1,8},{2,12},{3,0},{4,5},{5,9},{6,13},{7,1},{8,6},{9,10},{10... | collective-permute-start | bytes 393224 | tf_op jit(solution)/shard_map/ppermute | solution.py:898
  73.3 13.7 %collective-permute-start.14 = (f32[8,32,128]{2,1,0:T(8,128)}, f32[8,32,128]{2,1,0:T(8,128)}, u32[]{:S(2)}, u32[]{:S(2)}) collective-permute-start(f32[8,32,128]{2,1,0:T(8,128)} %get-tuple-element.86), channel_id=1, source_target_pairs={{0,8},{1,12},{2,0},{3,4},{4,9},{5,13},{6,1},{7,5},{8,10},{9,14},{1... | collective-permute-start | bytes 393224 | tf_op jit(solution)/shard_map/ppermute | solution.py:898
  76.8 10.8 %collective-permute-start.15 = (f32[8,32,128]{2,1,0:T(8,128)}, f32[8,32,128]{2,1,0:T(8,128)}, u32[]{:S(2)}, u32[]{:S(2)}) collective-permute-start(f32[8,32,128]{2,1,0:T(8,128)} %get-tuple-element.87), channel_id=1, source_target_pairs={{0,12},{1,0},{2,4},{3,8},{4,13},{5,1},{6,5},{7,9},{8,14},{9,2},{10... | collective-permute-start | bytes 393224 | tf_op jit(solution)/shard_map/ppermute | solution.py:898
  78.8 11.1 %copy-start = (bf16[256,256]{1,0:T(8,128)(2,1)S(1)}, bf16[256,256]{1,0:T(8,128)(2,1)}, u32[]{:S(2)}) copy-start(bf16[256,256]{1,0:T(8,128)(2,1)} %constant.21.clone.refs_5_) | copy-start | bytes 393220
  78.8 11.1 %copy-start.1 = (bf16[256,256]{1,0:T(8,128)(2,1)S(1)}, bf16[256,256]{1,0:T(8,128)(2,1)}, u32[]{:S(2)}) copy-start(bf16[256,256]{1,0:T(8,128)(2,1)} %constant.20.clone.refs_4_) | copy-start | bytes 393220
  81.9 10.2 %collective-permute-start.16 = (f32[8,32,128]{2,1,0:T(8,128)}, f32[8,32,128]{2,1,0:T(8,128)}, u32[]{:S(2)}, u32[]{:S(2)}) collective-permute-start(f32[8,32,128]{2,1,0:T(8,128)} %get-tuple-element.88), channel_id=1, source_target_pairs={{0,0},{1,4},{2,8},{3,12},{4,1},{5,5},{6,9},{7,13},{8,2},{9,6},{10,... | collective-permute-start | bytes 393224 | tf_op jit(solution)/shard_map/ppermute | solution.py:898
  84.1 8.1 %collective-permute-start.17 = (f32[8,32,128]{2,1,0:T(8,128)}, f32[8,32,128]{2,1,0:T(8,128)}, u32[]{:S(2)}, u32[]{:S(2)}) collective-permute-start(f32[8,32,128]{2,1,0:T(8,128)} %get-tuple-element.89), channel_id=1, source_target_pairs={{0,4},{1,8},{2,12},{3,0},{4,5},{5,9},{6,13},{7,1},{8,6},{9,10},{10... | collective-permute-start | bytes 393224 | tf_op jit(solution)/shard_map/ppermute | solution.py:898
  84.1 10.1 %collective-permute-start.18 = (f32[8,32,128]{2,1,0:T(8,128)}, f32[8,32,128]{2,1,0:T(8,128)}, u32[]{:S(2)}, u32[]{:S(2)}) collective-permute-start(f32[8,32,128]{2,1,0:T(8,128)} %get-tuple-element.90), channel_id=1, source_target_pairs={{0,8},{1,12},{2,0},{3,4},{4,9},{5,13},{6,1},{7,5},{8,10},{9,14},{1... | collective-permute-start | bytes 393224 | tf_op jit(solution)/shard_map/ppermute | solution.py:898
  87.0 7.2 %collective-permute-start.19 = (f32[8,32,128]{2,1,0:T(8,128)}, f32[8,32,128]{2,1,0:T(8,128)}, u32[]{:S(2)}, u32[]{:S(2)}) collective-permute-start(f32[8,32,128]{2,1,0:T(8,128)} %get-tuple-element.91), channel_id=1, source_target_pairs={{0,12},{1,0},{2,4},{3,8},{4,13},{5,1},{6,5},{7,9},{8,14},{9,2},{10... | collective-permute-start | bytes 393224 | tf_op jit(solution)/shard_map/ppermute | solution.py:898
  87.6 14.9 %collective-permute-start.5 = (f32[8,64,128]{2,1,0:T(8,128)}, f32[8,64,128]{2,1,0:T(8,128)}, u32[]{:S(2)}, u32[]{:S(2)}) collective-permute-start(f32[8,64,128]{2,1,0:T(8,128)} %get-tuple-element.69), channel_id=1, source_target_pairs={{0,2},{1,3},{2,0},{3,1},{4,6},{5,7},{6,4},{7,5},{8,10},{9,11},{10,... | collective-permute-start | bytes 786440 | tf_op jit(solution)/shard_map/ppermute | solution.py:881
  89.9 4.3 %copy-start.2 = (f32[5,96]{1,0:T(8,128)S(1)}, f32[5,96]{1,0:T(8,128)}, u32[]{:S(2)}) copy-start(f32[5,96]{1,0:T(8,128)} %constant.22.clone.scan) | copy-start | bytes 5764
  92.1 13.6 %copy-start.3 = (f32[4,4]{1,0:T(4,128)S(1)}, f32[4,4]{1,0:T(4,128)}, u32[]{:S(2)}) copy-start(f32[4,4]{1,0:T(4,128)} %constant.23.clone.carry) | copy-start | bytes 196
  96.9 7.3 %collective-permute-start.20 = (f32[32,256]{1,0:T(8,128)S(1)}, f32[32,256]{1,0:T(8,128)S(1)}, u32[]{:S(2)}, u32[]{:S(2)}) collective-permute-start(f32[32,256]{1,0:T(8,128)S(1)} %get-tuple-element.93), channel_id=1, source_target_pairs={{0,1},{1,0},{2,3},{3,2},{4,5},{5,4},{6,7},{7,6},{8,9},{9,8},{10,11... | collective-permute-start | bytes 98312 | tf_op jit(solution)/shard_map/ppermute | solution.py:881
  100.1 4.3 %collective-permute-start.21 = (f32[32,256]{1,0:T(8,128)S(1)}, f32[32,256]{1,0:T(8,128)S(1)}, u32[]{:S(2)}, u32[]{:S(2)}) collective-permute-start(f32[32,256]{1,0:T(8,128)S(1)} %get-tuple-element.94), channel_id=1, source_target_pairs={{0,2},{1,3},{2,0},{3,1},{4,6},{5,7},{6,4},{7,5},{8,10},{9,11},{10,... | collective-permute-start | bytes 98312 | tf_op jit(solution)/shard_map/ppermute | solution.py:881
  102.4 3.3 %collective-permute-start.22 = (f32[32,256]{1,0:T(8,128)S(1)}, f32[32,256]{1,0:T(8,128)S(1)}, u32[]{:S(2)}, u32[]{:S(2)}) collective-permute-start(f32[32,256]{1,0:T(8,128)S(1)} %get-tuple-element.95), channel_id=1, source_target_pairs={{0,3},{1,2},{2,1},{3,0},{4,7},{5,6},{6,5},{7,4},{8,11},{9,10},{10,... | collective-permute-start | bytes 98312 | tf_op jit(solution)/shard_map/ppermute | solution.py:881

commit v4 on v3

--- a/solution.py
+++ b/solution.py
@@ -276,7 +276,7 @@
         gt_buf[i] = (first * acc_buf[p] + a_mid[p + REACH] * accel).reshape(blocks, ny // blocks, nz)
         return 0
 
-    lax.fori_loop(0, rows - 4 * REACH, inner, 0)
+    lax.fori_loop(0, rows - 4 * REACH, inner, 0, unroll=2)
     wait_all(put_blocks(Copies(term_sems), gt_buf, slice(None), lax.axis_index("shot"), terms_out))
 
 
@@ -380,16 +380,23 @@
 
 
 def correct_kernel(
-    c_buf, acc_in, next_in, mid_in, base_in, halo0, halo1, acc_buf, f_next, a_mid, a_base, edge0, edge1
+    c_buf, acc_in, next_in, mid_in, base_in, halo0, halo1, acc_buf, f_next, a_mid, a_base, edge0, edge1,
+    halo_buf, edge_buf, sems,
 ):
-    edges = (edge0, edge1)
     rows, ny, _ = c_buf.shape
-
-    def strip(part):
+    copies = Copies(sems)
+    step = max(STRIP, ny // 4)
+    parts = [slice(low, low + step) for low in range(0, ny, step)]
+    loads = [
+        [copies.start(halo.at[:, :, part], halo_buf.at[s, :, :, part]) for s, halo in enumerate((halo0, halo1))]
+        for part in parts
+    ]
+
+    def strip(i, _):
+        part = pl.ds(pl.multiple_of(i * STRIP, STRIP), STRIP)
         for s, (base, upper) in enumerate(sides(rows)):
-            halo = (halo0, halo1)[s]
-            forward = halo_sums(lambda h, halo=halo: halo[0, h, part], upper)
-            adjoint = halo_sums(lambda h, halo=halo: halo[1, h, part], upper)
+            forward = halo_sums(lambda h, s=s: halo_buf[s, 0, h, part], upper)
+            adjoint = halo_sums(lambda h, s=s: halo_buf[s, 1, h, part], upper)
             for q in range(REACH):
                 place = jnp.where(upper, q, REACH - 1 - q)
                 here = base + place
@@ -398,14 +405,21 @@
                 acc_buf[here, part] = acc_in[here, part] + change
                 value = next_in[here + REACH, part] + change
                 f_next[here + REACH, part] = value
-                edges[s][0, place, part] = value
+                edge_buf[s, 0, place, part] = value
                 change = c * adjoint[q]
                 value = mid_in[here + REACH, part] + change
                 a_mid[here + REACH, part] = value
-                edges[s][1, place, part] = value
+                edge_buf[s, 1, place, part] = value
                 a_base[here, part] = base_in[here, part] + 2.0 * change
-
-    strips(ny, strip)
+        return 0
+
+    stores = []
+    for part, group in zip(parts, loads, strict=True):
+        wait_all(group)
+        lax.fori_loop(part.start // STRIP, part.stop // STRIP, strip, 0)
+        for s, edge in enumerate((edge0, edge1)):
+            stores.append(copies.start(edge_buf.at[s, :, :, part], edge.at[:, :, part]))
+    wait_all(stores)
 
 
 def correct(c, accel, nxt, mid, a_base, halos):
@@ -414,8 +428,12 @@
     return pl.pallas_call(
         correct_kernel,
         out_shape=tuple(held(*array.shape) for array in (accel, nxt, mid, a_base)) + (both, both),
-        in_specs=[VMEM] * 7,
-        out_specs=(VMEM,) * 6,
+        in_specs=[VMEM] * 5 + [ANY] * 2,
+        out_specs=(VMEM,) * 4 + (ANY,) * 2,
+        scratch_shapes=[
+            held(2, 2, REACH, ny, nz), held(2, 2, REACH, ny, nz),
+            pltpu.SemaphoreType.DMA((4 * len(range(0, ny, max(STRIP, ny // 4))),)),
+        ],
         input_output_aliases={1: 0, 2: 1, 3: 2, 4: 3},
         compiler_params=cheap(8),
         cost_estimate=COST,
@@ -442,7 +460,7 @@
     def inner(i, _):
         return plane(jnp.where(i < REACH, i + REACH, i + rows - 3 * REACH), 0)
 
-    lax.fori_loop(0, 2 * REACH, inner, 0)
+    lax.fori_loop(0, 2 * REACH, inner, 0, unroll=2)
     stores = []
     for i, low in enumerate((REACH, rows - 2 * REACH)):
         outs = [out.at[pl.ds(i * REACH, REACH)] for out in terms_out]
@@ -460,7 +478,7 @@
         edge_out[s, q] = gt_buf[p].reshape(ny, nz)
         return 0
 
-    lax.fori_loop(0, 2 * REACH, outer, 0)
+    lax.fori_loop(0, 2 * REACH, outer, 0, unroll=2)
     wait_all(stores)
 
 
@@ -503,27 +521,40 @@
     return outs[0], outs[1:]
 
 
-def finish_kernel(edge, by_f, by_a, halo0, halo1, near_out, keep_out):
+def finish_kernel(edge, by_f, by_a, halo0, halo1, near_out, keep_out, halo_buf, near_buf, sems):
     _, blocks, yb, _ = near_out.shape
+    copies = Copies(sems)
     bit = lax.rem(lax.axis_index("shot"), 2)
     width = math.gcd(yb, STRIP)
-
-    def strip(i, _):
-        for out, mine in ((near_out, 1 - bit), (keep_out, bit)):
-            for j in range(blocks):
-                inside = pl.ds(pl.multiple_of(i * width, width), width)
-                part = pl.ds(pl.multiple_of((2 * j + mine) * yb + i * width, width), width)
-                for s, (_, upper) in enumerate(sides(2 * REACH)):
-                    halo = (halo0, halo1)[s]
-                    forward = halo_sums(lambda h, halo=halo: halo[0, h, part], upper)
-                    adjoint = halo_sums(lambda h, halo=halo: halo[1, h, part], upper)
-                    for q in range(REACH):
-                        place = jnp.where(upper, q, REACH - 1 - q)
-                        total = edge[s, place, part] + by_f[s, place, part] * forward[q]
-                        out[s * REACH + place, j, inside] = total + by_a[s, place, part] * adjoint[q]
-        return 0
-
-    lax.fori_loop(0, yb // width, strip, 0)
+    jobs = []
+    for out, mine in ((near_buf, 1 - bit), (keep_out, bit)):
+        for j in range(blocks):
+            low = pl.multiple_of((2 * j + mine) * yb, yb)
+            here = pl.ds(low, yb)
+            loads = [
+                copies.start(halo.at[:, :, here], halo_buf.at[s, :, :, here]) for s, halo in enumerate((halo0, halo1))
+            ]
+            jobs.append((out, j, low, loads))
+    stores = []
+    for out, j, low, loads in jobs:
+        wait_all(loads)
+
+        def strip(i, _, out=out, j=j, low=low):
+            inside = pl.ds(pl.multiple_of(i * width, width), width)
+            part = pl.ds(pl.multiple_of(low + i * width, width), width)
+            for s, (_, upper) in enumerate(sides(2 * REACH)):
+                forward = halo_sums(lambda h, s=s: halo_buf[s, 0, h, part], upper)
+                adjoint = halo_sums(lambda h, s=s: halo_buf[s, 1, h, part], upper)
+                for q in range(REACH):
+                    place = jnp.where(upper, q, REACH - 1 - q)
+                    total = edge[s, place, part] + by_f[s, place, part] * forward[q]
+                    out[s * REACH + place, j, inside] = total + by_a[s, place, part] * adjoint[q]
+            return 0
+
+        lax.fori_loop(0, yb // width, strip, 0)
+        if out is near_buf:
+            stores.append(copies.start(near_buf.at[:, j], near_out.at[:, j]))
+    wait_all(stores)
 
 
 def finish(edge, by_f, by_a, halos, shots):
@@ -532,8 +563,13 @@
     return pl.pallas_call(
         finish_kernel,
         out_shape=(half, half),
-        in_specs=[VMEM] * 5,
-        out_specs=(VMEM,) * 2,
+        in_specs=[VMEM] * 3 + [ANY] * 2,
+        out_specs=(ANY, VMEM),
+        scratch_shapes=[
+            held(2, 2, reach, ny, nz),
+            held(*half.shape),
+            pltpu.SemaphoreType.DMA((shots * 2 + shots // 2,)),
+        ],
         compiler_params=cheap(16),
         cost_estimate=LONG,
         name="finish",

time: 108 us -> 106 us (0.981)
  Pallas kernels: 52.3 us -> 49.9 us
  transfers between devices with their start and end apart: 23 -> 23, of which waited for: 4 -> 4; matrix products, arithmetic and copies ran while one was open for 0% -> 0% of each run, Pallas kernels for 44% -> 43%
where the time goes in v4:
time: 106 us
  Pallas kernels  49.9 us (47%)
  starting transfers between devices  39.7 us (37%)
  waiting for transfers between devices  15.3 us (14%)
    pallas_call x1, Pallas kernels, step_one(): pl.pallas_call(step_one_kernel, out_shape=tuple((held(*shape) for shape i...  20 us
    ppermute x8, starting transfers between devices, spread(): out.append(lax.ppermute(piece, ('mp', 'shot'), pairs))  17 us
    ppermute x11, starting transfers between devices, flip(): got = lax.ppermute(value, 'shot', [(i, i ^ bit) for i in range(count)])  11.7 us
    ppermute x4, waiting for transfers between devices, swap(): lax.ppermute(v, 'mp', neighbours(count, start))  11.6 us
    ppermute x4, starting transfers between devices, swap(): lax.ppermute(v, 'mp', neighbours(count, start))  11 us
    pallas_call x1, Pallas kernels, step_two(): pl.pallas_call(functools.partial(step_two_kernel, len(after)), out_shape=...  6.26 us
    pallas_call x1, Pallas kernels, depth_edge(): pl.pallas_call(functools.partial(depth_edge_kernel, pieces), out_shape=(t...  3.16 us
    pallas_call x1, Pallas kernels, depth(): pl.pallas_call(functools.partial(depth_kernel, layout, offsets, pieces),...  3.13 us
  transfers between devices with their start and end apart: 23, of which 4 were waited for; matrix products, arithmetic and copies ran while one was open for 0% of the time, Pallas kernels for 43%

profile of v4, /device:TPU:0, one launch (start us, length us, event | category | flops | bytes accessed | tf_op | source)
XLA Modules:
  0.0 106.0 jit_solution(9831200239120027960)
XLA Ops:
  0.7 0.0 copy-start.8
  0.7 0.0 copy-start.9
  0.7 3.0 %pick.1 = (f32[2,4,256,128]{3,2,1,0:T(8,128)}, f32[2,4,256,128]{3,2,1,0:T(8,128)}) custom-call(f32[24,256,128]{2,1,0:T(8,128)} %bitcast.13, f32[24,256,128]{2,1,0:T(8,128)} %bitcast.15), custom_call_target="tpu_custom_call" | custom-call | flops 1000 | bytes 1000 | tf_op jit(solution)/shard_map/pick/pallas_call | solution.py:370
  3.7 3.1 %collective-permute-start = (f32[2,4,256,128]{3,2,1,0:T(8,128)}, f32[2,4,256,128]{3,2,1,0:T(8,128)}, u32[]{:S(2)}, u32[]{:S(2)}) collective-permute-start(f32[2,4,256,128]{3,2,1,0:T(8,128)} %get-tuple-element.54), channel_id=1, source_target_pairs={{0,4},{8,12},{4,0},{12,8},{1,5},{9,13},{5,1},{13,9},{2,6},{10,14},... | collective-permute-start | bytes 3145736 | tf_op jit(solution)/shard_map/ppermute | solution.py:912
  6.8 1.6 %collective-permute-start.1 = (f32[2,4,256,128]{3,2,1,0:T(8,128)}, f32[2,4,256,128]{3,2,1,0:T(8,128)}, u32[]{:S(2)}, u32[]{:S(2)}) collective-permute-start(f32[2,4,256,128]{3,2,1,0:T(8,128)} %get-tuple-element.55), channel_id=1, source_target_pairs={{4,8},{8,4},{5,9},{9,5},{6,10},{10,6},{7,11},{11,7},{20,24},{24,20... | collective-permute-start | bytes 3145736 | tf_op jit(solution)/shard_map/ppermute | solution.py:912
  8.5 20.0 %step_one.1 = (f32[24,256,128]{2,1,0:T(8,128)S(1)}, f32[24,256,128]{2,1,0:T(8,128)S(1)}, f32[32,256,128]{2,1,0:T(8,128)S(1)}, f32[32,256,128]{2,1,0:T(8,128)S(1)...) custom-call(s32[1,64]{1,0:T(1,128)S(1)} %copy-done.6, ...), custom_call_target="tpu_custom_call" | custom-call | flops 999999995904 | bytes 1000 | tf_op jit(solution)/shard_map/step_one/pallas_call | solution.py:308
  28.5 0.1 collective-permute-start.6
  28.6 1.6 %collective-permute-start.7 = (f32[8,64,128]{2,1,0:T(8,128)}, f32[8,64,128]{2,1,0:T(8,128)}, u32[]{:S(2)}, u32[]{:S(2)}) collective-permute-start(f32[8,64,128]{2,1,0:T(8,128)} %get-tuple-element.72), channel_id=1, source_target_pairs={{0,2},{1,3},{2,0},{3,1},{4,6},{5,7},{6,4},{7,5},{8,10},{9,11},{10,... | collective-permute-start | bytes 786440 | tf_op jit(solution)/shard_map/ppermute | solution.py:917
  30.1 0.3 collective-permute-start.8
  30.4 0.0 collective-permute-done.halo0
  30.4 0.0 collective-permute-done.1.halo1
  30.4 2.8 %correct.1 = (f32[24,256,128]{2,1,0:T(8,128)S(1)}, f32[32,256,128]{2,1,0:T(8,128)S(1)}, f32[32,256,128]{2,1,0:T(8,128)S(1)}, f32[24,256,128]{2,1,0:T(8,128)S(1)}...) custom-call(f32[24,256,128]{2,1,0:T(8,128)S(1)} %get-tuple-element.4, ...), custom_call_target="tpu_custom_call", output_to_operand_aliasing={{0}: (1, {}), {1}: (2, {}), {2}: (3, {}), {3}: (4, {})} | custom-call | flops 1000 | bytes 1000 | tf_op jit(solution)/shard_map/correct/pallas_call | solution.py:428
  33.2 4.7 %collective-permute-start.2 = (f32[2,4,256,128]{3,2,1,0:T(8,128)}, f32[2,4,256,128]{3,2,1,0:T(8,128)}, u32[]{:S(2)}, u32[]{:S(2)}) collective-permute-start(f32[2,4,256,128]{3,2,1,0:T(8,128)} %get-tuple-element.64), channel_id=1, source_target_pairs={{0,4},{8,12},{4,0},{12,8},{1,5},{9,13},{5,1},{13,9},{2,6},{10,14},... | collective-permute-start | bytes 3145736 | tf_op jit(solution)/shard_map/ppermute | solution.py:912
  37.9 1.6 %collective-permute-start.3 = (f32[2,4,256,128]{3,2,1,0:T(8,128)}, f32[2,4,256,128]{3,2,1,0:T(8,128)}, u32[]{:S(2)}, u32[]{:S(2)}) collective-permute-start(f32[2,4,256,128]{3,2,1,0:T(8,128)} %get-tuple-element.65), channel_id=1, source_target_pairs={{4,8},{8,4},{5,9},{9,5},{6,10},{10,6},{7,11},{11,7},{20,24},{24,20... | collective-permute-start | bytes 3145736 | tf_op jit(solution)/shard_map/ppermute | solution.py:912
  39.5 6.3 %step_two.1 = (f32[2,4,256,128]{3,2,1,0:T(8,128)S(1)}, f32[2,4,256,128]{3,2,1,0:T(8,128)S(1)}, f32[2,4,256,128]{3,2,1,0:T(8,128)S(1)}, f32[8,64,128]{2,1,0:T(8,1...) custom-call(f32[24,256,128]{2,1,0:T(8,128)S(1)} %get-tuple-element.49.c_buf, ...), custom_call_target="tpu_custom_call" | custom-call | flops 999999995904 | bytes 1000 | tf_op jit(solution)/shard_map/step_two/pallas_call | solution.py:489
  45.8 0.0 collective-permute-done.7.refs_2_
  45.8 0.0 collective-permute-done.8.refs_3_
  45.8 1.2 %add_up.1 = (f32[8,64,128]{2,1,0:T(8,128)S(1)}, f32[8,64,128]{2,1,0:T(8,128)S(1)}, f32[8,64,128]{2,1,0:T(8,128)}, f32[8,64,128]{2,1,0:T(8,128)}, f32[8,64,128]{2,1,0:T(8,128)}) custom-call(f32[8,64,128]{2,1,0:T(8,128)S(1)} %get-tuple-element.70.refs_0_, ...), custom_call_target="tpu_custom_call", output_to_operand_aliasing={{1}: (4, {}), {2}: (5, {}), {3}: (6, {}), {4}: (7, {})} | custom-call | flops 1000 | bytes 1000 | tf_op jit(solution)/shard_map/add_up/pallas_call | solution.py:511
  47.0 0.1 collective-permute-start.9
  47.1 1.6 %collective-permute-start.10 = (f32[8,64,128]{2,1,0:T(8,128)}, f32[8,64,128]{2,1,0:T(8,128)}, u32[]{:S(2)}, u32[]{:S(2)}) collective-permute-start(f32[8,64,128]{2,1,0:T(8,128)} %get-tuple-element.81), channel_id=1, source_target_pairs={{0,2},{1,3},{2,0},{3,1},{4,6},{5,7},{6,4},{7,5},{8,10},{9,11},{10,... | collective-permute-start | bytes 786440 | tf_op jit(solution)/shard_map/ppermute | solution.py:917
  48.6 0.3 collective-permute-start.11
  48.9 11.6 %collective-permute-done.2.halo0 = f32[2,4,256,128]{3,2,1,0:T(8,128)} collective-permute-done((f32[2,4,256,128]{3,2,1,0:T(8,128)}, f32[2,4,256,128]{3,2,1,0:T(8,128)}, u32[]{:S(2)}, u32[]{:S(2)}) %collective-permute-start.2) | collective-permute-done | bytes 1048608 | tf_op jit(solution)/shard_map/ppermute | solution.py:912
  60.5 2.1 %finish.1 = (f32[8,2,64,128]{3,2,1,0:T(8,128)}, f32[8,2,64,128]{3,2,1,0:T(8,128)S(1)}) custom-call(f32[2,4,256,128]{3,2,1,0:T(8,128)S(1)} %get-tuple-element.61.edge, f32[2,4,256,128]{3,2,1,0:T(8,128)S(1)} %get-tuple-element.62.by_f, f32[2,4,256,128]{3,2,1,0:T(8,128)S(1)} %get-tuple-element.63.by_a, f32[2,4,256,128]{3,2,1,0:T(8,128)} %collective-permute-done.2.halo0, ...), custom_call_target="tpu_custom_call" | custom-call | flops 999999995904 | bytes 1000 | tf_op jit(solution)/shard_map/finish/pallas_call | solution.py:563
  62.6 0.1 collective-permute-start.4
  62.7 0.0 collective-permute-done.9.refs_2_
  62.7 0.0 collective-permute-done.11.refs_4_
  62.8 3.1 %depth.1 = (f32[24,64,128]{2,1,0:T(8,128)}, f32[8,32,128]{2,1,0:T(8,128)}, f32[8,32,128]{2,1,0:T(8,128)}, f32[8,32,128]{2,1,0:T(8,128)}, f32[8,32,128]{2,1,0:T(8,128)}) custom-call(f32[8,64,128]{2,1,0:T(8,128)S(1)} %get-tuple-element.78.refs_0_, f32[8,64,128]{2,1,0:T(8,128)S(1)} %get-tuple-element.79.refs_1_, f32[8,64,128]{2,1,0:T(8,128)} %collective-permute-done.9.refs_2_, ...), custom_call_target="tpu_custom_call" | custom-call | flops 999999995904 | bytes 1000 | tf_op jit(solution)/shard_map/depth/pallas_call | solution.py:632
  65.9 2.2 %collective-permute-start.12 = (f32[8,32,128]{2,1,0:T(8,128)}, f32[8,32,128]{2,1,0:T(8,128)}, u32[]{:S(2)}, u32[]{:S(2)}) collective-permute-start(f32[8,32,128]{2,1,0:T(8,128)} %get-tuple-element.84), channel_id=1, source_target_pairs={{0,0},{1,4},{2,8},{3,12},{4,1},{5,5},{6,9},{7,13},{8,2},{9,6},{10,... | collective-permute-start | bytes 393224 | tf_op jit(solution)/shard_map/ppermute | solution.py:934
  68.1 3.4 %collective-permute-start.13 = (f32[8,32,128]{2,1,0:T(8,128)}, f32[8,32,128]{2,1,0:T(8,128)}, u32[]{:S(2)}, u32[]{:S(2)}) collective-permute-start(f32[8,32,128]{2,1,0:T(8,128)} %get-tuple-element.85), channel_id=1, source_target_pairs={{0,4},{1,8},{2,12},{3,0},{4,5},{5,9},{6,13},{7,1},{8,6},{9,10},{10... | collective-permute-start | bytes 393224 | tf_op jit(solution)/shard_map/ppermute | solution.py:934
  71.5 3.8 %collective-permute-start.14 = (f32[8,32,128]{2,1,0:T(8,128)}, f32[8,32,128]{2,1,0:T(8,128)}, u32[]{:S(2)}, u32[]{:S(2)}) collective-permute-start(f32[8,32,128]{2,1,0:T(8,128)} %get-tuple-element.86), channel_id=1, source_target_pairs={{0,8},{1,12},{2,0},{3,4},{4,9},{5,13},{6,1},{7,5},{8,10},{9,14},{1... | collective-permute-start | bytes 393224 | tf_op jit(solution)/shard_map/ppermute | solution.py:934
  75.3 2.0 %collective-permute-start.15 = (f32[8,32,128]{2,1,0:T(8,128)}, f32[8,32,128]{2,1,0:T(8,128)}, u32[]{:S(2)}, u32[]{:S(2)}) collective-permute-start(f32[8,32,128]{2,1,0:T(8,128)} %get-tuple-element.87), channel_id=1, source_target_pairs={{0,12},{1,0},{2,4},{3,8},{4,13},{5,1},{6,5},{7,9},{8,14},{9,2},{10... | collective-permute-start | bytes 393224 | tf_op jit(solution)/shard_map/ppermute | solution.py:934
  77.3 0.0 collective-permute-done.4.near
  77.4 3.2 %depth_edge.1 = (f32[8,64,128]{2,1,0:T(8,128)S(1)}, f32[8,64,128]{2,1,0:T(8,128)}, f32[8,32,128]{2,1,0:T(8,128)}, f32[8,32,128]{2,1,0:T(8,128)}, f32[8,32,128]{2,1,0:T(8,128)}, /*index=5*/f32[8,32,128]{2,1,0:T(8,128)}) custom-call(f32[8,2,64,128]{3,2,1,0:T(8,128)S(1)} %get-tuple-element.66.keep, f32[8,2,64,128]{3,2,1,0:T(8,128)} %collective-permute-done.4.near, ...), custom_call_target="tpu_custom_call" | custom-call | flops 999999995904 | bytes 1000 | tf_op jit(solution)/shard_map/depth_edge/pallas_call | solution.py:677
  80.5 2.2 %collective-permute-start.16 = (f32[8,32,128]{2,1,0:T(8,128)}, f32[8,32,128]{2,1,0:T(8,128)}, u32[]{:S(2)}, u32[]{:S(2)}) collective-permute-start(f32[8,32,128]{2,1,0:T(8,128)} %get-tuple-element.88), channel_id=1, source_target_pairs={{0,0},{1,4},{2,8},{3,12},{4,1},{5,5},{6,9},{7,13},{8,2},{9,6},{10,... | collective-permute-start | bytes 393224 | tf_op jit(solution)/shard_map/ppermute | solution.py:934
  82.7 2.4 %collective-permute-start.18 = (f32[8,32,128]{2,1,0:T(8,128)}, f32[8,32,128]{2,1,0:T(8,128)}, u32[]{:S(2)}, u32[]{:S(2)}) collective-permute-start(f32[8,32,128]{2,1,0:T(8,128)} %get-tuple-element.90), channel_id=1, source_target_pairs={{0,8},{1,12},{2,0},{3,4},{4,9},{5,13},{6,1},{7,5},{8,10},{9,14},{1... | collective-permute-start | bytes 393224 | tf_op jit(solution)/shard_map/ppermute | solution.py:934
  85.1 1.1 collective-permute-start.19
  86.1 2.4 %collective-permute-start.5 = (f32[8,64,128]{2,1,0:T(8,128)}, f32[8,64,128]{2,1,0:T(8,128)}, u32[]{:S(2)}, u32[]{:S(2)}) collective-permute-start(f32[8,64,128]{2,1,0:T(8,128)} %get-tuple-element.69), channel_id=1, source_target_pairs={{0,2},{1,3},{2,0},{3,1},{4,6},{5,7},{6,4},{7,5},{8,10},{9,11},{10,... | collective-permute-start | bytes 786440 | tf_op jit(solution)/shard_map/ppermute | solution.py:917
  88.6 2.3 %gather.1.mains = f32[16,32,256]{2,1,0:T(8,128)S(1)} custom-call(f32[8,32,128]{2,1,0:T(8,128)} %collective-permute-done.12.refs_0_, f32[8,32,128]{2,1,0:T(8,128)} %collective-permute-done.13.refs_1_, f32[8,32,128]{2,1,0:T(8,128)} %collective-permute-done.14.refs_2_, f32[8,32,128]{2,1,0:T(8,128)} %collective-permute-done.15.refs_3_, ...), custom_call_target="tpu_custom_call" | custom-call | flops 999999995904 | bytes 1000 | tf_op jit(solution)/shard_map/gather/pallas_call | solution.py:798
  90.8 0.0 copy-start.3
  90.9 2.2 %collective-permute-done.18.refs_2_ = f32[8,32,128]{2,1,0:T(8,128)} collective-permute-done((f32[8,32,128]{2,1,0:T(8,128)}, f32[8,32,128]{2,1,0:T(8,128)}, u32[]{:S(2)}, u32[]{:S(2)}) %collective-permute-start.18) | collective-permute-done | bytes 131104 | tf_op jit(solution)/shard_map/ppermute | solution.py:934
  93.0 2.7 %scan.3 = (f32[24,32,256]{2,1,0:T(8,128)S(1)}, f32[32,256]{1,0:T(8,128)S(1)}, f32[32,256]{1,0:T(8,128)S(1)}, f32[32,256]{1,0:T(8,128)S(1)}) custom-call(f32[5,96]{1,0:T(8,128)S(1)} %copy-done.2, f32[16,32,256]{2,1,0:T(8,128)S(1)} %gather.1.mains, f32[8,32,128]{2,1,0:T(8,128)} %collective-permute-done.16.refs_0_, ...), custom_call_target="tpu_custom_call" | custom-call | flops 1000 | bytes 1000 | tf_op jit(solution)/shard_map/scan/pallas_call | solution.py:857
  95.7 2.8 %collective-permute-start.20 = (f32[32,256]{1,0:T(8,128)S(1)}, f32[32,256]{1,0:T(8,128)S(1)}, u32[]{:S(2)}, u32[]{:S(2)}) collective-permute-start(f32[32,256]{1,0:T(8,128)S(1)} %get-tuple-element.93), channel_id=1, source_target_pairs={{0,1},{1,0},{2,3},{3,2},{4,5},{5,4},{6,7},{7,6},{8,9},{9,8},{10,11... | collective-permute-start | bytes 98312 | tf_op jit(solution)/shard_map/ppermute | solution.py:917
  98.5 2.5 %collective-permute-start.21 = (f32[32,256]{1,0:T(8,128)S(1)}, f32[32,256]{1,0:T(8,128)S(1)}, u32[]{:S(2)}, u32[]{:S(2)}) collective-permute-start(f32[32,256]{1,0:T(8,128)S(1)} %get-tuple-element.94), channel_id=1, source_target_pairs={{0,2},{1,3},{2,0},{3,1},{4,6},{5,7},{6,4},{7,5},{8,10},{9,11},{10,... | collective-permute-start | bytes 98312 | tf_op jit(solution)/shard_map/ppermute | solution.py:917
  101.0 0.1 collective-permute-start.22
  101.0 1.7 %raw_edge.1.refs_3_ = f32[24,64,128]{2,1,0:T(8,128)} custom-call(f32[8,64,128]{2,1,0:T(8,128)S(1)} %get-tuple-element.68.refs_0_, f32[8,64,128]{2,1,0:T(8,128)} %collective-permute-done.5.refs_1_, f32[24,64,128]{2,1,0:T(8,128)} %get-tuple-element.83.refs_2_), custom_call_target="tpu_custom_call", output_to_operand_aliasing={{}: (2, {})} | custom-call | flops 1000 | bytes 1000 | tf_op jit(solution)/shard_map/raw_edge/pallas_call | solution.py:707
  102.8 0.2 collective-permute-done.21.refs_1_
  103.0 1.4 %collective-permute-done.22.refs_2_ = f32[32,256]{1,0:T(8,128)S(1)} collective-permute-done((f32[32,256]{1,0:T(8,128)S(1)}, f32[32,256]{1,0:T(8,128)S(1)}, u32[]{:S(2)}, u32[]{:S(2)}) %collective-permute-start.22) | collective-permute-done | bytes 32800 | tf_op jit(solution)/shard_map/ppermute | solution.py:917
  104.3 1.6 %join.1 = f32[24,32,256]{2,1,0:T(8,128)} custom-call(f32[5,96]{1,0:T(8,128)S(1)} %copy-done.2, f32[4,4]{1,0:T(4,128)S(1)} %copy-done.3, f32[24,32,256]{2,1,0:T(8,128)S(1)} %get-tuple-element.92.part, f32[32,256]{1,0:T(8,128)S(1)} %collective-permute-done.20.refs_0_, f32[32,256]{1,0:T(8,128)S(1)} %collective-permute-done.21.refs_1_, ...), custom_call_target="tpu_custom_call" | custom-call | flops 1000 | bytes 1000 | tf_op jit(solution)/shard_map/join/pallas_call | solution.py:894
  (37 shorter events, 0.1 us)
Async XLA Ops:
  0.6 7.8 %copy-start.12 = (f32[1,2,2048]{2,1,0:T(2,128)S(1)}, f32[1,2,2048]{2,1,0:T(2,128)}, u32[]{:S(2)}) copy-start(f32[1,2,2048]{2,1,0:T(2,128)} %param.27) | copy-start | bytes 49156
  0.6 7.8 %copy-start.4 = (s32[2048]{0:T(1024)S(1)}, s32[2048]{0:T(1024)}, u32[]{:S(2)}) copy-start(s32[2048]{0:T(1024)} %param.26) | copy-start | bytes 24580
  0.7 7.8 %copy-start.5 = (f32[1,2,64]{2,1,0:T(2,128)S(1)}, f32[1,2,64]{2,1,0:T(2,128)}, u32[]{:S(2)}) copy-start(f32[1,2,64]{2,1,0:T(2,128)} %wavelet.1) | copy-start | bytes 1540
  0.7 7.8 %copy-start.6 = (s32[1,64]{1,0:T(1,128)S(1)}, s32[1,64]{1,0:T(1,128)}, u32[]{:S(2)}) copy-start(s32[1,64]{1,0:T(1,128)} %src_cell.1) | copy-start | bytes 772
  0.7 7.8 %copy-start.7 = (s32[1,64]{1,0:T(1,128)S(1)}, s32[1,64]{1,0:T(1,128)}, u32[]{:S(2)}) copy-start(s32[1,64]{1,0:T(1,128)} %src_sign.1) | copy-start | bytes 772
  0.7 7.8 %copy-start.8 = (bf16[256,256]{1,0:T(8,128)(2,1)S(1)}, bf16[256,256]{1,0:T(8,128)(2,1)}, u32[]{:S(2)}) copy-start(bf16[256,256]{1,0:T(8,128)(2,1)} %constant.16.clone.band_y) | copy-start | bytes 393220
  0.7 7.8 %copy-start.9 = (bf16[256,128]{1,0:T(8,128)(2,1)S(1)}, bf16[256,128]{1,0:T(8,128)(2,1)}, u32[]{:S(2)}) copy-start(bf16[256,128]{1,0:T(8,128)(2,1)} %constant.17.clone.band_z) | copy-start | bytes 196612
  3.7 26.7 %collective-permute-start = (f32[2,4,256,128]{3,2,1,0:T(8,128)}, f32[2,4,256,128]{3,2,1,0:T(8,128)}, u32[]{:S(2)}, u32[]{:S(2)}) collective-permute-start(f32[2,4,256,128]{3,2,1,0:T(8,128)} %get-tuple-element.54), channel_id=1, source_target_pairs={{0,4},{8,12},{4,0},{12,8},{1,5},{9,13},{5,1},{13,9},{2,6},{10,14},... | collective-permute-start | bytes 3145736 | tf_op jit(solution)/shard_map/ppermute | solution.py:912
  6.8 23.6 %collective-permute-start.1 = (f32[2,4,256,128]{3,2,1,0:T(8,128)}, f32[2,4,256,128]{3,2,1,0:T(8,128)}, u32[]{:S(2)}, u32[]{:S(2)}) collective-permute-start(f32[2,4,256,128]{3,2,1,0:T(8,128)} %get-tuple-element.55), channel_id=1, source_target_pairs={{4,8},{8,4},{5,9},{9,5},{6,10},{10,6},{7,11},{11,7},{20,24},{24,20... | collective-permute-start | bytes 3145736 | tf_op jit(solution)/shard_map/ppermute | solution.py:912
  28.5 17.3 %collective-permute-start.6 = (f32[8,64,128]{2,1,0:T(8,128)}, f32[8,64,128]{2,1,0:T(8,128)}, u32[]{:S(2)}, u32[]{:S(2)}) collective-permute-start(f32[8,64,128]{2,1,0:T(8,128)} %get-tuple-element.71), channel_id=1, source_target_pairs={{0,1},{1,0},{2,3},{3,2},{4,5},{5,4},{6,7},{7,6},{8,9},{9,8},{10,11... | collective-permute-start | bytes 786440 | tf_op jit(solution)/shard_map/ppermute | solution.py:917
  28.6 17.2 %collective-permute-start.7 = (f32[8,64,128]{2,1,0:T(8,128)}, f32[8,64,128]{2,1,0:T(8,128)}, u32[]{:S(2)}, u32[]{:S(2)}) collective-permute-start(f32[8,64,128]{2,1,0:T(8,128)} %get-tuple-element.72), channel_id=1, source_target_pairs={{0,2},{1,3},{2,0},{3,1},{4,6},{5,7},{6,4},{7,5},{8,10},{9,11},{10,... | collective-permute-start | bytes 786440 | tf_op jit(solution)/shard_map/ppermute | solution.py:917
  30.1 15.7 %collective-permute-start.8 = (f32[8,64,128]{2,1,0:T(8,128)}, f32[8,64,128]{2,1,0:T(8,128)}, u32[]{:S(2)}, u32[]{:S(2)}) collective-permute-start(f32[8,64,128]{2,1,0:T(8,128)} %get-tuple-element.73), channel_id=1, source_target_pairs={{0,3},{1,2},{2,1},{3,0},{4,7},{5,6},{6,5},{7,4},{8,11},{9,10},{10,... | collective-permute-start | bytes 786440 | tf_op jit(solution)/shard_map/ppermute | solution.py:917
  33.2 27.3 %collective-permute-start.2 = (f32[2,4,256,128]{3,2,1,0:T(8,128)}, f32[2,4,256,128]{3,2,1,0:T(8,128)}, u32[]{:S(2)}, u32[]{:S(2)}) collective-permute-start(f32[2,4,256,128]{3,2,1,0:T(8,128)} %get-tuple-element.64), channel_id=1, source_target_pairs={{0,4},{8,12},{4,0},{12,8},{1,5},{9,13},{5,1},{13,9},{2,6},{10,14},... | collective-permute-start | bytes 3145736 | tf_op jit(solution)/shard_map/ppermute | solution.py:912
  37.9 22.6 %collective-permute-start.3 = (f32[2,4,256,128]{3,2,1,0:T(8,128)}, f32[2,4,256,128]{3,2,1,0:T(8,128)}, u32[]{:S(2)}, u32[]{:S(2)}) collective-permute-start(f32[2,4,256,128]{3,2,1,0:T(8,128)} %get-tuple-element.65), channel_id=1, source_target_pairs={{4,8},{8,4},{5,9},{9,5},{6,10},{10,6},{7,11},{11,7},{20,24},{24,20... | collective-permute-start | bytes 3145736 | tf_op jit(solution)/shard_map/ppermute | solution.py:912
  47.0 15.7 %collective-permute-start.9 = (f32[8,64,128]{2,1,0:T(8,128)}, f32[8,64,128]{2,1,0:T(8,128)}, u32[]{:S(2)}, u32[]{:S(2)}) collective-permute-start(f32[8,64,128]{2,1,0:T(8,128)} %get-tuple-element.80), channel_id=1, source_target_pairs={{0,1},{1,0},{2,3},{3,2},{4,5},{5,4},{6,7},{7,6},{8,9},{9,8},{10,11... | collective-permute-start | bytes 786440 | tf_op jit(solution)/shard_map/ppermute | solution.py:917
  47.1 15.7 %collective-permute-start.10 = (f32[8,64,128]{2,1,0:T(8,128)}, f32[8,64,128]{2,1,0:T(8,128)}, u32[]{:S(2)}, u32[]{:S(2)}) collective-permute-start(f32[8,64,128]{2,1,0:T(8,128)} %get-tuple-element.81), channel_id=1, source_target_pairs={{0,2},{1,3},{2,0},{3,1},{4,6},{5,7},{6,4},{7,5},{8,10},{9,11},{10,... | collective-permute-start | bytes 786440 | tf_op jit(solution)/shard_map/ppermute | solution.py:917
  48.6 14.1 %collective-permute-start.11 = (f32[8,64,128]{2,1,0:T(8,128)}, f32[8,64,128]{2,1,0:T(8,128)}, u32[]{:S(2)}, u32[]{:S(2)}) collective-permute-start(f32[8,64,128]{2,1,0:T(8,128)} %get-tuple-element.82), channel_id=1, source_target_pairs={{0,3},{1,2},{2,1},{3,0},{4,7},{5,6},{6,5},{7,4},{8,11},{9,10},{10,... | collective-permute-start | bytes 786440 | tf_op jit(solution)/shard_map/ppermute | solution.py:917
  60.5 2.2 %copy-start.10 = (bf16[128,128]{1,0:T(8,128)(2,1)S(1)}, bf16[128,128]{1,0:T(8,128)(2,1)}, u32[]{:S(2)}) copy-start(bf16[128,128]{1,0:T(8,128)(2,1)} %constant.19.clone.z_low.refs_6_) | copy-start | bytes 98308
  60.5 2.3 %copy-start.11 = (bf16[128,128]{1,0:T(8,128)(2,1)S(1)}, bf16[128,128]{1,0:T(8,128)(2,1)}, u32[]{:S(2)}) copy-start(bf16[128,128]{1,0:T(8,128)(2,1)} %constant.18.clone.z_high.refs_5_) | copy-start | bytes 98308
  62.6 14.7 %collective-permute-start.4 = (f32[8,2,64,128]{3,2,1,0:T(8,128)}, f32[8,2,64,128]{3,2,1,0:T(8,128)}, u32[]{:S(2)}, u32[]{:S(2)}) collective-permute-start(f32[8,2,64,128]{3,2,1,0:T(8,128)} %get-tuple-element.67), channel_id=1, source_target_pairs={{0,1},{1,0},{2,3},{3,2},{4,5},{5,4},{6,7},{7,6},{8,9},{9,8},{10,11... | collective-permute-start | bytes 1572872 | tf_op jit(solution)/shard_map/ppermute | solution.py:917
  65.9 16.8 %collective-permute-start.12 = (f32[8,32,128]{2,1,0:T(8,128)}, f32[8,32,128]{2,1,0:T(8,128)}, u32[]{:S(2)}, u32[]{:S(2)}) collective-permute-start(f32[8,32,128]{2,1,0:T(8,128)} %get-tuple-element.84), channel_id=1, source_target_pairs={{0,0},{1,4},{2,8},{3,12},{4,1},{5,5},{6,9},{7,13},{8,2},{9,6},{10,... | collective-permute-start | bytes 393224 | tf_op jit(solution)/shard_map/ppermute | solution.py:934
  68.1 14.6 %collective-permute-start.13 = (f32[8,32,128]{2,1,0:T(8,128)}, f32[8,32,128]{2,1,0:T(8,128)}, u32[]{:S(2)}, u32[]{:S(2)}) collective-permute-start(f32[8,32,128]{2,1,0:T(8,128)} %get-tuple-element.85), channel_id=1, source_target_pairs={{0,4},{1,8},{2,12},{3,0},{4,5},{5,9},{6,13},{7,1},{8,6},{9,10},{10... | collective-permute-start | bytes 393224 | tf_op jit(solution)/shard_map/ppermute | solution.py:934
  71.5 13.6 %collective-permute-start.14 = (f32[8,32,128]{2,1,0:T(8,128)}, f32[8,32,128]{2,1,0:T(8,128)}, u32[]{:S(2)}, u32[]{:S(2)}) collective-permute-start(f32[8,32,128]{2,1,0:T(8,128)} %get-tuple-element.86), channel_id=1, source_target_pairs={{0,8},{1,12},{2,0},{3,4},{4,9},{5,13},{6,1},{7,5},{8,10},{9,14},{1... | collective-permute-start | bytes 393224 | tf_op jit(solution)/shard_map/ppermute | solution.py:934
  75.3 10.8 %collective-permute-start.15 = (f32[8,32,128]{2,1,0:T(8,128)}, f32[8,32,128]{2,1,0:T(8,128)}, u32[]{:S(2)}, u32[]{:S(2)}) collective-permute-start(f32[8,32,128]{2,1,0:T(8,128)} %get-tuple-element.87), channel_id=1, source_target_pairs={{0,12},{1,0},{2,4},{3,8},{4,13},{5,1},{6,5},{7,9},{8,14},{9,2},{10... | collective-permute-start | bytes 393224 | tf_op jit(solution)/shard_map/ppermute | solution.py:934
  77.3 11.2 %copy-start = (bf16[256,256]{1,0:T(8,128)(2,1)S(1)}, bf16[256,256]{1,0:T(8,128)(2,1)}, u32[]{:S(2)}) copy-start(bf16[256,256]{1,0:T(8,128)(2,1)} %constant.21.clone.refs_5_) | copy-start | bytes 393220
  77.4 11.2 %copy-start.1 = (bf16[256,256]{1,0:T(8,128)(2,1)S(1)}, bf16[256,256]{1,0:T(8,128)(2,1)}, u32[]{:S(2)}) copy-start(bf16[256,256]{1,0:T(8,128)(2,1)} %constant.20.clone.refs_4_) | copy-start | bytes 393220
  80.5 10.3 %collective-permute-start.16 = (f32[8,32,128]{2,1,0:T(8,128)}, f32[8,32,128]{2,1,0:T(8,128)}, u32[]{:S(2)}, u32[]{:S(2)}) collective-permute-start(f32[8,32,128]{2,1,0:T(8,128)} %get-tuple-element.88), channel_id=1, source_target_pairs={{0,0},{1,4},{2,8},{3,12},{4,1},{5,5},{6,9},{7,13},{8,2},{9,6},{10,... | collective-permute-start | bytes 393224 | tf_op jit(solution)/shard_map/ppermute | solution.py:934
  82.7 8.2 %collective-permute-start.17 = (f32[8,32,128]{2,1,0:T(8,128)}, f32[8,32,128]{2,1,0:T(8,128)}, u32[]{:S(2)}, u32[]{:S(2)}) collective-permute-start(f32[8,32,128]{2,1,0:T(8,128)} %get-tuple-element.89), channel_id=1, source_target_pairs={{0,4},{1,8},{2,12},{3,0},{4,5},{5,9},{6,13},{7,1},{8,6},{9,10},{10... | collective-permute-start | bytes 393224 | tf_op jit(solution)/shard_map/ppermute | solution.py:934
  82.7 10.3 %collective-permute-start.18 = (f32[8,32,128]{2,1,0:T(8,128)}, f32[8,32,128]{2,1,0:T(8,128)}, u32[]{:S(2)}, u32[]{:S(2)}) collective-permute-start(f32[8,32,128]{2,1,0:T(8,128)} %get-tuple-element.90), channel_id=1, source_target_pairs={{0,8},{1,12},{2,0},{3,4},{4,9},{5,13},{6,1},{7,5},{8,10},{9,14},{1... | collective-permute-start | bytes 393224 | tf_op jit(solution)/shard_map/ppermute | solution.py:934
  85.1 8.0 %collective-permute-start.19 = (f32[8,32,128]{2,1,0:T(8,128)}, f32[8,32,128]{2,1,0:T(8,128)}, u32[]{:S(2)}, u32[]{:S(2)}) collective-permute-start(f32[8,32,128]{2,1,0:T(8,128)} %get-tuple-element.91), channel_id=1, source_target_pairs={{0,12},{1,0},{2,4},{3,8},{4,13},{5,1},{6,5},{7,9},{8,14},{9,2},{10... | collective-permute-start | bytes 393224 | tf_op jit(solution)/shard_map/ppermute | solution.py:934
  86.1 14.9 %collective-permute-start.5 = (f32[8,64,128]{2,1,0:T(8,128)}, f32[8,64,128]{2,1,0:T(8,128)}, u32[]{:S(2)}, u32[]{:S(2)}) collective-permute-start(f32[8,64,128]{2,1,0:T(8,128)} %get-tuple-element.69), channel_id=1, source_target_pairs={{0,2},{1,3},{2,0},{3,1},{4,6},{5,7},{6,4},{7,5},{8,10},{9,11},{10,... | collective-permute-start | bytes 786440 | tf_op jit(solution)/shard_map/ppermute | solution.py:917
  88.6 4.5 %copy-start.2 = (f32[5,96]{1,0:T(8,128)S(1)}, f32[5,96]{1,0:T(8,128)}, u32[]{:S(2)}) copy-start(f32[5,96]{1,0:T(8,128)} %constant.22.clone.scan) | copy-start | bytes 5764
  90.8 13.5 %copy-start.3 = (f32[4,4]{1,0:T(4,128)S(1)}, f32[4,4]{1,0:T(4,128)}, u32[]{:S(2)}) copy-start(f32[4,4]{1,0:T(4,128)} %constant.23.clone.carry) | copy-start | bytes 196
  95.7 7.0 %collective-permute-start.20 = (f32[32,256]{1,0:T(8,128)S(1)}, f32[32,256]{1,0:T(8,128)S(1)}, u32[]{:S(2)}, u32[]{:S(2)}) collective-permute-start(f32[32,256]{1,0:T(8,128)S(1)} %get-tuple-element.93), channel_id=1, source_target_pairs={{0,1},{1,0},{2,3},{3,2},{4,5},{5,4},{6,7},{7,6},{8,9},{9,8},{10,11... | collective-permute-start | bytes 98312 | tf_op jit(solution)/shard_map/ppermute | solution.py:917
  98.5 4.4 %collective-permute-start.21 = (f32[32,256]{1,0:T(8,128)S(1)}, f32[32,256]{1,0:T(8,128)S(1)}, u32[]{:S(2)}, u32[]{:S(2)}) collective-permute-start(f32[32,256]{1,0:T(8,128)S(1)} %get-tuple-element.94), channel_id=1, source_target_pairs={{0,2},{1,3},{2,0},{3,1},{4,6},{5,7},{6,4},{7,5},{8,10},{9,11},{10,... | collective-permute-start | bytes 98312 | tf_op jit(solution)/shard_map/ppermute | solution.py:917
  101.0 3.3 %collective-permute-start.22 = (f32[32,256]{1,0:T(8,128)S(1)}, f32[32,256]{1,0:T(8,128)S(1)}, u32[]{:S(2)}, u32[]{:S(2)}) collective-permute-start(f32[32,256]{1,0:T(8,128)S(1)} %get-tuple-element.95), channel_id=1, source_target_pairs={{0,3},{1,2},{2,1},{3,0},{4,7},{5,6},{6,5},{7,4},{8,11},{9,10},{10,... | collective-permute-start | bytes 98312 | tf_op jit(solution)/shard_map/ppermute | solution.py:917

commit v5 on v4

--- a/solution.py
+++ b/solution.py
@@ -354,14 +354,18 @@
     lax.fori_loop(0, count // STRIP, step, 0)
 
 
-def pick_kernel(f_now, a_now, *refs):
-    outs, sems = refs[:2], refs[2]
+def pick_kernel(f_now, a_now, out0, out1, buf, sems):
     copies = Copies(sems)
-    wait_all([
-        copies.start(field.at[pl.ds(base, REACH)], outs[s].at[i])
+    loads = [
+        (copies.start(field.at[pl.ds(base, REACH)], buf.at[s, i]), s, i)
         for s, (base, _) in enumerate(sides(f_now.shape[0]))
         for i, field in enumerate((f_now, a_now))
-    ])
+    ]
+    stores = []
+    for load, s, i in loads:
+        load.wait()
+        stores.append(copies.start(buf.at[s, i], (out0, out1)[s].at[i]))
+    wait_all(stores)
 
 
 def pick(f_now, a_now):
@@ -371,8 +375,8 @@
         pick_kernel,
         out_shape=(both, both),
         in_specs=[ANY] * 2,
-        out_specs=(VMEM,) * 2,
-        scratch_shapes=[pltpu.SemaphoreType.DMA((4,))],
+        out_specs=(ANY,) * 2,
+        scratch_shapes=[held(2, 2, REACH, ny, nz), pltpu.SemaphoreType.DMA((8,))],
         compiler_params=cheap(8),
         cost_estimate=COST,
         name="pick",

time: 106 us -> 106 us (level)
  no operation moved by 1% of the time
where the time goes in v5:
time: 106 us
  Pallas kernels  49.5 us (47%)
  starting transfers between devices  39.7 us (37%)
  waiting for transfers between devices  15.3 us (14%)
    pallas_call x1, Pallas kernels, step_one(): pl.pallas_call(step_one_kernel, out_shape=tuple((held(*shape) for shape i...  20 us
    ppermute x8, starting transfers between devices, spread(): out.append(lax.ppermute(piece, ('mp', 'shot'), pairs))  17 us
    ppermute x11, starting transfers between devices, flip(): got = lax.ppermute(value, 'shot', [(i, i ^ bit) for i in range(count)])  11.7 us
    ppermute x4, waiting for transfers between devices, swap(): lax.ppermute(v, 'mp', neighbours(count, start))  11.6 us
    ppermute x4, starting transfers between devices, swap(): lax.ppermute(v, 'mp', neighbours(count, start))  11 us
    pallas_call x1, Pallas kernels, step_two(): pl.pallas_call(functools.partial(step_two_kernel, len(after)), out_shape=...  6.26 us
    pallas_call x1, Pallas kernels, depth_edge(): pl.pallas_call(functools.partial(depth_edge_kernel, pieces), out_shape=(t...  3.16 us
    pallas_call x1, Pallas kernels, depth(): pl.pallas_call(functools.partial(depth_kernel, layout, offsets, pieces),...  3.12 us
  transfers between devices with their start and end apart: 23, of which 4 were waited for; matrix products, arithmetic and copies ran while one was open for 0% of the time, Pallas kernels for 43%

profile of v5, /device:TPU:0, one launch (start us, length us, event | category | flops | bytes accessed | tf_op | source)
XLA Modules:
  0.0 105.5 jit_solution(12878857544295905943)
XLA Ops:
  0.7 0.0 copy-start.8
  0.7 0.0 copy-start.9
  0.7 2.6 %pick.1 = (f32[2,4,256,128]{3,2,1,0:T(8,128)}, f32[2,4,256,128]{3,2,1,0:T(8,128)}) custom-call(f32[24,256,128]{2,1,0:T(8,128)} %bitcast.13, f32[24,256,128]{2,1,0:T(8,128)} %bitcast.15), custom_call_target="tpu_custom_call" | custom-call | flops 1000 | bytes 1000 | tf_op jit(solution)/shard_map/pick/pallas_call | solution.py:374
  3.3 3.1 %collective-permute-start = (f32[2,4,256,128]{3,2,1,0:T(8,128)}, f32[2,4,256,128]{3,2,1,0:T(8,128)}, u32[]{:S(2)}, u32[]{:S(2)}) collective-permute-start(f32[2,4,256,128]{3,2,1,0:T(8,128)} %get-tuple-element.54), channel_id=1, source_target_pairs={{0,4},{8,12},{4,0},{12,8},{1,5},{9,13},{5,1},{13,9},{2,6},{10,14},... | collective-permute-start | bytes 3145736 | tf_op jit(solution)/shard_map/ppermute | solution.py:916
  6.4 1.6 %collective-permute-start.1 = (f32[2,4,256,128]{3,2,1,0:T(8,128)}, f32[2,4,256,128]{3,2,1,0:T(8,128)}, u32[]{:S(2)}, u32[]{:S(2)}) collective-permute-start(f32[2,4,256,128]{3,2,1,0:T(8,128)} %get-tuple-element.55), channel_id=1, source_target_pairs={{4,8},{8,4},{5,9},{9,5},{6,10},{10,6},{7,11},{11,7},{20,24},{24,20... | collective-permute-start | bytes 3145736 | tf_op jit(solution)/shard_map/ppermute | solution.py:916
  8.1 20.0 %step_one.1 = (f32[24,256,128]{2,1,0:T(8,128)S(1)}, f32[24,256,128]{2,1,0:T(8,128)S(1)}, f32[32,256,128]{2,1,0:T(8,128)S(1)}, f32[32,256,128]{2,1,0:T(8,128)S(1)...) custom-call(s32[1,64]{1,0:T(1,128)S(1)} %copy-done.6, ...), custom_call_target="tpu_custom_call" | custom-call | flops 999999995904 | bytes 1000 | tf_op jit(solution)/shard_map/step_one/pallas_call | solution.py:308
  28.1 0.1 collective-permute-start.6
  28.1 1.6 %collective-permute-start.7 = (f32[8,64,128]{2,1,0:T(8,128)}, f32[8,64,128]{2,1,0:T(8,128)}, u32[]{:S(2)}, u32[]{:S(2)}) collective-permute-start(f32[8,64,128]{2,1,0:T(8,128)} %get-tuple-element.72), channel_id=1, source_target_pairs={{0,2},{1,3},{2,0},{3,1},{4,6},{5,7},{6,4},{7,5},{8,10},{9,11},{10,... | collective-permute-start | bytes 786440 | tf_op jit(solution)/shard_map/ppermute | solution.py:921
  29.7 0.3 collective-permute-start.8
  30.0 0.0 collective-permute-done.halo0
  30.0 2.8 %correct.1 = (f32[24,256,128]{2,1,0:T(8,128)S(1)}, f32[32,256,128]{2,1,0:T(8,128)S(1)}, f32[32,256,128]{2,1,0:T(8,128)S(1)}, f32[24,256,128]{2,1,0:T(8,128)S(1)}...) custom-call(f32[24,256,128]{2,1,0:T(8,128)S(1)} %get-tuple-element.4, ...), custom_call_target="tpu_custom_call", output_to_operand_aliasing={{0}: (1, {}), {1}: (2, {}), {2}: (3, {}), {3}: (4, {})} | custom-call | flops 1000 | bytes 1000 | tf_op jit(solution)/shard_map/correct/pallas_call | solution.py:432
  32.8 4.7 %collective-permute-start.2 = (f32[2,4,256,128]{3,2,1,0:T(8,128)}, f32[2,4,256,128]{3,2,1,0:T(8,128)}, u32[]{:S(2)}, u32[]{:S(2)}) collective-permute-start(f32[2,4,256,128]{3,2,1,0:T(8,128)} %get-tuple-element.64), channel_id=1, source_target_pairs={{0,4},{8,12},{4,0},{12,8},{1,5},{9,13},{5,1},{13,9},{2,6},{10,14},... | collective-permute-start | bytes 3145736 | tf_op jit(solution)/shard_map/ppermute | solution.py:916
  37.4 1.6 %collective-permute-start.3 = (f32[2,4,256,128]{3,2,1,0:T(8,128)}, f32[2,4,256,128]{3,2,1,0:T(8,128)}, u32[]{:S(2)}, u32[]{:S(2)}) collective-permute-start(f32[2,4,256,128]{3,2,1,0:T(8,128)} %get-tuple-element.65), channel_id=1, source_target_pairs={{4,8},{8,4},{5,9},{9,5},{6,10},{10,6},{7,11},{11,7},{20,24},{24,20... | collective-permute-start | bytes 3145736 | tf_op jit(solution)/shard_map/ppermute | solution.py:916
  39.1 6.3 %step_two.1 = (f32[2,4,256,128]{3,2,1,0:T(8,128)S(1)}, f32[2,4,256,128]{3,2,1,0:T(8,128)S(1)}, f32[2,4,256,128]{3,2,1,0:T(8,128)S(1)}, f32[8,64,128]{2,1,0:T(8,1...) custom-call(f32[24,256,128]{2,1,0:T(8,128)S(1)} %get-tuple-element.49.c_buf, ...), custom_call_target="tpu_custom_call" | custom-call | flops 999999995904 | bytes 1000 | tf_op jit(solution)/shard_map/step_two/pallas_call | solution.py:493
  45.4 0.0 collective-permute-done.6.refs_1_
  45.4 1.2 %add_up.1 = (f32[8,64,128]{2,1,0:T(8,128)S(1)}, f32[8,64,128]{2,1,0:T(8,128)S(1)}, f32[8,64,128]{2,1,0:T(8,128)}, f32[8,64,128]{2,1,0:T(8,128)}, f32[8,64,128]{2,1,0:T(8,128)}) custom-call(f32[8,64,128]{2,1,0:T(8,128)S(1)} %get-tuple-element.70.refs_0_, ...), custom_call_target="tpu_custom_call", output_to_operand_aliasing={{1}: (4, {}), {2}: (5, {}), {3}: (6, {}), {4}: (7, {})} | custom-call | flops 1000 | bytes 1000 | tf_op jit(solution)/shard_map/add_up/pallas_call | solution.py:515
  46.6 0.1 collective-permute-start.9
  46.6 1.6 %collective-permute-start.10 = (f32[8,64,128]{2,1,0:T(8,128)}, f32[8,64,128]{2,1,0:T(8,128)}, u32[]{:S(2)}, u32[]{:S(2)}) collective-permute-start(f32[8,64,128]{2,1,0:T(8,128)} %get-tuple-element.81), channel_id=1, source_target_pairs={{0,2},{1,3},{2,0},{3,1},{4,6},{5,7},{6,4},{7,5},{8,10},{9,11},{10,... | collective-permute-start | bytes 786440 | tf_op jit(solution)/shard_map/ppermute | solution.py:921
  48.2 0.3 collective-permute-start.11
  48.5 11.6 %collective-permute-done.2.halo0 = f32[2,4,256,128]{3,2,1,0:T(8,128)} collective-permute-done((f32[2,4,256,128]{3,2,1,0:T(8,128)}, f32[2,4,256,128]{3,2,1,0:T(8,128)}, u32[]{:S(2)}, u32[]{:S(2)}) %collective-permute-start.2) | collective-permute-done | bytes 1048608 | tf_op jit(solution)/shard_map/ppermute | solution.py:916
  60.0 0.0 collective-permute-done.3.halo1
  60.1 2.1 %finish.1 = (f32[8,2,64,128]{3,2,1,0:T(8,128)}, f32[8,2,64,128]{3,2,1,0:T(8,128)S(1)}) custom-call(f32[2,4,256,128]{3,2,1,0:T(8,128)S(1)} %get-tuple-element.61.edge, f32[2,4,256,128]{3,2,1,0:T(8,128)S(1)} %get-tuple-element.62.by_f, f32[2,4,256,128]{3,2,1,0:T(8,128)S(1)} %get-tuple-element.63.by_a, f32[2,4,256,128]{3,2,1,0:T(8,128)} %collective-permute-done.2.halo0, ...), custom_call_target="tpu_custom_call" | custom-call | flops 999999995904 | bytes 1000 | tf_op jit(solution)/shard_map/finish/pallas_call | solution.py:567
  62.2 0.1 collective-permute-start.4
  62.3 0.0 collective-permute-done.9.refs_2_
  62.3 0.0 collective-permute-done.10.refs_3_
  62.3 3.1 %depth.1 = (f32[24,64,128]{2,1,0:T(8,128)}, f32[8,32,128]{2,1,0:T(8,128)}, f32[8,32,128]{2,1,0:T(8,128)}, f32[8,32,128]{2,1,0:T(8,128)}, f32[8,32,128]{2,1,0:T(8,128)}) custom-call(f32[8,64,128]{2,1,0:T(8,128)S(1)} %get-tuple-element.78.refs_0_, f32[8,64,128]{2,1,0:T(8,128)S(1)} %get-tuple-element.79.refs_1_, f32[8,64,128]{2,1,0:T(8,128)} %collective-permute-done.9.refs_2_, ...), custom_call_target="tpu_custom_call" | custom-call | flops 999999995904 | bytes 1000 | tf_op jit(solution)/shard_map/depth/pallas_call | solution.py:636
  65.4 2.2 %collective-permute-start.12 = (f32[8,32,128]{2,1,0:T(8,128)}, f32[8,32,128]{2,1,0:T(8,128)}, u32[]{:S(2)}, u32[]{:S(2)}) collective-permute-start(f32[8,32,128]{2,1,0:T(8,128)} %get-tuple-element.84), channel_id=1, source_target_pairs={{0,0},{1,4},{2,8},{3,12},{4,1},{5,5},{6,9},{7,13},{8,2},{9,6},{10,... | collective-permute-start | bytes 393224 | tf_op jit(solution)/shard_map/ppermute | solution.py:938
  67.6 3.5 %collective-permute-start.13 = (f32[8,32,128]{2,1,0:T(8,128)}, f32[8,32,128]{2,1,0:T(8,128)}, u32[]{:S(2)}, u32[]{:S(2)}) collective-permute-start(f32[8,32,128]{2,1,0:T(8,128)} %get-tuple-element.85), channel_id=1, source_target_pairs={{0,4},{1,8},{2,12},{3,0},{4,5},{5,9},{6,13},{7,1},{8,6},{9,10},{10... | collective-permute-start | bytes 393224 | tf_op jit(solution)/shard_map/ppermute | solution.py:938
  71.1 3.8 %collective-permute-start.14 = (f32[8,32,128]{2,1,0:T(8,128)}, f32[8,32,128]{2,1,0:T(8,128)}, u32[]{:S(2)}, u32[]{:S(2)}) collective-permute-start(f32[8,32,128]{2,1,0:T(8,128)} %get-tuple-element.86), channel_id=1, source_target_pairs={{0,8},{1,12},{2,0},{3,4},{4,9},{5,13},{6,1},{7,5},{8,10},{9,14},{1... | collective-permute-start | bytes 393224 | tf_op jit(solution)/shard_map/ppermute | solution.py:938
  74.9 2.0 %collective-permute-start.15 = (f32[8,32,128]{2,1,0:T(8,128)}, f32[8,32,128]{2,1,0:T(8,128)}, u32[]{:S(2)}, u32[]{:S(2)}) collective-permute-start(f32[8,32,128]{2,1,0:T(8,128)} %get-tuple-element.87), channel_id=1, source_target_pairs={{0,12},{1,0},{2,4},{3,8},{4,13},{5,1},{6,5},{7,9},{8,14},{9,2},{10... | collective-permute-start | bytes 393224 | tf_op jit(solution)/shard_map/ppermute | solution.py:938
  76.9 3.2 %depth_edge.1 = (f32[8,64,128]{2,1,0:T(8,128)S(1)}, f32[8,64,128]{2,1,0:T(8,128)}, f32[8,32,128]{2,1,0:T(8,128)}, f32[8,32,128]{2,1,0:T(8,128)}, f32[8,32,128]{2,1,0:T(8,128)}, /*index=5*/f32[8,32,128]{2,1,0:T(8,128)}) custom-call(f32[8,2,64,128]{3,2,1,0:T(8,128)S(1)} %get-tuple-element.66.keep, f32[8,2,64,128]{3,2,1,0:T(8,128)} %collective-permute-done.4.near, ...), custom_call_target="tpu_custom_call" | custom-call | flops 999999995904 | bytes 1000 | tf_op jit(solution)/shard_map/depth_edge/pallas_call | solution.py:681
  80.1 2.2 %collective-permute-start.16 = (f32[8,32,128]{2,1,0:T(8,128)}, f32[8,32,128]{2,1,0:T(8,128)}, u32[]{:S(2)}, u32[]{:S(2)}) collective-permute-start(f32[8,32,128]{2,1,0:T(8,128)} %get-tuple-element.88), channel_id=1, source_target_pairs={{0,0},{1,4},{2,8},{3,12},{4,1},{5,5},{6,9},{7,13},{8,2},{9,6},{10,... | collective-permute-start | bytes 393224 | tf_op jit(solution)/shard_map/ppermute | solution.py:938
  82.2 2.4 %collective-permute-start.18 = (f32[8,32,128]{2,1,0:T(8,128)}, f32[8,32,128]{2,1,0:T(8,128)}, u32[]{:S(2)}, u32[]{:S(2)}) collective-permute-start(f32[8,32,128]{2,1,0:T(8,128)} %get-tuple-element.90), channel_id=1, source_target_pairs={{0,8},{1,12},{2,0},{3,4},{4,9},{5,13},{6,1},{7,5},{8,10},{9,14},{1... | collective-permute-start | bytes 393224 | tf_op jit(solution)/shard_map/ppermute | solution.py:938
  84.6 0.0 collective-permute-done.14.refs_2_
  84.6 1.1 collective-permute-start.19
  85.7 2.4 %collective-permute-start.5 = (f32[8,64,128]{2,1,0:T(8,128)}, f32[8,64,128]{2,1,0:T(8,128)}, u32[]{:S(2)}, u32[]{:S(2)}) collective-permute-start(f32[8,64,128]{2,1,0:T(8,128)} %get-tuple-element.69), channel_id=1, source_target_pairs={{0,2},{1,3},{2,0},{3,1},{4,6},{5,7},{6,4},{7,5},{8,10},{9,11},{10,... | collective-permute-start | bytes 786440 | tf_op jit(solution)/shard_map/ppermute | solution.py:921
  88.1 2.3 %gather.1.mains = f32[16,32,256]{2,1,0:T(8,128)S(1)} custom-call(f32[8,32,128]{2,1,0:T(8,128)} %collective-permute-done.12.refs_0_, f32[8,32,128]{2,1,0:T(8,128)} %collective-permute-done.13.refs_1_, f32[8,32,128]{2,1,0:T(8,128)} %collective-permute-done.14.refs_2_, f32[8,32,128]{2,1,0:T(8,128)} %collective-permute-done.15.refs_3_, ...), custom_call_target="tpu_custom_call" | custom-call | flops 999999995904 | bytes 1000 | tf_op jit(solution)/shard_map/gather/pallas_call | solution.py:802
  90.4 0.0 copy-start.3
  90.4 0.0 collective-permute-done.16.refs_0_
  90.4 2.2 %collective-permute-done.18.refs_2_ = f32[8,32,128]{2,1,0:T(8,128)} collective-permute-done((f32[8,32,128]{2,1,0:T(8,128)}, f32[8,32,128]{2,1,0:T(8,128)}, u32[]{:S(2)}, u32[]{:S(2)}) %collective-permute-start.18) | collective-permute-done | bytes 131104 | tf_op jit(solution)/shard_map/ppermute | solution.py:938
  92.6 2.7 %scan.3 = (f32[24,32,256]{2,1,0:T(8,128)S(1)}, f32[32,256]{1,0:T(8,128)S(1)}, f32[32,256]{1,0:T(8,128)S(1)}, f32[32,256]{1,0:T(8,128)S(1)}) custom-call(f32[5,96]{1,0:T(8,128)S(1)} %copy-done.2, f32[16,32,256]{2,1,0:T(8,128)S(1)} %gather.1.mains, f32[8,32,128]{2,1,0:T(8,128)} %collective-permute-done.16.refs_0_, ...), custom_call_target="tpu_custom_call" | custom-call | flops 1000 | bytes 1000 | tf_op jit(solution)/shard_map/scan/pallas_call | solution.py:861
  95.3 2.8 %collective-permute-start.20 = (f32[32,256]{1,0:T(8,128)S(1)}, f32[32,256]{1,0:T(8,128)S(1)}, u32[]{:S(2)}, u32[]{:S(2)}) collective-permute-start(f32[32,256]{1,0:T(8,128)S(1)} %get-tuple-element.93), channel_id=1, source_target_pairs={{0,1},{1,0},{2,3},{3,2},{4,5},{5,4},{6,7},{7,6},{8,9},{9,8},{10,11... | collective-permute-start | bytes 98312 | tf_op jit(solution)/shard_map/ppermute | solution.py:921
  98.1 2.4 %collective-permute-start.21 = (f32[32,256]{1,0:T(8,128)S(1)}, f32[32,256]{1,0:T(8,128)S(1)}, u32[]{:S(2)}, u32[]{:S(2)}) collective-permute-start(f32[32,256]{1,0:T(8,128)S(1)} %get-tuple-element.94), channel_id=1, source_target_pairs={{0,2},{1,3},{2,0},{3,1},{4,6},{5,7},{6,4},{7,5},{8,10},{9,11},{10,... | collective-permute-start | bytes 98312 | tf_op jit(solution)/shard_map/ppermute | solution.py:921
  100.5 0.1 collective-permute-start.22
  100.6 1.7 %raw_edge.1.refs_3_ = f32[24,64,128]{2,1,0:T(8,128)} custom-call(f32[8,64,128]{2,1,0:T(8,128)S(1)} %get-tuple-element.68.refs_0_, f32[8,64,128]{2,1,0:T(8,128)} %collective-permute-done.5.refs_1_, f32[24,64,128]{2,1,0:T(8,128)} %get-tuple-element.83.refs_2_), custom_call_target="tpu_custom_call", output_to_operand_aliasing={{}: (2, {})} | custom-call | flops 1000 | bytes 1000 | tf_op jit(solution)/shard_map/raw_edge/pallas_call | solution.py:711
  102.3 0.2 collective-permute-done.21.refs_1_
  102.5 1.4 %collective-permute-done.22.refs_2_ = f32[32,256]{1,0:T(8,128)S(1)} collective-permute-done((f32[32,256]{1,0:T(8,128)S(1)}, f32[32,256]{1,0:T(8,128)S(1)}, u32[]{:S(2)}, u32[]{:S(2)}) %collective-permute-start.22) | collective-permute-done | bytes 32800 | tf_op jit(solution)/shard_map/ppermute | solution.py:921
  103.9 1.6 %join.1 = f32[24,32,256]{2,1,0:T(8,128)} custom-call(f32[5,96]{1,0:T(8,128)S(1)} %copy-done.2, f32[4,4]{1,0:T(4,128)S(1)} %copy-done.3, f32[24,32,256]{2,1,0:T(8,128)S(1)} %get-tuple-element.92.part, f32[32,256]{1,0:T(8,128)S(1)} %collective-permute-done.20.refs_0_, f32[32,256]{1,0:T(8,128)S(1)} %collective-permute-done.21.refs_1_, ...), custom_call_target="tpu_custom_call" | custom-call | flops 1000 | bytes 1000 | tf_op jit(solution)/shard_map/join/pallas_call | solution.py:898
  (37 shorter events, 0.1 us)
Async XLA Ops:
  0.6 7.4 %copy-start.12 = (f32[1,2,2048]{2,1,0:T(2,128)S(1)}, f32[1,2,2048]{2,1,0:T(2,128)}, u32[]{:S(2)}) copy-start(f32[1,2,2048]{2,1,0:T(2,128)} %param.27) | copy-start | bytes 49156
  0.6 7.4 %copy-start.4 = (s32[2048]{0:T(1024)S(1)}, s32[2048]{0:T(1024)}, u32[]{:S(2)}) copy-start(s32[2048]{0:T(1024)} %param.26) | copy-start | bytes 24580
  0.7 7.4 %copy-start.5 = (f32[1,2,64]{2,1,0:T(2,128)S(1)}, f32[1,2,64]{2,1,0:T(2,128)}, u32[]{:S(2)}) copy-start(f32[1,2,64]{2,1,0:T(2,128)} %wavelet.1) | copy-start | bytes 1540
  0.7 7.4 %copy-start.6 = (s32[1,64]{1,0:T(1,128)S(1)}, s32[1,64]{1,0:T(1,128)}, u32[]{:S(2)}) copy-start(s32[1,64]{1,0:T(1,128)} %src_cell.1) | copy-start | bytes 772
  0.7 7.4 %copy-start.7 = (s32[1,64]{1,0:T(1,128)S(1)}, s32[1,64]{1,0:T(1,128)}, u32[]{:S(2)}) copy-start(s32[1,64]{1,0:T(1,128)} %src_sign.1) | copy-start | bytes 772
  0.7 7.4 %copy-start.8 = (bf16[256,256]{1,0:T(8,128)(2,1)S(1)}, bf16[256,256]{1,0:T(8,128)(2,1)}, u32[]{:S(2)}) copy-start(bf16[256,256]{1,0:T(8,128)(2,1)} %constant.16.clone.band_y) | copy-start | bytes 393220
  0.7 7.4 %copy-start.9 = (bf16[256,128]{1,0:T(8,128)(2,1)S(1)}, bf16[256,128]{1,0:T(8,128)(2,1)}, u32[]{:S(2)}) copy-start(bf16[256,128]{1,0:T(8,128)(2,1)} %constant.17.clone.band_z) | copy-start | bytes 196612
  3.3 26.7 %collective-permute-start = (f32[2,4,256,128]{3,2,1,0:T(8,128)}, f32[2,4,256,128]{3,2,1,0:T(8,128)}, u32[]{:S(2)}, u32[]{:S(2)}) collective-permute-start(f32[2,4,256,128]{3,2,1,0:T(8,128)} %get-tuple-element.54), channel_id=1, source_target_pairs={{0,4},{8,12},{4,0},{12,8},{1,5},{9,13},{5,1},{13,9},{2,6},{10,14},... | collective-permute-start | bytes 3145736 | tf_op jit(solution)/shard_map/ppermute | solution.py:916
  6.4 23.6 %collective-permute-start.1 = (f32[2,4,256,128]{3,2,1,0:T(8,128)}, f32[2,4,256,128]{3,2,1,0:T(8,128)}, u32[]{:S(2)}, u32[]{:S(2)}) collective-permute-start(f32[2,4,256,128]{3,2,1,0:T(8,128)} %get-tuple-element.55), channel_id=1, source_target_pairs={{4,8},{8,4},{5,9},{9,5},{6,10},{10,6},{7,11},{11,7},{20,24},{24,20... | collective-permute-start | bytes 3145736 | tf_op jit(solution)/shard_map/ppermute | solution.py:916
  28.1 17.3 %collective-permute-start.6 = (f32[8,64,128]{2,1,0:T(8,128)}, f32[8,64,128]{2,1,0:T(8,128)}, u32[]{:S(2)}, u32[]{:S(2)}) collective-permute-start(f32[8,64,128]{2,1,0:T(8,128)} %get-tuple-element.71), channel_id=1, source_target_pairs={{0,1},{1,0},{2,3},{3,2},{4,5},{5,4},{6,7},{7,6},{8,9},{9,8},{10,11... | collective-permute-start | bytes 786440 | tf_op jit(solution)/shard_map/ppermute | solution.py:921
  28.1 17.2 %collective-permute-start.7 = (f32[8,64,128]{2,1,0:T(8,128)}, f32[8,64,128]{2,1,0:T(8,128)}, u32[]{:S(2)}, u32[]{:S(2)}) collective-permute-start(f32[8,64,128]{2,1,0:T(8,128)} %get-tuple-element.72), channel_id=1, source_target_pairs={{0,2},{1,3},{2,0},{3,1},{4,6},{5,7},{6,4},{7,5},{8,10},{9,11},{10,... | collective-permute-start | bytes 786440 | tf_op jit(solution)/shard_map/ppermute | solution.py:921
  29.7 15.7 %collective-permute-start.8 = (f32[8,64,128]{2,1,0:T(8,128)}, f32[8,64,128]{2,1,0:T(8,128)}, u32[]{:S(2)}, u32[]{:S(2)}) collective-permute-start(f32[8,64,128]{2,1,0:T(8,128)} %get-tuple-element.73), channel_id=1, source_target_pairs={{0,3},{1,2},{2,1},{3,0},{4,7},{5,6},{6,5},{7,4},{8,11},{9,10},{10,... | collective-permute-start | bytes 786440 | tf_op jit(solution)/shard_map/ppermute | solution.py:921
  32.8 27.3 %collective-permute-start.2 = (f32[2,4,256,128]{3,2,1,0:T(8,128)}, f32[2,4,256,128]{3,2,1,0:T(8,128)}, u32[]{:S(2)}, u32[]{:S(2)}) collective-permute-start(f32[2,4,256,128]{3,2,1,0:T(8,128)} %get-tuple-element.64), channel_id=1, source_target_pairs={{0,4},{8,12},{4,0},{12,8},{1,5},{9,13},{5,1},{13,9},{2,6},{10,14},... | collective-permute-start | bytes 3145736 | tf_op jit(solution)/shard_map/ppermute | solution.py:916
  37.4 22.6 %collective-permute-start.3 = (f32[2,4,256,128]{3,2,1,0:T(8,128)}, f32[2,4,256,128]{3,2,1,0:T(8,128)}, u32[]{:S(2)}, u32[]{:S(2)}) collective-permute-start(f32[2,4,256,128]{3,2,1,0:T(8,128)} %get-tuple-element.65), channel_id=1, source_target_pairs={{4,8},{8,4},{5,9},{9,5},{6,10},{10,6},{7,11},{11,7},{20,24},{24,20... | collective-permute-start | bytes 3145736 | tf_op jit(solution)/shard_map/ppermute | solution.py:916
  46.6 15.7 %collective-permute-start.9 = (f32[8,64,128]{2,1,0:T(8,128)}, f32[8,64,128]{2,1,0:T(8,128)}, u32[]{:S(2)}, u32[]{:S(2)}) collective-permute-start(f32[8,64,128]{2,1,0:T(8,128)} %get-tuple-element.80), channel_id=1, source_target_pairs={{0,1},{1,0},{2,3},{3,2},{4,5},{5,4},{6,7},{7,6},{8,9},{9,8},{10,11... | collective-permute-start | bytes 786440 | tf_op jit(solution)/shard_map/ppermute | solution.py:921
  46.6 15.7 %collective-permute-start.10 = (f32[8,64,128]{2,1,0:T(8,128)}, f32[8,64,128]{2,1,0:T(8,128)}, u32[]{:S(2)}, u32[]{:S(2)}) collective-permute-start(f32[8,64,128]{2,1,0:T(8,128)} %get-tuple-element.81), channel_id=1, source_target_pairs={{0,2},{1,3},{2,0},{3,1},{4,6},{5,7},{6,4},{7,5},{8,10},{9,11},{10,... | collective-permute-start | bytes 786440 | tf_op jit(solution)/shard_map/ppermute | solution.py:921
  48.2 14.1 %collective-permute-start.11 = (f32[8,64,128]{2,1,0:T(8,128)}, f32[8,64,128]{2,1,0:T(8,128)}, u32[]{:S(2)}, u32[]{:S(2)}) collective-permute-start(f32[8,64,128]{2,1,0:T(8,128)} %get-tuple-element.82), channel_id=1, source_target_pairs={{0,3},{1,2},{2,1},{3,0},{4,7},{5,6},{6,5},{7,4},{8,11},{9,10},{10,... | collective-permute-start | bytes 786440 | tf_op jit(solution)/shard_map/ppermute | solution.py:921
  60.1 2.2 %copy-start.10 = (bf16[128,128]{1,0:T(8,128)(2,1)S(1)}, bf16[128,128]{1,0:T(8,128)(2,1)}, u32[]{:S(2)}) copy-start(bf16[128,128]{1,0:T(8,128)(2,1)} %constant.19.clone.z_low.refs_6_) | copy-start | bytes 98308
  60.1 2.3 %copy-start.11 = (bf16[128,128]{1,0:T(8,128)(2,1)S(1)}, bf16[128,128]{1,0:T(8,128)(2,1)}, u32[]{:S(2)}) copy-start(bf16[128,128]{1,0:T(8,128)(2,1)} %constant.18.clone.z_high.refs_5_) | copy-start | bytes 98308
  62.2 14.7 %collective-permute-start.4 = (f32[8,2,64,128]{3,2,1,0:T(8,128)}, f32[8,2,64,128]{3,2,1,0:T(8,128)}, u32[]{:S(2)}, u32[]{:S(2)}) collective-permute-start(f32[8,2,64,128]{3,2,1,0:T(8,128)} %get-tuple-element.67), channel_id=1, source_target_pairs={{0,1},{1,0},{2,3},{3,2},{4,5},{5,4},{6,7},{7,6},{8,9},{9,8},{10,11... | collective-permute-start | bytes 1572872 | tf_op jit(solution)/shard_map/ppermute | solution.py:921
  65.4 16.8 %collective-permute-start.12 = (f32[8,32,128]{2,1,0:T(8,128)}, f32[8,32,128]{2,1,0:T(8,128)}, u32[]{:S(2)}, u32[]{:S(2)}) collective-permute-start(f32[8,32,128]{2,1,0:T(8,128)} %get-tuple-element.84), channel_id=1, source_target_pairs={{0,0},{1,4},{2,8},{3,12},{4,1},{5,5},{6,9},{7,13},{8,2},{9,6},{10,... | collective-permute-start | bytes 393224 | tf_op jit(solution)/shard_map/ppermute | solution.py:938
  67.6 14.6 %collective-permute-start.13 = (f32[8,32,128]{2,1,0:T(8,128)}, f32[8,32,128]{2,1,0:T(8,128)}, u32[]{:S(2)}, u32[]{:S(2)}) collective-permute-start(f32[8,32,128]{2,1,0:T(8,128)} %get-tuple-element.85), channel_id=1, source_target_pairs={{0,4},{1,8},{2,12},{3,0},{4,5},{5,9},{6,13},{7,1},{8,6},{9,10},{10... | collective-permute-start | bytes 393224 | tf_op jit(solution)/shard_map/ppermute | solution.py:938
  71.1 13.6 %collective-permute-start.14 = (f32[8,32,128]{2,1,0:T(8,128)}, f32[8,32,128]{2,1,0:T(8,128)}, u32[]{:S(2)}, u32[]{:S(2)}) collective-permute-start(f32[8,32,128]{2,1,0:T(8,128)} %get-tuple-element.86), channel_id=1, source_target_pairs={{0,8},{1,12},{2,0},{3,4},{4,9},{5,13},{6,1},{7,5},{8,10},{9,14},{1... | collective-permute-start | bytes 393224 | tf_op jit(solution)/shard_map/ppermute | solution.py:938
  74.9 10.8 %collective-permute-start.15 = (f32[8,32,128]{2,1,0:T(8,128)}, f32[8,32,128]{2,1,0:T(8,128)}, u32[]{:S(2)}, u32[]{:S(2)}) collective-permute-start(f32[8,32,128]{2,1,0:T(8,128)} %get-tuple-element.87), channel_id=1, source_target_pairs={{0,12},{1,0},{2,4},{3,8},{4,13},{5,1},{6,5},{7,9},{8,14},{9,2},{10... | collective-permute-start | bytes 393224 | tf_op jit(solution)/shard_map/ppermute | solution.py:938
  76.9 11.2 %copy-start = (bf16[256,256]{1,0:T(8,128)(2,1)S(1)}, bf16[256,256]{1,0:T(8,128)(2,1)}, u32[]{:S(2)}) copy-start(bf16[256,256]{1,0:T(8,128)(2,1)} %constant.21.clone.refs_5_) | copy-start | bytes 393220
  76.9 11.2 %copy-start.1 = (bf16[256,256]{1,0:T(8,128)(2,1)S(1)}, bf16[256,256]{1,0:T(8,128)(2,1)}, u32[]{:S(2)}) copy-start(bf16[256,256]{1,0:T(8,128)(2,1)} %constant.20.clone.refs_4_) | copy-start | bytes 393220
  80.1 10.3 %collective-permute-start.16 = (f32[8,32,128]{2,1,0:T(8,128)}, f32[8,32,128]{2,1,0:T(8,128)}, u32[]{:S(2)}, u32[]{:S(2)}) collective-permute-start(f32[8,32,128]{2,1,0:T(8,128)} %get-tuple-element.88), channel_id=1, source_target_pairs={{0,0},{1,4},{2,8},{3,12},{4,1},{5,5},{6,9},{7,13},{8,2},{9,6},{10,... | collective-permute-start | bytes 393224 | tf_op jit(solution)/shard_map/ppermute | solution.py:938
  82.2 8.2 %collective-permute-start.17 = (f32[8,32,128]{2,1,0:T(8,128)}, f32[8,32,128]{2,1,0:T(8,128)}, u32[]{:S(2)}, u32[]{:S(2)}) collective-permute-start(f32[8,32,128]{2,1,0:T(8,128)} %get-tuple-element.89), channel_id=1, source_target_pairs={{0,4},{1,8},{2,12},{3,0},{4,5},{5,9},{6,13},{7,1},{8,6},{9,10},{10... | collective-permute-start | bytes 393224 | tf_op jit(solution)/shard_map/ppermute | solution.py:938
  82.2 10.3 %collective-permute-start.18 = (f32[8,32,128]{2,1,0:T(8,128)}, f32[8,32,128]{2,1,0:T(8,128)}, u32[]{:S(2)}, u32[]{:S(2)}) collective-permute-start(f32[8,32,128]{2,1,0:T(8,128)} %get-tuple-element.90), channel_id=1, source_target_pairs={{0,8},{1,12},{2,0},{3,4},{4,9},{5,13},{6,1},{7,5},{8,10},{9,14},{1... | collective-permute-start | bytes 393224 | tf_op jit(solution)/shard_map/ppermute | solution.py:938
  84.6 8.0 %collective-permute-start.19 = (f32[8,32,128]{2,1,0:T(8,128)}, f32[8,32,128]{2,1,0:T(8,128)}, u32[]{:S(2)}, u32[]{:S(2)}) collective-permute-start(f32[8,32,128]{2,1,0:T(8,128)} %get-tuple-element.91), channel_id=1, source_target_pairs={{0,12},{1,0},{2,4},{3,8},{4,13},{5,1},{6,5},{7,9},{8,14},{9,2},{10... | collective-permute-start | bytes 393224 | tf_op jit(solution)/shard_map/ppermute | solution.py:938
  85.7 14.9 %collective-permute-start.5 = (f32[8,64,128]{2,1,0:T(8,128)}, f32[8,64,128]{2,1,0:T(8,128)}, u32[]{:S(2)}, u32[]{:S(2)}) collective-permute-start(f32[8,64,128]{2,1,0:T(8,128)} %get-tuple-element.69), channel_id=1, source_target_pairs={{0,2},{1,3},{2,0},{3,1},{4,6},{5,7},{6,4},{7,5},{8,10},{9,11},{10,... | collective-permute-start | bytes 786440 | tf_op jit(solution)/shard_map/ppermute | solution.py:921
  88.1 4.5 %copy-start.2 = (f32[5,96]{1,0:T(8,128)S(1)}, f32[5,96]{1,0:T(8,128)}, u32[]{:S(2)}) copy-start(f32[5,96]{1,0:T(8,128)} %constant.22.clone.scan) | copy-start | bytes 5764
  90.4 13.5 %copy-start.3 = (f32[4,4]{1,0:T(4,128)S(1)}, f32[4,4]{1,0:T(4,128)}, u32[]{:S(2)}) copy-start(f32[4,4]{1,0:T(4,128)} %constant.23.clone.carry) | copy-start | bytes 196
  95.3 7.0 %collective-permute-start.20 = (f32[32,256]{1,0:T(8,128)S(1)}, f32[32,256]{1,0:T(8,128)S(1)}, u32[]{:S(2)}, u32[]{:S(2)}) collective-permute-start(f32[32,256]{1,0:T(8,128)S(1)} %get-tuple-element.93), channel_id=1, source_target_pairs={{0,1},{1,0},{2,3},{3,2},{4,5},{5,4},{6,7},{7,6},{8,9},{9,8},{10,11... | collective-permute-start | bytes 98312 | tf_op jit(solution)/shard_map/ppermute | solution.py:921
  98.1 4.4 %collective-permute-start.21 = (f32[32,256]{1,0:T(8,128)S(1)}, f32[32,256]{1,0:T(8,128)S(1)}, u32[]{:S(2)}, u32[]{:S(2)}) collective-permute-start(f32[32,256]{1,0:T(8,128)S(1)} %get-tuple-element.94), channel_id=1, source_target_pairs={{0,2},{1,3},{2,0},{3,1},{4,6},{5,7},{6,4},{7,5},{8,10},{9,11},{10,... | collective-permute-start | bytes 98312 | tf_op jit(solution)/shard_map/ppermute | solution.py:921
  100.5 3.3 %collective-permute-start.22 = (f32[32,256]{1,0:T(8,128)S(1)}, f32[32,256]{1,0:T(8,128)S(1)}, u32[]{:S(2)}, u32[]{:S(2)}) collective-permute-start(f32[32,256]{1,0:T(8,128)S(1)} %get-tuple-element.95), channel_id=1, source_target_pairs={{0,3},{1,2},{2,1},{3,0},{4,7},{5,6},{6,5},{7,4},{8,11},{9,10},{10,... | collective-permute-start | bytes 98312 | tf_op jit(solution)/shard_map/ppermute | solution.py:921
